TPU v7x, 32 devices: a whole 2x2x4 slice. The times are simulated.
32 devices in a mesh: groups: 2 (over y), seq: 16 (over z, x, core).
Axes of the slice: x: 2, y: 2, z: 4, core: 2. Of those that a mesh axis runs over, the one named last changes fastest.
Arguments:
- inputs: bfloat16 [4, 8192, 1536], P('groups', 'seq'), parts along dimension 0, may hold values from -6 to 6
- conv_weight: bfloat16 [3, 1536, 768], P(None, 'seq'), may hold values from -0.09375 to 0.09375
- proj_weight: bfloat16 [1536, 768], P('seq'), may hold values from -0.21875 to 0.21875
- cotangent: bfloat16 [4, 8192, 1536], P('groups', 'seq'), parts along dimension 0, may hold values from -6 to 6
Outputs:
- outputs: bfloat16 [4, 8192, 1536], P('groups', 'seq'), parts along dimension 0
- input_grad: bfloat16 [4, 8192, 1536], P('groups', 'seq'), parts along dimension 0
- conv_grad: float32 [3072, 3, 768], P(('groups', 'seq')), parts along dimension 0
- proj_grad: float32 [3072, 768], P(('groups', 'seq')), parts along dimension 0
There are 2 independent parts, one for each index of `groups`. A program takes and returns all parts, laid end to end along the dimension named above; an argument that names none is the same for every part. Nothing has to cross between parts.
All inputs are finite; a program needn't handle non-finite values.
Results may differ from a plain program's by a relative error of at most 0.0051.
Values may be sent and summed in bfloat16 or wider, within the bound.
No kernel may reach another device: no remote copies, remote signals or barrier semaphores. Data moves between devices by JAX's collectives and lax.ppermute only.
A program may use at most 128 MiB of HBM per device.

v0:
```python
import jax
import jax.numpy as jnp
from jax import lax
from jax.sharding import PartitionSpec as P

L = 8192


def from_behind(block, axis, distance):
    devices = range(lax.axis_size(axis))
    route = [(i - distance, i) for i in devices if i - distance in devices]
    return lax.ppermute(block, axis, route)


def gelu_grad(point, upstream):
    return jax.vjp(jax.nn.gelu, point)[1](upstream)[0]


def shards(inputs, conv_weight, proj_weight, cotangent):
    batch, local_len, chans = inputs.shape
    devices = lax.axis_size("seq")
    stride = devices // 8
    scale = 1.0 / float(batch * L) ** 0.5
    acted = jax.nn.gelu(inputs.astype(jnp.float32)).astype(jnp.bfloat16)
    conv_weight, proj_weight = (
        lax.all_gather(conv_weight, "seq", axis=1, tiled=True),
        lax.all_gather(proj_weight, "seq", axis=0, tiled=True),
    )
    hid = conv_weight.shape[2]
    acted_rows = acted.reshape(-1, chans)
    before = from_behind(acted, "seq", stride)
    after = from_behind(acted, "seq", -stride)
    hidden = jnp.dot(before.reshape(-1, chans), conv_weight[0], preferred_element_type=jnp.float32)
    hidden = hidden + jnp.dot(acted_rows, conv_weight[1], preferred_element_type=jnp.float32)
    hidden = hidden + jnp.dot(
        after.reshape(-1, chans), conv_weight[2], preferred_element_type=jnp.float32
    )
    gated = jax.nn.gelu(hidden).astype(jnp.bfloat16)
    outputs = (
        inputs.reshape(-1, chans).astype(jnp.float32)
        + jnp.dot(gated, proj_weight.T, preferred_element_type=jnp.float32)
    ).astype(jnp.bfloat16)
    cot_rows = cotangent.reshape(-1, chans)
    gated_grad = jnp.dot(cot_rows, proj_weight, preferred_element_type=jnp.float32)
    hidden_grad = gelu_grad(hidden, gated_grad).astype(jnp.bfloat16)
    grad_blocks = hidden_grad.reshape(batch, local_len, hid)
    grad_later = from_behind(grad_blocks, "seq", -stride).reshape(-1, hid)
    grad_earlier = from_behind(grad_blocks, "seq", stride).reshape(-1, hid)
    acted_grad = jnp.dot(grad_later, conv_weight[0].T, preferred_element_type=jnp.float32)
    acted_grad = acted_grad + jnp.dot(
        hidden_grad, conv_weight[1].T, preferred_element_type=jnp.float32
    )
    acted_grad = acted_grad + jnp.dot(
        grad_earlier, conv_weight[2].T, preferred_element_type=jnp.float32
    )
    input_grad = (
        cot_rows.astype(jnp.float32)
        + gelu_grad(inputs.reshape(-1, chans).astype(jnp.float32), acted_grad)
    ).astype(jnp.bfloat16)
    tap_grads = (grad_later, hidden_grad, grad_earlier)
    share = chans // devices
    local_terms = [
        jnp.dot(acted_rows.T, piece, preferred_element_type=jnp.float32) for piece in tap_grads
    ]
    local_terms.append(jnp.dot(cot_rows.T, gated, preferred_element_type=jnp.float32))
    stacked = jnp.stack(local_terms, axis=1)
    received = lax.all_to_all(stacked, "seq", split_axis=0, concat_axis=0, tiled=True)
    summed = jnp.sum(received.reshape(devices, share, 4, received.shape[2]), axis=0)
    conv_sum = summed[:, 0:3, :]
    proj_sum = summed[:, 3, :]
    return (
        outputs.reshape(batch, local_len, chans),
        input_grad.reshape(batch, local_len, chans),
        conv_sum * scale,
        proj_sum * scale,
    )


def solution(mesh):
    return jax.shard_map(
        shards,
        mesh=mesh,
        in_specs=(
            P("groups", "seq", None),
            P(None, "seq", None),
            P("seq", None),
            P("groups", "seq", None),
        ),
        out_specs=(
            P("groups", "seq", None),
            P("groups", "seq", None),
            P(("groups", "seq"), None, None),
            P(("groups", "seq"), None),
        ),
        check_vma=False,
    )
```

profile of v0, /device:TPU:16, one launch (start us, length us, event | category | flops | bytes accessed | tf_op | source)
XLA Modules:
  0.0 772.1 jit_solution(15523567253440921126)
XLA Ops:
  7.2 0.7 all-gather.5.cloned.1.call-update
  7.9 0.7 all-gather.3.cloned.1.call-update
  8.6 3.6 fusion.15
  12.2 3.4 collective-permute-start
  15.7 3.3 collective-permute-start.1
  19.0 106.8 %all-gather.5.cloned.1.call-done = bf16[1536,768]{1,0:T(8,128)(2,1)} async-done(((bf16[96,768]{1,0:T(8,128)(2,1)}), bf16[1536,768]{1,0:T(8,128)(2,1)}) %all-gather.5.cloned.1.call-update) | async-done | bytes 2359312 | tf_op jit(solution)/shard_map/all_gather | solution.py:27
  125.8 6.9 fusion.34
  132.7 33.0 %collective-permute-done = bf16[2,512,1536]{2,1,0:T(8,128)(2,1)} collective-permute-done((bf16[2,512,1536]{2,1,0:T(8,128)(2,1)S(1)}, bf16[2,512,1536]{2,1,0:T(8,128)(2,1)}, u32[]{:S(2)}, u32[]{:S(2)}) %collective-permute-start) | collective-permute-done | bytes 3145760 | tf_op jit(solution)/shard_map/ppermute | solution.py:12
  165.8 32.5 %all-gather.3.cloned.1.call-done = bf16[3,1536,768]{2,1,0:T(8,128)(2,1)} async-done(((bf16[3,96,768]{2,1,0:T(8,128)(2,1)}), bf16[3,1536,768]{2,1,0:T(8,128)(2,1)}) %all-gather.3.cloned.1.call-update) | async-done | bytes 7077904 | tf_op jit(solution)/shard_map/all_gather | solution.py:26
  198.2 5.4 fusion.27
  203.6 2.6 fusion.29
  206.2 6.2 fusion.25
  212.5 2.3 collective-permute-start.3
  214.8 4.9 collective-permute-start.2
  219.7 2.8 convolution_bitcast_fusion.2
  222.6 3.2 convolution_bitcast_fusion
  225.8 57.0 %collective-permute-done.3 = bf16[2,512,768]{2,1,0:T(8,128)(2,1)S(1)} collective-permute-done((bf16[2,512,768]{2,1,0:T(8,128)(2,1)S(1)}, bf16[2,512,768]{2,1,0:T(8,128)(2,1)S(1)}, u32[]{:S(2)}, u32[]{:S(2)}) %collective-permute-start.3) | collective-permute-done | bytes 1572896 | tf_op jit(solution)/shard_map/ppermute | solution.py:12
  282.8 4.0 convolution_bitcast_fusion.1
  286.9 1.2 copy-done.8
  288.1 14.4 %convolution_bitcast_fusion.3 = f32[1536,1,768]{2,0,1:T(8,128)S(1)} fusion(bf16[2,512,768]{2,1,0:T(8,128)(2,1)S(1)} %collective-permute-done.2, bf16[2,512,1536]{2,1,0:T(8,128)(2,1)S(1)} %copy-done), kind=kOutput, calls=%fused_computation.30 | convolution fusion | flops 2431647744 | bytes 9437184 | tf_op jit(solution)/shard_map/dot_general | solution.py:63
  302.4 1.9 pad_maximum_fusion
  304.4 34.4 %copy.18 = f32[1536,4,768]{2,1,0:T(4,128)} copy(f32[1536,4,768]{2,0,1:T(8,128)S(1)} %pad_maximum_fusion) | data formatting | bytes 37748736 | tf_op jit(solution)/shard_map/stack | solution.py:66
  338.7 6.1 all-to-all-start
  344.9 4.9 fusion.28
  349.9 4.3 fusion.16
  354.2 4.7 fusion.26
  358.8 9.7 %fusion.7 = bf16[1024,1536]{1,0:T(8,128)(2,1)} fusion(bf16[2,512,1536]{2,1,0:T(8,128)(2,1)S(1)} %copy-done, f32[1024,1536]{1,0:T(8,128)} %fusion.26, f32[1024,1536]{1,0:T(8,128)S(1)} %fusion.28, bf16[1024,1536]{1,0:T(8,128)(2,1)S(1)} %bitcast.79, bf16[1024,768]{1,0:T(8,128)(2,1)S(1)} %bitcast.82, bf16[3,1536,768]{2,1,0:T(8,128)(2,1)S(1)} %bitcast.76), kind=kOutput, calls=%fused_computation.11 | convolution fusion | flops 2455240704 | bytes 25952256 | tf_op jit(solution)/shard_map/dot_general | solution.py:53
  368.5 383.6 %all-to-all-done = f32[1536,4,768]{2,1,0:T(4,128)} async-done(((f32[1536,4,768]{2,1,0:T(4,128)}), f32[1536,4,768]{2,1,0:T(4,128)}, u32[]{:S(2)}, u32[]{:S(2)}) %all-to-all-start) | async-done | bytes 18874400 | tf_op jit(solution)/shard_map/all_to_all | solution.py:67
  752.1 10.4 %reduce_sum.9 = f32[96,4,768]{2,1,0:T(4,128)S(1)} reduce(f32[16,96,4,768]{3,2,1,0:T(4,128)} %bitcast.20, f32[]{:T(128)} %constant.14.clone.1), dimensions={0}, to_apply=%region_0.0 | reduce | flops 4423680 | bytes 20054020 | tf_op jit(solution)/shard_map/reduce_sum | solution.py:68
  762.8 0.4 slice_multiply_fusion.1
  763.2 1.1 copy.19
  764.3 0.7 copy.25
  (35 shorter events, 0.4 us)
Async XLA Ops:
  7.2 118.7 %all-gather.5.cloned.1.call-start = ((), (), s32[]{:S(2)}) async-start(), calls=%async_computation.2 | async-start | bytes 2506752 | tf_op jit(solution)/shard_map/all_gather | solution.py:27
  7.9 190.3 %all-gather.3.cloned.1.call-start = ((), (), s32[]{:S(2)}) async-start(), calls=%async_computation.1 | async-start | bytes 7520256 | tf_op jit(solution)/shard_map/all_gather | solution.py:26
  12.2 153.5 %collective-permute-start = (bf16[2,512,1536]{2,1,0:T(8,128)(2,1)S(1)}, bf16[2,512,1536]{2,1,0:T(8,128)(2,1)}, u32[]{:S(2)}, u32[]{:S(2)}) collective-permute-start(bf16[2,512,1536]{2,1,0:T(8,128)(2,1)S(1)} %fusion.15), channel_id=1, source_target_pairs={{0,2},{1,3},{2,4},{3,5},{4,6},{5,7},{6,8},{7,9},{8,10},{9,11},{10,... | collective-permute-start | bytes 9437192 | tf_op jit(solution)/shard_map/ppermute | solution.py:12
  15.7 190.6 %collective-permute-start.1 = (bf16[2,512,1536]{2,1,0:T(8,128)(2,1)S(1)}, bf16[2,512,1536]{2,1,0:T(8,128)(2,1)}, u32[]{:S(2)}, u32[]{:S(2)}) collective-permute-start(bf16[2,512,1536]{2,1,0:T(8,128)(2,1)S(1)} %fusion.15), channel_id=1, source_target_pairs={{2,0},{3,1},{4,2},{5,3},{6,4},{7,5},{8,6},{9,7},{10,8},{11,9},{12,... | collective-permute-start | bytes 9437192 | tf_op jit(solution)/shard_map/ppermute | solution.py:12
  198.2 5.4 copy-start.1
  203.6 2.6 copy-start.12
  212.4 10.1 %copy-start.5 = (bf16[1024,768]{1,0:T(8,128)(2,1)}, bf16[1024,768]{1,0:T(8,128)(2,1)S(1)}, u32[]{:S(2)}) copy-start(bf16[1024,768]{1,0:T(8,128)(2,1)S(1)} %get-tuple-element.8) | copy-start | bytes 4718596
  212.4 10.1 %copy-start.10 = (f32[1024,768]{1,0:T(8,128)}, f32[1024,768]{1,0:T(8,128)S(1)}, u32[]{:S(2)}) copy-start(f32[1024,768]{1,0:T(8,128)S(1)} %get-tuple-element.9) | copy-start | bytes 9437188
  212.5 10.1 %copy-start.2 = (bf16[2,512,1536]{2,1,0:T(8,128)(2,1)S(1)}, bf16[2,512,1536]{2,1,0:T(8,128)(2,1)}, u32[]{:S(2)}) copy-start(bf16[2,512,1536]{2,1,0:T(8,128)(2,1)} %param.7) | copy-start | bytes 9437188
  212.5 70.4 %collective-permute-start.3 = (bf16[2,512,768]{2,1,0:T(8,128)(2,1)S(1)}, bf16[2,512,768]{2,1,0:T(8,128)(2,1)S(1)}, u32[]{:S(2)}, u32[]{:S(2)}) collective-permute-start(bf16[2,512,768]{2,1,0:T(8,128)(2,1)S(1)} %bitcast.80), channel_id=1, source_target_pairs={{0,2},{1,3},{2,4},{3,5},{4,6},{5,7},{6,8},{7,9},{8,10},{9,11},{10,... | collective-permute-start | bytes 4718600 | tf_op jit(solution)/shard_map/ppermute | solution.py:12
  214.8 72.1 %collective-permute-start.2 = (bf16[2,512,768]{2,1,0:T(8,128)(2,1)S(1)}, bf16[2,512,768]{2,1,0:T(8,128)(2,1)S(1)}, u32[]{:S(2)}, u32[]{:S(2)}) collective-permute-start(bf16[2,512,768]{2,1,0:T(8,128)(2,1)S(1)} %bitcast.81), channel_id=1, source_target_pairs={{2,0},{3,1},{4,2},{5,3},{6,4},{7,5},{8,6},{9,7},{10,8},{11,9},{12,... | collective-permute-start | bytes 4718600 | tf_op jit(solution)/shard_map/ppermute | solution.py:12
  222.6 60.3 %copy-start = (bf16[2,512,1536]{2,1,0:T(8,128)(2,1)S(1)}, bf16[2,512,1536]{2,1,0:T(8,128)(2,1)}, u32[]{:S(2)}) copy-start(bf16[2,512,1536]{2,1,0:T(8,128)(2,1)} %param.4) | copy-start | bytes 9437188
  282.8 4.0 copy-start.6
  286.9 1.2 copy-start.8
  338.7 413.4 %all-to-all-start = ((f32[1536,4,768]{2,1,0:T(4,128)}), f32[1536,4,768]{2,1,0:T(4,128)}, u32[]{:S(2)}, u32[]{:S(2)}) async-start(f32[1536,4,768]{2,1,0:T(4,128)} %copy.18), calls=%async_computation | async-start | bytes 37748736 | tf_op jit(solution)/shard_map/all_to_all | solution.py:67
  344.9 5.0 copy-start.4
  344.9 5.0 copy-start.11
  344.9 9.2 %slice-start = ((s8[7077888]{0:T(1024)(128)(4,1)}), s8[4194304]{0:T(1024)(128)(4,1)S(1)}, s32[]{:S(2)}) async-start(s8[7077888]{0:T(1024)(128)(4,1)} %bitcast.75), calls=%async_computation.3 | async-start | bytes 8388608
  349.8 4.3 slice-start.1
  349.8 4.3 copy-start.9
  354.1 4.7 copy-start.3
  354.1 4.7 copy-start.7
Sparse Core Ops, SparseCore 0:
  10.3 115.4 all-gather.4
  128.1 70.0 all-gather.2
where the time goes:
time: 775 us; the launch traced here: 772 us
  waiting for transfers between devices  614 us (79%)
  matrix products  69 us (9%)
  local copies, waits for them, and re-layouts  37.4 us (5%)
  starting transfers between devices  20.2 us (3%)
  other arithmetic  16.6 us (2%)
  between operations  14.5 us (2%)
    all_to_all x1, waiting for transfers between devices, shards(): lax.all_to_all(stacked, 'seq', split_axis=0, concat_axis=0, tiled=True)  384 us
    all_gather x1, waiting for transfers between devices, shards(): lax.all_gather(proj_weight, 'seq', axis=0, tiled=True)  107 us
    ppermute x4, waiting for transfers between devices, from_behind(): return lax.ppermute(block, axis, route)  90.1 us
    another operation x1, local copies, waits for them, and re-layouts, shards(): stacked = jnp.stack(local_terms, axis=1)  34.4 us
    all_gather x1, waiting for transfers between devices, shards(): lax.all_gather(conv_weight, 'seq', axis=1, tiled=True)  32.5 us
    dot_general x3, matrix products, shards(): jnp.dot(acted_rows.T, piece, preferred_element_type=jnp.float32)  21.2 us
  transfers between devices with their start and end apart: 7, of which 5 were waited for; matrix products, arithmetic and copies ran while one was open for 7% of the time, Pallas kernels for 0%

commit v1 on v0

--- a/solution.py
+++ b/solution.py
@@ -76,9 +76,111 @@
     )
 
 
+def dot(a, b):
+    return jnp.dot(a, b, preferred_element_type=jnp.float32)
+
+
+def tdot(a, b):
+    return lax.dot_general(a, b, (((0,), (0,)), ((), ())), preferred_element_type=jnp.float32)
+
+
+def dot_t(a, b):
+    return lax.dot_general(a, b, (((1,), (1,)), ((), ())), preferred_element_type=jnp.float32)
+
+
+def paired(inputs, conv_weight, proj_weight, cotangent):
+    batch, local_len, chans = inputs.shape
+    hid = conv_weight.shape[2]
+    devices = lax.axis_size("seq")
+    depth = devices // 4
+    share = chans // devices
+    scale = 1.0 / float(batch * L) ** 0.5
+    me = lax.axis_index("seq")
+    core, x, z = me % 2, (me // 2) % 2, me // 4
+    everyone = range(devices)
+
+    def swap(value, bits):
+        return lax.ppermute(value, "seq", [(i, i ^ bits) for i in everyone])
+
+    def up(value):
+        return lax.ppermute(value, "seq", [(i, i + 4) for i in everyone if i + 4 in everyone])
+
+    def down(value):
+        return lax.ppermute(value, "seq", [(i + 4, i) for i in everyone if i + 4 in everyone])
+
+    def pick(value, index, axis=0):
+        return lax.dynamic_index_in_dim(value, index, axis, keepdims=False)
+
+    def exchange(pair):
+        kept, got = pick(pair, x), swap(pick(pair, 1 - x), 2)
+        first = jnp.where(x == 0, kept, got)
+        second = jnp.where(x == 0, got, kept)
+        return first, second
+
+    in_a, in_b = exchange(inputs)
+    weights = lax.all_gather(
+        jnp.concatenate([conv_weight, proj_weight[None]], axis=0), "seq", axis=1, tiled=True
+    )
+    w0, w1, w2, wp = weights[0], weights[1], weights[2], weights[3]
+    cot_a, cot_b = exchange(cotangent)
+    cot = jnp.concatenate([cot_a, cot_b], axis=0)
+
+    def act(v):
+        return jax.nn.gelu(v.astype(jnp.float32)).astype(jnp.bfloat16)
+
+    act_a, act_b = act(in_a), act(in_b)
+    acted = jnp.concatenate([act_a, act_b], axis=0)
+    from_prev = up(dot(act_b, w0).astype(jnp.bfloat16))
+    from_next = down(dot(act_a, w2).astype(jnp.bfloat16))
+    hidden_a = dot(act_a, w1) + dot(act_b, w2) + from_prev.astype(jnp.float32)
+    hidden_b = dot(act_b, w1) + dot(act_a, w0) + from_next.astype(jnp.float32)
+    hidden = jnp.concatenate([hidden_a, hidden_b], axis=0)
+    gated = jax.nn.gelu(hidden).astype(jnp.bfloat16)
+    gated_grad = dot(cot, wp)
+    hidden_grad = gelu_grad(hidden, gated_grad).astype(jnp.bfloat16)
+    hg_a, hg_b = hidden_grad[:local_len], hidden_grad[local_len:]
+    hg_prev, hg_next = up(hg_b), down(hg_a)
+
+    def scattered(term):
+        cols = term.shape[1]
+        parts = term.reshape(depth, 2, 2, share, cols)
+        parts = pick(parts, core, 2) + swap(pick(parts, 1 - core, 2), 1)
+        parts = pick(parts, x, 1) + swap(pick(parts, 1 - x, 1).astype(jnp.bfloat16), 2).astype(jnp.float32)
+        total = pick(parts, z)
+        for k in range(1, depth):
+            total = total + swap(pick(parts, z ^ k).astype(jnp.bfloat16), 4 * k).astype(jnp.float32)
+        return total * scale
+
+    first = scattered(jnp.concatenate([tdot(acted, hidden_grad), tdot(cot, gated)], axis=1))
+    gated_own = exchange(gated.reshape(2, local_len, hid))
+    gated_own = jnp.concatenate(gated_own, axis=0)
+    outputs = (
+        inputs.reshape(-1, chans).astype(jnp.float32) + dot_t(gated_own, wp)
+    ).astype(jnp.bfloat16)
+    left = jnp.concatenate([hg_b, hg_next], axis=0)
+    right = jnp.concatenate([hg_prev, hg_a], axis=0)
+    second = scattered(tdot(acted, jnp.concatenate([left, right], axis=1)))
+    acted_grad = dot_t(left, w0) + dot_t(hidden_grad, w1) + dot_t(right, w2)
+    into = jnp.concatenate([in_a, in_b], axis=0).astype(jnp.float32)
+    input_grad = (cot.astype(jnp.float32) + gelu_grad(into, acted_grad)).astype(jnp.bfloat16)
+    input_grad = jnp.stack(exchange(input_grad.reshape(2, local_len, chans)))
+    conv_grad = jnp.stack([second[:, :hid], first[:, :hid], second[:, hid:]], axis=1)
+    return (
+        outputs.reshape(batch, local_len, chans),
+        input_grad,
+        conv_grad,
+        first[:, hid:],
+    )
+
+
 def solution(mesh):
+    def body(inputs, conv_weight, proj_weight, cotangent):
+        devices = lax.axis_size("seq")
+        by_pairs = devices == 16 and inputs.shape[0] == 2
+        return (paired if by_pairs else shards)(inputs, conv_weight, proj_weight, cotangent)
+
     return jax.shard_map(
-        shards,
+        body,
         mesh=mesh,
         in_specs=(
             P("groups", "seq", None),

time: 775 us -> 381 us (0.49)
  waiting for transfers between devices: 614 us -> 202 us
  other arithmetic: 16.6 us -> 32.4 us
    all_to_all x1 -> x0, waiting for transfers between devices: 384 us -> none  [shards(): lax.all_to_all(stacked, 'seq', split_axis=0, concat_axis=0, tiled=True)]
    all_gather x2 -> x1, waiting for transfers between devices: 139 us -> 2.15 us  [paired(): lax.all_gather(jnp.concatenate([conv_weight, proj_weight[None]], axis=0),...]
    ppermute x4 -> x18, waiting for transfers between devices: 90.1 us -> 199 us  [the longest x14 182 us: swap(): return lax.ppermute(value, 'seq', [(i, i ^ bits) for i in everyone])]
    another operation x1, local copies, waits for them, and re-layouts: 34.4 us -> 0.04 us  [paired(): jnp.stack([second[:, :hid], first[:, :hid], second[:, hid:]], axis=1)]
    squeeze x0 -> x5, local copies, waits for them, and re-layouts: none -> 12.5 us  [pick(): return lax.dynamic_index_in_dim(value, index, axis, keepdims=False)]
    ppermute x4 -> x18, starting transfers between devices: 14 us -> 24.8 us  [the longest x14 12.6 us: swap(): return lax.ppermute(value, 'seq', [(i, i ^ bits) for i in everyone])]
    reduce_sum x1 -> x0, other arithmetic: 10.4 us -> none  [shards(): jnp.sum(received.reshape(devices, share, 4, received.shape[2]), axis=0)]
    concatenate x0 -> x1, local copies, waits for them, and re-layouts: none -> 9.59 us  [paired(): jnp.concatenate([tdot(acted, hidden_grad), tdot(cot, gated)], axis=1)]
  transfers between devices with their start and end apart: 7 -> 19, of which waited for: 5 -> 14; matrix products, arithmetic and copies ran while one was open for 7% -> 21% of each run, Pallas kernels for 0% -> 0%
where the time goes in v1:
time: 381 us
  waiting for transfers between devices  202 us (53%)
  matrix products  76.1 us (20%)
  other arithmetic  32.4 us (9%)
  local copies, waits for them, and re-layouts  31.7 us (8%)
  starting transfers between devices  24.8 us (7%)
  between operations  14.8 us (4%)
    ppermute x14, waiting for transfers between devices, swap(): return lax.ppermute(value, 'seq', [(i, i ^ bits) for i in everyone])  182 us
    dot_general x4, matrix products, dot_t(): lax.dot_general(a, b, (((1,), (1,)), ((), ())), preferred_element_type=jn...  32.3 us
    dot_general x7, matrix products, dot(): return jnp.dot(a, b, preferred_element_type=jnp.float32)  31.4 us
    ppermute x14, starting transfers between devices, swap(): return lax.ppermute(value, 'seq', [(i, i ^ bits) for i in everyone])  12.6 us
    squeeze x5, local copies, waits for them, and re-layouts, pick(): return lax.dynamic_index_in_dim(value, index, axis, keepdims=False)  12.5 us
    dot_general x3, matrix products, tdot(): lax.dot_general(a, b, (((0,), (0,)), ((), ())), preferred_element_type=jn...  12.5 us
    ppermute x2, waiting for transfers between devices, down(): lax.ppermute(value, 'seq', [(i + 4, i) for i in everyone if i + 4 in ever...  9.79 us
    concatenate x1, local copies, waits for them, and re-layouts, paired(): jnp.concatenate([tdot(acted, hidden_grad), tdot(cot, gated)], axis=1)  9.59 us
  transfers between devices with their start and end apart: 19, of which 14 were waited for; matrix products, arithmetic and copies ran while one was open for 21% of the time, Pallas kernels for 0%

profile of v1, /device:TPU:16, one launch (start us, length us, event | category | flops | bytes accessed | tf_op | source)
XLA Modules:
  0.0 381.3 jit_solution(3203508814311027004)
XLA Ops:
  9.4 2.7 dynamic-slice_bitcast_fusion.2
  15.3 43.2 %collective-permute-done.4 = bf16[512,1536]{1,0:T(8,128)(2,1)} collective-permute-done((bf16[512,1536]{1,0:T(8,128)(2,1)}, bf16[512,1536]{1,0:T(8,128)(2,1)}, u32[]{:S(2)}, u32[]{:S(2)}) %collective-permute-start.4) | collective-permute-done | bytes 1572896 | tf_op jit(solution)/shard_map/ppermute | solution.py:103
  58.5 3.8 bitcast_select_fusion.3
  62.2 51.6 %collective-permute-done = bf16[512,1536]{1,0:T(8,128)(2,1)} collective-permute-done((bf16[512,1536]{1,0:T(8,128)(2,1)}, bf16[512,1536]{1,0:T(8,128)(2,1)}, u32[]{:S(2)}, u32[]{:S(2)}) %collective-permute-start) | collective-permute-done | bytes 1572896 | tf_op jit(solution)/shard_map/ppermute | solution.py:103
  113.8 5.5 %fusion.37 = (bf16[512,1536]{1,0:T(8,128)(2,1)}, bf16[512,1536]{1,0:T(8,128)(2,1)}, bf16[512,1536]{1,0:T(8,128)(2,1)}, bf16[512,1536]{1,0:T(8,128)(2,1)}) fusion(bf16[512,1536]{1,0:T(8,128)(2,1)} %collective-permute-done, bf16[2,512,1536]{2,1,0:T(8,128)(2,1)S(1)} %copy-done.2, s32[]{:T(128)S(6)} %select_n.107, pred[]{:T(512)S(6)} %eq.5), kind=kLoop, calls=%fused_computation.58 | loop fusion | flops 17301504 | bytes 9437189 | tf_op jit(solution)/shard_map/convert_element_type | solution.py:129
  121.5 4.3 %fusion.73 = bf16[512,768]{1,0:T(8,128)(2,1)S(1)} fusion(bf16[4,1536,768]{2,1,0:T(8,128)(2,1)} %all-gather.2.cloned.1.call-done, bf16[512,1536]{1,0:T(8,128)(2,1)} %get-tuple-element.7), kind=kOutput, calls=%fused_computation.118 | convolution fusion | flops 1216217088 | bytes 4718592 | tf_op jit(solution)/shard_map/dot_general | solution.py:80
  130.3 3.9 %collective-permute-start.2 = (bf16[512,768]{1,0:T(8,128)(2,1)S(1)}, bf16[512,768]{1,0:T(8,128)(2,1)S(1)}, u32[]{:S(2)}, u32[]{:S(2)}) collective-permute-start(bf16[512,768]{1,0:T(8,128)(2,1)S(1)} %fusion.74), channel_id=1, source_target_pairs={{4,0},{5,1},{6,2},{7,3},{8,4},{9,5},{10,6},{11,7},{12,8},{13,9},{1... | collective-permute-start | bytes 2359304 | tf_op jit(solution)/shard_map/ppermute | solution.py:109
  142.5 4.9 %collective-permute-done.1 = bf16[512,768]{1,0:T(8,128)(2,1)S(1)} collective-permute-done((bf16[512,768]{1,0:T(8,128)(2,1)S(1)}, bf16[512,768]{1,0:T(8,128)(2,1)S(1)}, u32[]{:S(2)}, u32[]{:S(2)}) %collective-permute-start.1) | collective-permute-done | bytes 786464 | tf_op jit(solution)/shard_map/ppermute | solution.py:106
  147.6 4.1 %collective-permute-done.2 = bf16[512,768]{1,0:T(8,128)(2,1)S(1)} collective-permute-done((bf16[512,768]{1,0:T(8,128)(2,1)S(1)}, bf16[512,768]{1,0:T(8,128)(2,1)S(1)}, u32[]{:S(2)}, u32[]{:S(2)}) %collective-permute-start.2) | collective-permute-done | bytes 786464 | tf_op jit(solution)/shard_map/ppermute | solution.py:109
  153.9 3.0 fusion.57
  156.9 16.8 %fusion.17 = bf16[1024,768]{1,0:T(8,128)(2,1)S(1)} fusion(bf16[4,1536,768]{2,1,0:T(8,128)(2,1)S(1)} %copy-done.21, bf16[512,1536]{1,0:T(8,128)(2,1)S(1)} %copy-done.17, bf16[512,1536]{1,0:T(8,128)(2,1)S(1)} %copy-done.15, f32[512,768]{1,0:T(8,128)S(1)} %convert_add_fusion.4, f32[512,768]{1,0:T(8,128)S(1)} %convert_add_fusion.5), kind=kOutput, calls=%fused_computation.38 | convolution fusion | flops 2438725632 | bytes 10223616 | tf_op jit(solution)/shard_map/dot_general | solution.py:80
  176.7 4.3 %fusion.47 = f32[1536,768]{0,1:T(8,128)} fusion(bf16[1024,768]{1,0:T(8,128)(2,1)S(1)} %fusion.17, bf16[512,1536]{1,0:T(8,128)(2,1)S(1)} %copy-done.9, bf16[512,1536]{1,0:T(8,128)(2,1)S(1)} %copy-done.11), kind=kOutput, calls=%fused_computation.81 | convolution fusion | flops 2422210560 | bytes 9437184 | tf_op jit(solution)/shard_map/dot_general | solution.py:84
  181.0 6.8 %pad_maximum_fusion = f32[1536,1536]{0,1:T(8,128)} fusion(f32[1536,768]{0,1:T(8,128)S(1)} %fusion.57, f32[1536,768]{0,1:T(8,128)} %fusion.47), kind=kLoop, calls=%fused_computation.4 | loop fusion | flops 2359296 | bytes 18874368 | tf_op jit(solution)/shard_map/concatenate | solution.py:154
  187.8 9.6 %copy.17 = f32[1536,1536]{1,0:T(8,128)} copy(f32[1536,1536]{0,1:T(8,128)} %pad_maximum_fusion) | data formatting | bytes 18874368 | tf_op jit(solution)/shard_map/concatenate | solution.py:154
  197.4 4.9 %dynamic-slice_bitcast_fusion = f32[4,2,96,1536]{3,2,1,0:T(8,128)} fusion(f32[4,2,2,96,1536]{4,3,2,1,0:T(8,128)} %bitcast.118, s32[]{:T(128)S(6)} %select_n.119), kind=kLoop, calls=%fused_computation.29 | loop fusion | bytes 9437188 | tf_op jit(solution)/shard_map/jit(dynamic_index_in_dim)/squeeze | solution.py:112
  202.2 3.4 collective-permute-start.5
  205.7 2.5 collective-permute-start.6
  211.9 6.5 %fusion.48 = f32[1024,1536]{1,0:T(8,128)} fusion(bf16[1024,768]{1,0:T(8,128)(2,1)S(1)} %copy-done.14, bf16[4,1536,768]{2,1,0:T(8,128)(2,1)} %all-gather.2.cloned.1.call-done), kind=kOutput, calls=%fused_computation.82 | convolution fusion | flops 2415919104 | bytes 10223616 | tf_op jit(solution)/shard_map/dot_general | solution.py:88
  218.4 5.7 %collective-permute-done.5 = bf16[512,768]{1,0:T(8,128)(2,1)S(1)} collective-permute-done((bf16[512,768]{1,0:T(8,128)(2,1)S(1)}, bf16[512,768]{1,0:T(8,128)(2,1)S(1)}, u32[]{:S(2)}, u32[]{:S(2)}) %collective-permute-start.5) | collective-permute-done | bytes 786464 | tf_op jit(solution)/shard_map/ppermute | solution.py:109
  224.1 3.2 collective-permute-done.6
  227.3 5.2 %fusion.38 = f32[1536,1536]{1,0:T(8,128)S(1)} fusion(bf16[512,768]{1,0:T(8,128)(2,1)S(1)} %copy-done.18, bf16[512,768]{1,0:T(8,128)(2,1)S(1)} %collective-permute-done.6, bf16[512,768]{1,0:T(8,128)(2,1)S(1)} %collective-permute-done.5, bf16[512,768]{1,0:T(8,128)(2,1)S(1)} %copy-done.19, bf16[512,1536]{1,0:T(8,128)(2,1)S(1)} %copy-done.10, ...), kind=kOutput, calls=%fused_computation.63 | convolution fusion | flops 4850712576 | bytes 15728640 | tf_op jit(solution)/shard_map/dot_general | solution.py:84
  235.0 7.4 %fusion.54 = f32[1024,1536]{1,0:T(8,128)} fusion(bf16[4,1536,768]{2,1,0:T(8,128)(2,1)} %all-gather.2.cloned.1.call-done, bf16[512,768]{1,0:T(8,128)(2,1)S(1)} %copy-done.24, bf16[512,768]{1,0:T(8,128)(2,1)S(1)} %copy-done.20), kind=kOutput, calls=%fused_computation.88 | convolution fusion | flops 2419064832 | bytes 10223616 | tf_op jit(solution)/shard_map/dot_general | solution.py:88
  242.4 11.6 %fusion.4 = bf16[1024,1536]{1,0:T(8,128)(2,1)} fusion(f32[1024,1536]{1,0:T(8,128)} %fusion.54, f32[1024,1536]{1,0:T(8,128)} %fusion.48, bf16[512,1536]{1,0:T(8,128)(2,1)S(1)} %copy-done.6, bf16[512,1536]{1,0:T(8,128)(2,1)S(1)} %copy-done.8, bf16[4,1536,768]{2,1,0:T(8,128)(2,1)} %all-gather.2.cloned.1.call-done, bf16[512,768]{1,0:T(8,128)(2,1)} %get-tuple-element.25, ...), kind=kOutput, calls=%fused_computation.9 | convolution fusion | flops 2467823616 | bytes 25952256 | tf_op jit(solution)/shard_map/dot_general | solution.py:88
  254.0 2.8 dynamic-slice_bitcast_fusion.1
  258.9 6.8 %fusion.10 = bf16[1024,1536]{1,0:T(8,128)(2,1)} fusion(bf16[1024,1536]{1,0:T(8,128)(2,1)S(1)} %bitcast.125, bf16[4,1536,768]{2,1,0:T(8,128)(2,1)} %all-gather.2.cloned.1.call-done, bf16[512,768]{1,0:T(8,128)(2,1)S(1)} %get-tuple-element.23, bf16[512,768]{1,0:T(8,128)(2,1)S(1)} %get-tuple-element.22), kind=kOutput, calls=%fused_computation.16 | convolution fusion | flops 2423783424 | bytes 10223616 | tf_op jit(solution)/shard_map/dot_general | solution.py:88
  265.7 3.3 bitcast_add_fusion
  272.5 22.0 %collective-permute-done.7 = bf16[512,1536]{1,0:T(8,128)(2,1)} collective-permute-done((bf16[512,1536]{1,0:T(8,128)(2,1)}, bf16[512,1536]{1,0:T(8,128)(2,1)}, u32[]{:S(2)}, u32[]{:S(2)}) %collective-permute-start.7) | collective-permute-done | bytes 1572896 | tf_op jit(solution)/shard_map/ppermute | solution.py:103
  298.1 21.7 %collective-permute-done.14 = bf16[4,96,1536]{2,1,0:T(8,128)(2,1)} collective-permute-done((bf16[4,96,1536]{2,1,0:T(8,128)(2,1)S(1)}, bf16[4,96,1536]{2,1,0:T(8,128)(2,1)}, u32[]{:S(2)}, u32[]{:S(2)}) %collective-permute-start.14) | collective-permute-done | bytes 1179680 | tf_op jit(solution)/shard_map/ppermute | solution.py:103
  325.1 18.4 %collective-permute-done.9 = bf16[4,96,1536]{2,1,0:T(8,128)(2,1)S(1)} collective-permute-done((bf16[4,96,1536]{2,1,0:T(8,128)(2,1)S(1)}, bf16[4,96,1536]{2,1,0:T(8,128)(2,1)S(1)}, u32[]{:S(2)}, u32[]{:S(2)}) %collective-permute-start.9) | collective-permute-done | bytes 1179680 | tf_op jit(solution)/shard_map/ppermute | solution.py:103
  350.4 3.6 collective-permute-done.10
  353.9 12.1 %collective-permute-done.11 = bf16[96,1536]{1,0:T(8,128)(2,1)S(1)} collective-permute-done((bf16[96,1536]{1,0:T(8,128)(2,1)S(1)}, bf16[96,1536]{1,0:T(8,128)(2,1)S(1)}, u32[]{:S(2)}, u32[]{:S(2)}) %collective-permute-start.11) | collective-permute-done | bytes 294944 | tf_op jit(solution)/shard_map/ppermute | solution.py:103
  366.0 7.1 %collective-permute-done.12 = bf16[96,1536]{1,0:T(8,128)(2,1)S(1)} collective-permute-done((bf16[96,1536]{1,0:T(8,128)(2,1)S(1)}, bf16[96,1536]{1,0:T(8,128)(2,1)S(1)}, u32[]{:S(2)}, u32[]{:S(2)}) %collective-permute-start.12) | collective-permute-done | bytes 294944 | tf_op jit(solution)/shard_map/ppermute | solution.py:103
  (111 shorter events, 54.2 us)
Async XLA Ops:
  7.2 114.3 %all-gather.2.cloned.1.call-start = ((), (), s32[]{:S(2)}) async-start(), calls=%async_computation | async-start | bytes 10027008 | tf_op jit(solution)/shard_map/all_gather | solution.py:121
  12.0 46.4 %collective-permute-start.4 = (bf16[512,1536]{1,0:T(8,128)(2,1)}, bf16[512,1536]{1,0:T(8,128)(2,1)}, u32[]{:S(2)}, u32[]{:S(2)}) collective-permute-start(bf16[512,1536]{1,0:T(8,128)(2,1)} %dynamic-slice_bitcast_fusion.2), channel_id=1, source_target_pairs={{0,2},{1,3},{2,0},{3,1},{4,6},{5,7},{6,4},{7,5},{8,10},{9,11},{10,... | collective-permute-start | bytes 4718600 | tf_op jit(solution)/shard_map/ppermute | solution.py:103
  14.8 99.0 %collective-permute-start = (bf16[512,1536]{1,0:T(8,128)(2,1)}, bf16[512,1536]{1,0:T(8,128)(2,1)}, u32[]{:S(2)}, u32[]{:S(2)}) collective-permute-start(bf16[512,1536]{1,0:T(8,128)(2,1)} %dynamic-slice_bitcast_fusion.3), channel_id=1, source_target_pairs={{0,2},{1,3},{2,0},{3,1},{4,6},{5,7},{6,4},{7,5},{8,10},{9,11},{10,... | collective-permute-start | bytes 4718600 | tf_op jit(solution)/shard_map/ppermute | solution.py:103
  121.5 6.8 %copy-start.7 = (bf16[512,1536]{1,0:T(8,128)(2,1)S(1)}, bf16[512,1536]{1,0:T(8,128)(2,1)}, u32[]{:S(2)}) copy-start(bf16[512,1536]{1,0:T(8,128)(2,1)} %get-tuple-element.15) | copy-start | bytes 4718596
  121.5 6.8 %copy-start.21 = (bf16[4,1536,768]{2,1,0:T(8,128)(2,1)S(1)}, bf16[4,1536,768]{2,1,0:T(8,128)(2,1)}, u32[]{:S(2)}) copy-start(bf16[4,1536,768]{2,1,0:T(8,128)(2,1)} %all-gather.2.cloned.1.call-done) | copy-start | bytes 28311556
  125.8 21.6 %collective-permute-start.1 = (bf16[512,768]{1,0:T(8,128)(2,1)S(1)}, bf16[512,768]{1,0:T(8,128)(2,1)S(1)}, u32[]{:S(2)}, u32[]{:S(2)}) collective-permute-start(bf16[512,768]{1,0:T(8,128)(2,1)S(1)} %fusion.73), channel_id=1, source_target_pairs={{0,4},{1,5},{2,6},{3,7},{4,8},{5,9},{6,10},{7,11},{8,12},{9,13},{1... | collective-permute-start | bytes 2359304 | tf_op jit(solution)/shard_map/ppermute | solution.py:106
  130.3 21.4 %collective-permute-start.2 = (bf16[512,768]{1,0:T(8,128)(2,1)S(1)}, bf16[512,768]{1,0:T(8,128)(2,1)S(1)}, u32[]{:S(2)}, u32[]{:S(2)}) collective-permute-start(bf16[512,768]{1,0:T(8,128)(2,1)S(1)} %fusion.74), channel_id=1, source_target_pairs={{4,0},{5,1},{6,2},{7,3},{8,4},{9,5},{10,6},{11,7},{12,8},{13,9},{1... | collective-permute-start | bytes 2359304 | tf_op jit(solution)/shard_map/ppermute | solution.py:109
  197.4 8.3 %copy-start.19 = (bf16[512,768]{1,0:T(8,128)(2,1)S(1)}, bf16[512,768]{1,0:T(8,128)(2,1)}, u32[]{:S(2)}) copy-start(bf16[512,768]{1,0:T(8,128)(2,1)} %get-tuple-element.24) | copy-start | bytes 2359300
  202.2 63.5 %collective-permute-start.13 = (f32[4,2,96,1536]{3,2,1,0:T(8,128)}, f32[4,2,96,1536]{3,2,1,0:T(8,128)}, u32[]{:S(2)}, u32[]{:S(2)}) collective-permute-start(f32[4,2,96,1536]{3,2,1,0:T(8,128)} %dynamic-slice_bitcast_fusion), channel_id=1, source_target_pairs={{0,1},{1,0},{2,3},{3,2},{4,5},{5,4},{6,7},{7,6},{8,9},{9,8},{10,11... | collective-permute-start | bytes 14155784 | tf_op jit(solution)/shard_map/ppermute | solution.py:103
  202.2 21.8 %collective-permute-start.5 = (bf16[512,768]{1,0:T(8,128)(2,1)S(1)}, bf16[512,768]{1,0:T(8,128)(2,1)S(1)}, u32[]{:S(2)}, u32[]{:S(2)}) collective-permute-start(bf16[512,768]{1,0:T(8,128)(2,1)S(1)} %copy-done.18), channel_id=1, source_target_pairs={{4,0},{5,1},{6,2},{7,3},{8,4},{9,5},{10,6},{11,7},{12,8},{13,9},{1... | collective-permute-start | bytes 2359304 | tf_op jit(solution)/shard_map/ppermute | solution.py:109
  205.7 21.6 %collective-permute-start.6 = (bf16[512,768]{1,0:T(8,128)(2,1)S(1)}, bf16[512,768]{1,0:T(8,128)(2,1)S(1)}, u32[]{:S(2)}, u32[]{:S(2)}) collective-permute-start(bf16[512,768]{1,0:T(8,128)(2,1)S(1)} %copy-done.19), channel_id=1, source_target_pairs={{0,4},{1,5},{2,6},{3,7},{4,8},{5,9},{6,10},{7,11},{8,12},{9,13},{1... | collective-permute-start | bytes 2359304 | tf_op jit(solution)/shard_map/ppermute | solution.py:106
  211.3 16.0 %copy-start.10 = (bf16[512,1536]{1,0:T(8,128)(2,1)S(1)}, bf16[512,1536]{1,0:T(8,128)(2,1)}, u32[]{:S(2)}) copy-start(bf16[512,1536]{1,0:T(8,128)(2,1)} %get-tuple-element.6) | copy-start | bytes 4718596
  211.3 16.0 %copy-start.12 = (bf16[512,1536]{1,0:T(8,128)(2,1)S(1)}, bf16[512,1536]{1,0:T(8,128)(2,1)}, u32[]{:S(2)}) copy-start(bf16[512,1536]{1,0:T(8,128)(2,1)} %get-tuple-element.14) | copy-start | bytes 4718596
  211.3 46.2 %collective-permute-start.3 = (bf16[512,768]{1,0:T(8,128)(2,1)}, bf16[512,768]{1,0:T(8,128)(2,1)}, u32[]{:S(2)}, u32[]{:S(2)}) collective-permute-start(bf16[512,768]{1,0:T(8,128)(2,1)} %dynamic-slice_bitcast_fusion.4), channel_id=1, source_target_pairs={{0,2},{1,3},{2,0},{3,1},{4,6},{5,7},{6,4},{7,5},{8,10},{9,11},{10,... | collective-permute-start | bytes 2359304 | tf_op jit(solution)/shard_map/ppermute | solution.py:103
  224.1 8.4 %copy-start.23 = (bf16[512,768]{1,0:T(8,128)(2,1)}, bf16[512,768]{1,0:T(8,128)(2,1)S(1)}, u32[]{:S(2)}) copy-start(bf16[512,768]{1,0:T(8,128)(2,1)S(1)} %collective-permute-done.5) | copy-start | bytes 2359300
  234.0 8.4 %copy-start.6 = (bf16[512,1536]{1,0:T(8,128)(2,1)S(1)}, bf16[512,1536]{1,0:T(8,128)(2,1)}, u32[]{:S(2)}) copy-start(bf16[512,1536]{1,0:T(8,128)(2,1)} %get-tuple-element.7) | copy-start | bytes 4718596
  234.0 8.4 %copy-start.8 = (bf16[512,1536]{1,0:T(8,128)(2,1)S(1)}, bf16[512,1536]{1,0:T(8,128)(2,1)}, u32[]{:S(2)}) copy-start(bf16[512,1536]{1,0:T(8,128)(2,1)} %get-tuple-element.15) | copy-start | bytes 4718596
  234.0 8.4 %copy-start.16 = (bf16[512,1536]{1,0:T(8,128)(2,1)S(1)}, bf16[512,1536]{1,0:T(8,128)(2,1)}, u32[]{:S(2)}) copy-start(bf16[512,1536]{1,0:T(8,128)(2,1)} %get-tuple-element.12) | copy-start | bytes 4718596
  234.1 36.7 %collective-permute-start.8 = (f32[4,2,96,1536]{3,2,0,1:T(8,128)S(1)}, f32[4,2,96,1536]{3,2,0,1:T(8,128)S(1)}, u32[]{:S(2)}, u32[]{:S(2)}) collective-permute-start(f32[4,2,96,1536]{3,2,0,1:T(8,128)S(1)} %bitcast.124), channel_id=1, source_target_pairs={{0,1},{1,0},{2,3},{3,2},{4,5},{5,4},{6,7},{7,6},{8,9},{9,8},{10,11... | collective-permute-start | bytes 14155784 | tf_op jit(solution)/shard_map/ppermute | solution.py:103
  256.9 37.6 %collective-permute-start.7 = (bf16[512,1536]{1,0:T(8,128)(2,1)}, bf16[512,1536]{1,0:T(8,128)(2,1)}, u32[]{:S(2)}, u32[]{:S(2)}) collective-permute-start(bf16[512,1536]{1,0:T(8,128)(2,1)} %dynamic-slice_bitcast_fusion.1), channel_id=1, source_target_pairs={{0,2},{1,3},{2,0},{3,1},{4,6},{5,7},{6,4},{7,5},{8,10},{9,11},{10,... | collective-permute-start | bytes 4718600 | tf_op jit(solution)/shard_map/ppermute | solution.py:103
  257.4 8.2 %slice-start = ((s8[9437184]{0:T(1024)(128)(4,1)}), s8[4194304]{0:T(1024)(128)(4,1)S(1)}, s32[]{:S(2)}) async-start(s8[9437184]{0:T(1024)(128)(4,1)} %bitcast.119), calls=%async_computation.1 | async-start | bytes 8388608
  258.9 6.8 %slice-start.1 = ((s8[9437184]{0:T(1024)(128)(4,1)}), s8[4194304]{0:T(1024)(128)(4,1)S(1)}, s32[]{:S(2)}) async-start(s8[9437184]{0:T(1024)(128)(4,1)} %bitcast.119), calls=%async_computation.2 | async-start | bytes 8388608
  258.9 6.8 %slice-start.2 = ((s8[9437184]{0:T(1024)(128)(4,1)}), s8[1048576]{0:T(1024)(128)(4,1)S(1)}, s32[]{:S(2)}) async-start(s8[9437184]{0:T(1024)(128)(4,1)} %bitcast.119), calls=%async_computation.3 | async-start | bytes 2097152
  269.2 50.6 %collective-permute-start.14 = (bf16[4,96,1536]{2,1,0:T(8,128)(2,1)S(1)}, bf16[4,96,1536]{2,1,0:T(8,128)(2,1)}, u32[]{:S(2)}, u32[]{:S(2)}) collective-permute-start(bf16[4,96,1536]{2,1,0:T(8,128)(2,1)S(1)} %fusion.76), channel_id=1, source_target_pairs={{0,2},{1,3},{2,0},{3,1},{4,6},{5,7},{6,4},{7,5},{8,10},{9,11},{10,... | collective-permute-start | bytes 3538952 | tf_op jit(solution)/shard_map/ppermute | solution.py:103
  270.7 23.8 %copy-start.4 = (bf16[1024,1536]{1,0:T(8,128)(2,1)S(1)}, bf16[1024,1536]{1,0:T(8,128)(2,1)}, u32[]{:S(2)}) copy-start(bf16[1024,1536]{1,0:T(8,128)(2,1)} %fusion.4) | copy-start | bytes 9437188
  271.9 71.6 %collective-permute-start.9 = (bf16[4,96,1536]{2,1,0:T(8,128)(2,1)S(1)}, bf16[4,96,1536]{2,1,0:T(8,128)(2,1)S(1)}, u32[]{:S(2)}, u32[]{:S(2)}) collective-permute-start(bf16[4,96,1536]{2,1,0:T(8,128)(2,1)S(1)} %fusion.75), channel_id=1, source_target_pairs={{0,2},{1,3},{2,0},{3,1},{4,6},{5,7},{6,4},{7,5},{8,10},{9,11},{10,... | collective-permute-start | bytes 3538952 | tf_op jit(solution)/shard_map/ppermute | solution.py:103
  321.5 24.3 %collective-permute-start.15 = (bf16[96,1536]{1,0:T(8,128)(2,1)S(1)}, bf16[96,1536]{1,0:T(8,128)(2,1)S(1)}, u32[]{:S(2)}, u32[]{:S(2)}) collective-permute-start(bf16[96,1536]{1,0:T(8,128)(2,1)S(1)} %get-tuple-element.16), channel_id=1, source_target_pairs={{0,4},{1,5},{2,6},{3,7},{4,0},{5,1},{6,2},{7,3},{8,12},{9,13},{10,... | collective-permute-start | bytes 884744 | tf_op jit(solution)/shard_map/ppermute | solution.py:103
  322.2 25.3 %collective-permute-start.16 = (bf16[96,1536]{1,0:T(8,128)(2,1)S(1)}, bf16[96,1536]{1,0:T(8,128)(2,1)S(1)}, u32[]{:S(2)}, u32[]{:S(2)}) collective-permute-start(bf16[96,1536]{1,0:T(8,128)(2,1)S(1)} %get-tuple-element.18), channel_id=1, source_target_pairs={{0,8},{1,9},{2,10},{3,11},{4,12},{5,13},{6,14},{7,15},{8,0},{9,1},... | collective-permute-start | bytes 884744 | tf_op jit(solution)/shard_map/ppermute | solution.py:103
  323.5 26.0 %collective-permute-start.17 = (bf16[96,1536]{1,0:T(8,128)(2,1)S(1)}, bf16[96,1536]{1,0:T(8,128)(2,1)S(1)}, u32[]{:S(2)}, u32[]{:S(2)}) collective-permute-start(bf16[96,1536]{1,0:T(8,128)(2,1)S(1)} %get-tuple-element.17), channel_id=1, source_target_pairs={{0,12},{1,13},{2,14},{3,15},{4,8},{5,9},{6,10},{7,11},{8,4},{9,5},... | collective-permute-start | bytes 884744 | tf_op jit(solution)/shard_map/ppermute | solution.py:103
  343.9 10.0 %collective-permute-start.10 = (bf16[96,1536]{1,0:T(8,128)(2,1)S(1)}, bf16[96,1536]{1,0:T(8,128)(2,1)S(1)}, u32[]{:S(2)}, u32[]{:S(2)}) collective-permute-start(bf16[96,1536]{1,0:T(8,128)(2,1)S(1)} %get-tuple-element.19), channel_id=1, source_target_pairs={{0,4},{1,5},{2,6},{3,7},{4,0},{5,1},{6,2},{7,3},{8,12},{9,13},{10,... | collective-permute-start | bytes 884744 | tf_op jit(solution)/shard_map/ppermute | solution.py:103
  344.5 21.5 %collective-permute-start.11 = (bf16[96,1536]{1,0:T(8,128)(2,1)S(1)}, bf16[96,1536]{1,0:T(8,128)(2,1)S(1)}, u32[]{:S(2)}, u32[]{:S(2)}) collective-permute-start(bf16[96,1536]{1,0:T(8,128)(2,1)S(1)} %get-tuple-element.21), channel_id=1, source_target_pairs={{0,8},{1,9},{2,10},{3,11},{4,12},{5,13},{6,14},{7,15},{8,0},{9,1},... | collective-permute-start | bytes 884744 | tf_op jit(solution)/shard_map/ppermute | solution.py:103
  345.8 27.2 %collective-permute-start.12 = (bf16[96,1536]{1,0:T(8,128)(2,1)S(1)}, bf16[96,1536]{1,0:T(8,128)(2,1)S(1)}, u32[]{:S(2)}, u32[]{:S(2)}) collective-permute-start(bf16[96,1536]{1,0:T(8,128)(2,1)S(1)} %get-tuple-element.20), channel_id=1, source_target_pairs={{0,12},{1,13},{2,14},{3,15},{4,8},{5,9},{6,10},{7,11},{8,4},{9,5},... | collective-permute-start | bytes 884744 | tf_op jit(solution)/shard_map/ppermute | solution.py:103
  (15 other events, 48.7 us)
Sparse Core Ops, SparseCore 0:
  10.9 110.5 all-gather.1

commit v2 on v0

--- a/solution.py
+++ b/solution.py
@@ -1,6 +1,8 @@
 import jax
 import jax.numpy as jnp
 from jax import lax
+from jax.experimental import pallas as pl
+from jax.experimental.pallas import tpu as pltpu
 from jax.sharding import PartitionSpec as P
 
 L = 8192
@@ -76,9 +78,352 @@
     )
 
 
+def dot(a, b):
+    return jnp.dot(a, b, preferred_element_type=jnp.float32)
+
+
+def dot_t(a, b):
+    return lax.dot_general(a, b, (((1,), (1,)), ((), ())), preferred_element_type=jnp.float32)
+
+
+def t_dot(a, b):
+    return lax.dot_general(a, b, (((0,), (0,)), ((), ())), preferred_element_type=jnp.float32)
+
+
+def act(v):
+    return jax.nn.gelu(v.astype(jnp.float32)).astype(jnp.bfloat16)
+
+
+def after(values, *earlier):
+    return lax.optimization_barrier((values, earlier))[0]
+
+
+def call(kernel, outs, place, *args, grid=(), ins=None, out_specs=None, scratch=()):
+    whole = pl.BlockSpec(memory_space=pltpu.VMEM)
+    ins = [whole] * len(args) if ins is None else ins
+    outs = [jax.ShapeDtypeStruct(shape, dtype) for shape, dtype in outs]
+    out_specs = [whole] * len(outs) if out_specs is None else out_specs
+    light = pl.CostEstimate(flops=1, bytes_accessed=1, transcendentals=0)
+    return pl.pallas_call(
+        kernel,
+        grid=grid,
+        out_shape=outs,
+        in_specs=[pl.BlockSpec(memory_space=pltpu.SMEM)] + ins,
+        out_specs=out_specs,
+        scratch_shapes=scratch,
+        compiler_params=pltpu.CompilerParams(vmem_limit_bytes=24 * 2**20),
+        cost_estimate=light,
+    )(place, *args)
+
+
+def block(shape, *index):
+    return pl.BlockSpec(shape, lambda i: tuple(i if d else 0 for d in index))
+
+
+def place_kernel(place, kept, got, out):
+    z, x, core, y = place[0], place[1], place[2], place[3]
+    for dy in range(kept.shape[0]):
+        for dz in range(kept.shape[1]):
+            for dx in range(kept.shape[2]):
+                out[z ^ dz, x ^ dx, core, y ^ dy] = kept[dy, dz, dx]
+                out[z ^ dz, x ^ dx, 1 - core, y ^ dy] = got[dy, dz, dx]
+
+
+def placed(place, kept, got):
+    ys, depth, xs, rows, cols = kept.shape
+    (out,) = call(place_kernel, [((depth, xs, 2, ys, rows, cols), kept.dtype)], place, kept, got)
+    return out.reshape(-1, cols)
+
+
+def tap_kernel(place, rows_sent, rows_kept, tap, sent, kept):
+    weight = tap[...]
+    sent[...] = dot(rows_sent[...], weight).astype(sent.dtype)
+    kept[...] = dot(rows_kept[...], weight)
+
+
+def gated_kernel(place, near_a, near_b, act_a, act_b, tap, from_prev, from_next, hidden, gated, sent):
+    x = place[1]
+    weight = tap[...]
+    hidden[0] = near_a[...] + dot(act_a[...], weight) + from_prev[...].astype(jnp.float32)
+    hidden[1] = near_b[...] + dot(act_b[...], weight) + from_next[...].astype(jnp.float32)
+    gated[...] = act(hidden[...])
+    sent[...] = gated[1 - x]
+
+
+def hidden_grad_kernel(place, hidden, cot_a, cot_b, proj, hg_a, hg_b):
+    weight = proj[...]
+    hg_a[...] = gelu_grad(hidden[0], dot(cot_a[...], weight)).astype(jnp.bfloat16)
+    hg_b[...] = gelu_grad(hidden[1], dot(cot_b[...], weight)).astype(jnp.bfloat16)
+
+
+def term_kernel(place, rows_a, rows_b, grad_a, grad_b, mine, theirs, product):
+    core = place[2]
+    sums = t_dot(rows_a[...], grad_a[...]) + t_dot(rows_b[...], grad_b[...])
+    product[...] = sums.reshape(product.shape)
+    mine[:, 0] = product[:, core]
+    theirs[:, 0] = product[:, 1 - core].astype(theirs.dtype)
+
+
+def first_x_kernel(place, mine, got, kept, sent):
+    x = place[1]
+    kept[...] = mine[x] + got[x].astype(jnp.float32)
+    sent[...] = (mine[1 - x] + got[1 - x].astype(jnp.float32)).astype(jnp.bfloat16)
+
+
+def first_z_kernel(place, mine, got, kept, *sent):
+    z = place[0]
+    kept[...] = mine[:, z] + got[:, z].astype(jnp.float32)
+    for k, out in enumerate(sent, 1):
+        out[...] = (mine[:, z ^ k] + got[:, z ^ k].astype(jnp.float32)).astype(jnp.bfloat16)
+
+
+def then_z_kernel(place, mine, got, kept, *sent):
+    z = place[0]
+    kept[...] = mine[z] + got[z].astype(jnp.float32)
+    for k, out in enumerate(sent, 1):
+        out[...] = (mine[z ^ k] + got[z ^ k].astype(jnp.float32)).astype(jnp.bfloat16)
+
+
+def then_x_kernel(place, mine, *refs):
+    x = place[1]
+    got, kept, sent = refs[:-2], refs[-2], refs[-1]
+    for index, out in ((x, kept), (1 - x, sent)):
+        total = mine[index]
+        for term in got:
+            total = total + term[index].astype(jnp.float32)
+        out[...] = total.astype(out.dtype)
+
+
+def input_grad_kernel(place, hg_next, hg_b, hg_a, hg_prev, w0, w1, w2, in_a, in_b, cot_a, cot_b, kept, sent):
+    x = place[1]
+
+    def grad(later, here, earlier, values, cot):
+        total = dot_t(later[...], w0[...]) + dot_t(here[...], w1[...]) + dot_t(earlier[...], w2[...])
+        wide = values[...].astype(jnp.float32)
+        return (cot[...].astype(jnp.float32) + gelu_grad(wide, total)).astype(jnp.bfloat16)
+
+    grad_a = grad(hg_b, hg_a, hg_prev, in_a, cot_a)
+    grad_b = grad(hg_next, hg_b, hg_a, in_b, cot_b)
+
+    @pl.when(x == 0)
+    def _():
+        kept[...] = grad_a
+        sent[...] = grad_b
+
+    @pl.when(x != 0)
+    def _():
+        kept[...] = grad_b
+        sent[...] = grad_a
+
+
+def outputs_kernel(place, gated, got, proj, inputs, outputs):
+    x = place[1]
+    weight = proj[...]
+    for window, rows in ((x, gated[x]), (1 - x, got[...])):
+        wide = inputs[window].astype(jnp.float32) + dot_t(rows, weight)
+        outputs[window] = wide.astype(jnp.bfloat16)
+
+
+def paired(inputs, conv_weight, proj_weight, cotangent):
+    batch, local_len, chans = inputs.shape
+    hid = conv_weight.shape[2]
+    devices = lax.axis_size("seq")
+    depth = devices // 4
+    share = chans // devices
+    scale = 1.0 / float(batch * L) ** 0.5
+    me, y = lax.axis_index("seq"), lax.axis_index("groups")
+    core, x, z = me % 2, (me // 2) % 2, me // 4
+    place = jnp.stack([z, x, core, y]).astype(jnp.int32)
+    everyone = range(devices)
+    bf16, f32 = jnp.bfloat16, jnp.float32
+    tile = 256
+    steps = chans // tile
+
+    def swap(value, bits):
+        return lax.ppermute(value, "seq", [(i, i ^ bits) for i in everyone])
+
+    def up(value):
+        return lax.ppermute(value, "seq", [(i, i + 4) for i in everyone if i + 4 in everyone])
+
+    def down(value):
+        return lax.ppermute(value, "seq", [(i + 4, i) for i in everyone if i + 4 in everyone])
+
+    def pick(value, index, axis=0):
+        return lax.dynamic_index_in_dim(value, index, axis, keepdims=False)
+
+    def ordered(kept, got):
+        return jnp.where(x == 0, kept, got), jnp.where(x == 0, got, kept)
+
+    half = share // 2
+    shard = jnp.concatenate([conv_weight, proj_weight[None]], axis=0)
+    shard = lax.dynamic_slice_in_dim(shard, y * half, half, 1)
+    shard_x = swap(shard, 2)
+    in_got = swap(after(pick(inputs, 1 - x), shard_x), 2)
+
+    def along_z(k, *earlier):
+        piece = after(jnp.stack([shard[k], shard_x[k]]), *earlier)
+        return jnp.stack([piece] + [swap(piece, 4 * d) for d in range(1, depth)])
+
+    def over_y(column, *earlier):
+        column = after(column, *earlier)
+        return jnp.stack([column, lax.ppermute(column, "groups", [(0, 1), (1, 0)])])
+
+    def tap_sums(rows_sent, rows_kept, tap):
+        return call(
+            tap_kernel,
+            [((local_len, hid), bf16), ((local_len, hid), f32)],
+            place, rows_sent, rows_kept, tap,
+            grid=(hid // tile,),
+            ins=[block((local_len, chans), 0, 0)] * 2 + [block((chans, tile), 0, 1)],
+            out_specs=[block((local_len, tile), 0, 1)] * 2,
+        )
+
+    column_0 = along_z(0)
+    column_2 = along_z(2, column_0)
+    half_0 = over_y(column_0)
+    column_1 = along_z(1, column_2, half_0, in_got)
+    half_2 = over_y(column_2, half_0)
+    in_a, in_b = ordered(pick(inputs, x), in_got)
+    act_a, act_b = act(in_a), act(in_b)
+    w0 = placed(place, half_0, swap(half_0, 1))
+    to_next, near_b = tap_sums(act_b, act_a, w0)
+    from_prev = up(to_next)
+    column_p = along_z(3, column_1, half_2, to_next)
+    cot_got = swap(after(pick(cotangent, 1 - x), in_got, column_1), 2)
+    half_1 = over_y(column_1, half_2)
+    w2 = placed(place, half_2, swap(half_2, 1))
+    to_prev, near_a = tap_sums(act_a, act_b, after(w2, to_next))
+    from_next = down(to_prev)
+    half_p = over_y(column_p, half_1, to_prev)
+    w1 = placed(place, half_1, swap(after(half_1, from_prev), 1))
+    hidden, gated, gated_sent = call(
+        gated_kernel,
+        [((2, local_len, hid), f32), ((2, local_len, hid), bf16), ((local_len, hid), bf16)],
+        place, near_a, near_b, act_a, act_b, after(w1, half_p), from_prev, from_next,
+        grid=(hid // tile,),
+        ins=[block((local_len, tile), 0, 1)] * 2
+        + [block((local_len, chans), 0, 0)] * 2
+        + [block((chans, tile), 0, 1)]
+        + [block((local_len, tile), 0, 1)] * 2,
+        out_specs=[block((2, local_len, tile), 0, 0, 1)] * 2 + [block((local_len, tile), 0, 1)],
+    )
+    gated_got = swap(gated_sent, 2)
+    def term(rows_a, rows_b, grad_a, grad_b):
+        cols = 4 * share
+        part = (2, depth, share, hid)
+        mine, theirs = call(
+            term_kernel,
+            [(part, f32), (part, bf16)],
+            place, rows_a, rows_b, grad_a, grad_b,
+            grid=(depth,),
+            ins=[block((local_len, cols), 0, 1)] * 2 + [block((local_len, hid), 0, 0)] * 2,
+            out_specs=[block((2, 1, share, hid), 0, 1, 0, 0)] * 2,
+            scratch=[pltpu.VMEM((2, 2, share, hid), f32)],
+        )
+        return mine, swap(theirs, 1)
+
+    def x_first(mine, got):
+        kept, sent = call(
+            first_x_kernel,
+            [((depth, share, hid), f32), ((depth, share, hid), bf16)],
+            place, mine, got,
+            grid=(depth,),
+            ins=[block((2, 1, share, hid), 0, 1, 0, 0)] * 2,
+            out_specs=[block((1, share, hid), 1, 0, 0)] * 2,
+        )
+        return kept, swap(sent, 2)
+
+    def then_z(kept, got):
+        kept, *sent = call(
+            then_z_kernel,
+            [((share, hid), f32)] + [((share, hid), bf16)] * (depth - 1),
+            place, kept, got,
+        )
+        return [kept] + [swap(value, 4 * k) for k, value in enumerate(sent, 1)]
+
+    def z_first(mine, got):
+        kept, *sent = call(
+            first_z_kernel,
+            [((2, share, hid), f32)] + [((2, share, hid), bf16)] * (depth - 1),
+            place, mine, got,
+        )
+        return [kept] + [swap(value, 4 * k) for k, value in enumerate(sent, 1)]
+
+    def then_x(kept, *got):
+        kept, sent = call(
+            then_x_kernel, [((share, hid), f32), ((share, hid), bf16)], place, kept, *got
+        )
+        return [kept, swap(sent, 2)]
+
+    def total(parts):
+        return sum(part.astype(f32) for part in parts)
+
+    cot_a, cot_b = ordered(pick(cotangent, x), cot_got)
+    term_p = term(cot_a, cot_b, gated[0], gated[1])
+    grad_p = x_first(*term_p)
+    wp = placed(place, half_p, swap(after(half_p, from_prev, from_next), 1))
+    hg_a, hg_b = call(
+        hidden_grad_kernel,
+        [((local_len, hid), bf16)] * 2,
+        place, hidden, cot_a, cot_b, after(wp, term_p[0]),
+        grid=(hid // tile,),
+        ins=[block((2, local_len, tile), 0, 0, 1)]
+        + [block((local_len, chans), 0, 0)] * 2
+        + [block((chans, tile), 0, 1)],
+        out_specs=[block((local_len, tile), 0, 1)] * 2,
+    )
+    hg_prev, hg_next = up(hg_b), down(hg_a)
+    grad_p = then_z(after(grad_p[0], hg_prev, hg_next, gated_got), grad_p[1])
+    term_1 = term(act_a, act_b, hg_a, after(hg_b, grad_p[0]))
+    term_0 = term(act_a, act_b, hg_b, after(hg_next, term_1[0]))
+    grad_1 = x_first(after(term_1[0], term_0[0]), term_1[1])
+    term_2 = term(act_a, act_b, hg_prev, after(hg_a, grad_1[0]))
+    input_kept, input_sent = call(
+        input_grad_kernel,
+        [((local_len, chans), bf16)] * 2,
+        place, hg_next, hg_b, hg_a, after(hg_prev, term_2[0]), w0, w1, w2, in_a, in_b, cot_a, cot_b,
+        grid=(steps,),
+        ins=[block((local_len, hid), 0, 0)] * 4
+        + [block((tile, hid), 1, 0)] * 3
+        + [block((local_len, tile), 0, 1)] * 4,
+        out_specs=[block((local_len, tile), 0, 1)] * 2,
+    )
+    grad_0 = x_first(after(term_0[0], input_sent, grad_1[1], grad_p), term_0[1])
+    grad_1 = then_z(after(grad_1[0], grad_0[0]), grad_1[1])
+    (outputs,) = call(
+        outputs_kernel,
+        [(inputs.shape, bf16)],
+        place, gated, after(gated_got, grad_1[0]), wp, inputs,
+        grid=(steps,),
+        ins=[
+            block((2, local_len, hid), 0, 0, 0),
+            block((local_len, hid), 0, 0),
+            block((tile, hid), 1, 0),
+            block((2, local_len, tile), 0, 0, 1),
+        ],
+        out_specs=[block((2, local_len, tile), 0, 0, 1)],
+    )
+    grad_2 = z_first(after(term_2[0], outputs, grad_0[1], grad_1), term_2[1])
+    input_got = swap(after(input_sent, grad_0, grad_1), 2)
+    grad_2 = then_x(after(grad_2[0], outputs), *grad_2[1:])
+    grad_0 = then_z(after(grad_0[0], grad_2[0]), grad_0[1])
+    conv_grad = jnp.stack([total(grad_0), total(grad_1), total(grad_2)], axis=1)
+    return (
+        outputs,
+        jnp.stack(ordered(input_kept, input_got)),
+        conv_grad * scale,
+        total(grad_p) * scale,
+    )
+
+
 def solution(mesh):
+    def body(inputs, conv_weight, proj_weight, cotangent):
+        devices = lax.axis_size("seq")
+        by_pairs = devices == 16 and inputs.shape[0] == 2 and lax.axis_size("groups") == 2
+        return (paired if by_pairs else shards)(inputs, conv_weight, proj_weight, cotangent)
+
     return jax.shard_map(
-        shards,
+        body,
         mesh=mesh,
         in_specs=(
             P("groups", "seq", None),

time: 775 us -> 281 us (0.36)
  waiting for transfers between devices: 614 us -> 130 us
  matrix products: 69 us -> 0 us
  Pallas kernels: 0 us -> 66.6 us
  starting transfers between devices: 20.2 us -> 65.4 us
  local copies, waits for them, and re-layouts: 37.4 us -> 2.96 us
  between operations: 14.5 us -> 1.16 us
    all_to_all x1 -> x0, waiting for transfers between devices: 384 us -> none  [shards(): lax.all_to_all(stacked, 'seq', split_axis=0, concat_axis=0, tiled=True)]
    all_gather x2 -> x0, waiting for transfers between devices: 139 us -> none  [the longest x1 107 us: shards(): lax.all_gather(proj_weight, 'seq', axis=0, tiled=True)]
    dot_general x12 -> x0, matrix products: 69 us -> none  [the longest x3 21.2 us: shards(): jnp.dot(acted_rows.T, piece, preferred_element_type=jnp.float32)]
    pallas_call x0 -> x22, Pallas kernels: none -> 66.6 us  [call(): pl.pallas_call(kernel, grid=grid, out_shape=outs, in_specs=[pl.BlockSpec(...]
    ppermute x4 -> x49, starting transfers between devices: 14 us -> 65.4 us  [the longest x41 47.9 us: swap(): return lax.ppermute(value, 'seq', [(i, i ^ bits) for i in everyone])]
    ppermute x4 -> x49, waiting for transfers between devices: 90.1 us -> 130 us  [the longest x41 99.5 us: swap(): return lax.ppermute(value, 'seq', [(i, i ^ bits) for i in everyone])]
    another operation x1 -> x0, local copies, waits for them, and re-layouts: 34.4 us -> none  [shards(): stacked = jnp.stack(local_terms, axis=1)]
    reduce_sum x1 -> x0, other arithmetic: 10.4 us -> none  [shards(): jnp.sum(received.reshape(devices, share, 4, received.shape[2]), axis=0)]
  transfers between devices with their start and end apart: 7 -> 49, of which waited for: 5 -> 25; matrix products, arithmetic and copies ran while one was open for 7% -> 3% of each run, Pallas kernels for 0% -> 22%
where the time goes in v2:
time: 281 us; the launch traced here: 276 us
  waiting for transfers between devices  130 us (46%)
  Pallas kernels  66.6 us (24%)
  starting transfers between devices  65.4 us (23%)
  other arithmetic  9.88 us (4%)
  local copies, waits for them, and re-layouts  2.96 us (1%)
    ppermute x41, waiting for transfers between devices, swap(): return lax.ppermute(value, 'seq', [(i, i ^ bits) for i in everyone])  99.5 us
    pallas_call x22, Pallas kernels, call(): pl.pallas_call(kernel, grid=grid, out_shape=outs, in_specs=[pl.BlockSpec(...  66.6 us
    ppermute x41, starting transfers between devices, swap(): return lax.ppermute(value, 'seq', [(i, i ^ bits) for i in everyone])  47.9 us
    ppermute x4, waiting for transfers between devices, over_y(): return jnp.stack([column, lax.ppermute(column, 'groups', [(0, 1), (1, 0)])])  16.5 us
    ppermute x2, waiting for transfers between devices, up(): lax.ppermute(value, 'seq', [(i, i + 4) for i in everyone if i + 4 in ever...  8.35 us
    ppermute x2, starting transfers between devices, up(): lax.ppermute(value, 'seq', [(i, i + 4) for i in everyone if i + 4 in ever...  7.08 us
    ppermute x2, starting transfers between devices, down(): lax.ppermute(value, 'seq', [(i + 4, i) for i in everyone if i + 4 in ever...  6.12 us
    ppermute x2, waiting for transfers between devices, down(): lax.ppermute(value, 'seq', [(i + 4, i) for i in everyone if i + 4 in ever...  5.8 us
  transfers between devices with their start and end apart: 49, of which 25 were waited for; matrix products, arithmetic and copies ran while one was open for 3% of the time, Pallas kernels for 22%

profile of v2, /device:TPU:16, one launch (start us, length us, event | category | flops | bytes accessed | tf_op | source)
XLA Modules:
  0.0 276.2 jit_solution(8879741166442928646)
XLA Ops:
  5.9 4.5 %collective-permute-done = bf16[4,48,768]{2,1,0:T(8,128)(2,1)S(1)} collective-permute-done((bf16[4,48,768]{2,1,0:T(8,128)(2,1)S(1)}, bf16[4,48,768]{2,1,0:T(8,128)(2,1)S(1)}, u32[]{:S(2)}, u32[]{:S(2)}) %collective-permute-start) | collective-permute-done | bytes 294944 | tf_op jit(solution)/shard_map/ppermute | solution.py:243
  12.5 3.5 %collective-permute-start.3 = (bf16[2,48,768]{2,1,0:T(8,128)(2,1)S(1)}, bf16[2,48,768]{2,1,0:T(8,128)(2,1)S(1)}, u32[]{:S(2)}, u32[]{:S(2)}) collective-permute-start(bf16[2,48,768]{2,1,0:T(8,128)(2,1)S(1)} %pad_maximum_fusion.10), channel_id=1, source_target_pairs={{0,8},{1,9},{2,10},{3,11},{4,12},{5,13},{6,14},{7,15},{8,0},{9,1},... | collective-permute-start | bytes 442376 | tf_op jit(solution)/shard_map/ppermute | solution.py:243
  16.0 8.4 %collective-permute-done.4 = bf16[2,48,768]{2,1,0:T(8,128)(2,1)S(1)} collective-permute-done((bf16[2,48,768]{2,1,0:T(8,128)(2,1)S(1)}, bf16[2,48,768]{2,1,0:T(8,128)(2,1)S(1)}, u32[]{:S(2)}, u32[]{:S(2)}) %collective-permute-start.4) | collective-permute-done | bytes 147488 | tf_op jit(solution)/shard_map/ppermute | solution.py:243
  27.3 4.3 %collective-permute-start.6 = (bf16[2,48,768]{2,1,0:T(8,128)(2,1)S(1)}, bf16[2,48,768]{2,1,0:T(8,128)(2,1)}, u32[]{:S(2)}, u32[]{:S(2)}) collective-permute-start(bf16[2,48,768]{2,1,0:T(8,128)(2,1)S(1)} %pad_maximum_fusion.9), channel_id=1, source_target_pairs={{0,8},{1,9},{2,10},{3,11},{4,12},{5,13},{6,14},{7,15},{8,0},{9,1},... | collective-permute-start | bytes 442376 | tf_op jit(solution)/shard_map/ppermute | solution.py:243
  31.6 7.4 %collective-permute-done.7 = bf16[2,48,768]{2,1,0:T(8,128)(2,1)S(1)} collective-permute-done((bf16[2,48,768]{2,1,0:T(8,128)(2,1)S(1)}, bf16[2,48,768]{2,1,0:T(8,128)(2,1)S(1)}, u32[]{:S(2)}, u32[]{:S(2)}) %collective-permute-start.7) | collective-permute-done | bytes 147488 | tf_op jit(solution)/shard_map/ppermute | solution.py:243
  41.8 4.1 %collective-permute-done.1 = bf16[512,1536]{1,0:T(8,128)(2,1)S(1)} collective-permute-done((bf16[512,1536]{1,0:T(8,128)(2,1)}, bf16[512,1536]{1,0:T(8,128)(2,1)S(1)}, u32[]{:S(2)}, u32[]{:S(2)}) %collective-permute-start.1) | collective-permute-done | bytes 1572896 | tf_op jit(solution)/shard_map/ppermute | solution.py:243
  46.4 3.5 %collective-permute-start.13 = (bf16[2,48,768]{2,1,0:T(8,128)(2,1)S(1)}, bf16[2,48,768]{2,1,0:T(8,128)(2,1)S(1)}, u32[]{:S(2)}, u32[]{:S(2)}) collective-permute-start(bf16[2,48,768]{2,1,0:T(8,128)(2,1)S(1)} %pad_maximum_fusion.11), channel_id=1, source_target_pairs={{0,8},{1,9},{2,10},{3,11},{4,12},{5,13},{6,14},{7,15},{8,0},{9,1},... | collective-permute-start | bytes 442376 | tf_op jit(solution)/shard_map/ppermute | solution.py:243
  49.9 5.1 %collective-permute-done.9 = bf16[4,2,48,768]{3,2,1,0:T(8,128)(2,1)S(1)} collective-permute-done((bf16[4,2,48,768]{3,2,1,0:T(8,128)(2,1)S(1)}, bf16[4,2,48,768]{3,2,1,0:T(8,128)(2,1)S(1)}, u32[]{:S(2)}, u32[]{:S(2)}) %collective-permute-start.9) | collective-permute-done | bytes 589856 | tf_op jit(solution)/shard_map/ppermute | solution.py:269
  64.1 3.8 %shard_map.77 = (bf16[512,768]{1,0:T(8,128)(2,1)S(1)}, f32[512,768]{1,0:T(8,128)S(1)}) custom-call(s32[4]{0:T(128)S(1)} %pad_add_fusion.place, bf16[512,1536]{1,0:T(8,128)(2,1)S(1)} %get-tuple-element.142.rows_sent.rows_kept.act_b.rows_b, bf16[512,1536]{1,0:T(8,128)(2,1)S(1)} %get-tuple-element.148.rows_kept.rows_sent.act_a.rows_a, ...), custom_call_target="tpu_custom_call" | custom-call | flops 1 | bytes 1 | tf_op jit(solution)/shard_map/pallas_call | solution.py:107
  69.1 5.2 %collective-permute-start.16 = (bf16[512,768]{1,0:T(8,128)(2,1)S(1)}, bf16[512,768]{1,0:T(8,128)(2,1)S(1)}, u32[]{:S(2)}, u32[]{:S(2)}) collective-permute-start(bf16[512,768]{1,0:T(8,128)(2,1)S(1)} %get-tuple-element.76), channel_id=1, source_target_pairs={{0,4},{1,5},{2,6},{3,7},{4,8},{5,9},{6,10},{7,11},{8,12},{9,13},{1... | collective-permute-start | bytes 2359304 | tf_op jit(solution)/shard_map/ppermute | solution.py:246
  78.5 15.9 %collective-permute-done.19 = bf16[2,48,768]{2,1,0:T(8,128)(2,1)S(1)} collective-permute-done((bf16[2,48,768]{2,1,0:T(8,128)(2,1)S(1)}, bf16[2,48,768]{2,1,0:T(8,128)(2,1)S(1)}, u32[]{:S(2)}, u32[]{:S(2)}) %collective-permute-start.19) | collective-permute-done | bytes 147488 | tf_op jit(solution)/shard_map/ppermute | solution.py:243
  94.4 5.6 %collective-permute-start.18 = (bf16[2,48,768]{2,1,0:T(8,128)(2,1)S(1)}, bf16[2,48,768]{2,1,0:T(8,128)(2,1)S(1)}, u32[]{:S(2)}, u32[]{:S(2)}) collective-permute-start(bf16[2,48,768]{2,1,0:T(8,128)(2,1)S(1)} %pad_maximum_fusion.12), channel_id=1, source_target_pairs={{0,4},{1,5},{2,6},{3,7},{4,0},{5,1},{6,2},{7,3},{8,12},{9,13},{10,... | collective-permute-start | bytes 442376 | tf_op jit(solution)/shard_map/ppermute | solution.py:243
  103.9 3.8 %shard_map.78 = (bf16[512,768]{1,0:T(8,128)(2,1)S(1)}, f32[512,768]{1,0:T(8,128)S(1)}) custom-call(s32[4]{0:T(128)S(1)} %pad_add_fusion.place, bf16[512,1536]{1,0:T(8,128)(2,1)S(1)} %get-tuple-element.148.rows_kept.rows_sent.act_a.rows_a, bf16[512,1536]{1,0:T(8,128)(2,1)S(1)} %get-tuple-element.142.rows_sent.rows_kept.act_b.rows_b, ...), custom_call_target="tpu_custom_call" | custom-call | flops 1 | bytes 1 | tf_op jit(solution)/shard_map/pallas_call | solution.py:107
  110.4 11.4 %collective-permute-done.21 = bf16[4,2,48,768]{3,2,1,0:T(8,128)(2,1)S(1)} collective-permute-done((bf16[4,2,48,768]{3,2,1,0:T(8,128)(2,1)S(1)}, bf16[4,2,48,768]{3,2,1,0:T(8,128)(2,1)S(1)}, u32[]{:S(2)}, u32[]{:S(2)}) %collective-permute-start.21) | collective-permute-done | bytes 589856 | tf_op jit(solution)/shard_map/ppermute | solution.py:269
  122.0 3.9 %collective-permute-done.22.from_next = bf16[512,768]{1,0:T(8,128)(2,1)S(1)} collective-permute-done((bf16[512,768]{1,0:T(8,128)(2,1)S(1)}, bf16[512,768]{1,0:T(8,128)(2,1)S(1)}, u32[]{:S(2)}, u32[]{:S(2)}) %collective-permute-start.22) | collective-permute-done | bytes 786464 | tf_op jit(solution)/shard_map/ppermute | solution.py:249
  126.8 5.9 %shard_map.80 = (f32[2,512,768]{2,1,0:T(8,128)S(1)}, bf16[2,512,768]{2,1,0:T(8,128)(2,1)S(1)}, bf16[512,768]{1,0:T(8,128)(2,1)}) custom-call(s32[4]{0:T(128)S(1)} %pad_add_fusion.place, f32[512,768]{1,0:T(8,128)S(1)} %get-tuple-element.78.near_a, f32[512,768]{1,0:T(8,128)S(1)} %get-tuple-element.79.near_b, ...), custom_call_target="tpu_custom_call" | custom-call | flops 1 | bytes 1 | tf_op jit(solution)/shard_map/pallas_call | solution.py:107
  132.8 4.6 %shard_map.82 = (f32[2,4,96,768]{3,2,1,0:T(8,128)S(1)}, bf16[2,4,96,768]{3,2,1,0:T(8,128)(2,1)S(1)}) custom-call(s32[4]{0:T(128)S(1)} %pad_add_fusion.place, bf16[512,1536]{1,0:T(8,128)(2,1)S(1)} %get-tuple-element.147.rows_a.cot_a, bf16[512,1536]{1,0:T(8,128)(2,1)S(1)} %get-tuple-element.146.rows_b.cot_b, bf16[512,768]{1,0:T(8,128)(2,1)S(1)} %get-tuple-element.153.grad_a, ...), custom_call_target="tpu_custom_call" | custom-call | flops 1 | bytes 1 | tf_op jit(solution)/shard_map/pallas_call | solution.py:107
  140.4 5.4 %shard_map.83 = (bf16[512,768]{1,0:T(8,128)(2,1)S(1)}, bf16[512,768]{1,0:T(8,128)(2,1)S(1)}) custom-call(s32[4]{0:T(128)S(1)} %pad_add_fusion.place, f32[2,512,768]{2,1,0:T(8,128)S(1)} %get-tuple-element.89.hidden, bf16[512,1536]{1,0:T(8,128)(2,1)S(1)} %get-tuple-element.147.rows_a.cot_a, bf16[512,1536]{1,0:T(8,128)(2,1)S(1)} %get-tuple-element.146.rows_b.cot_b, ...), custom_call_target="tpu_custom_call" | custom-call | flops 1 | bytes 1 | tf_op jit(solution)/shard_map/pallas_call | solution.py:107
  147.7 4.1 %collective-permute-start.28 = (bf16[512,768]{1,0:T(8,128)(2,1)S(1)}, bf16[512,768]{1,0:T(8,128)(2,1)S(1)}, u32[]{:S(2)}, u32[]{:S(2)}) collective-permute-start(bf16[512,768]{1,0:T(8,128)(2,1)S(1)} %get-tuple-element.108.grad_a.grad_b.hg_a), channel_id=1, source_target_pairs={{4,0},{5,1},{6,2},{7,3},{8,4},{9,5},{10,6},{11,7},{12,8},{13,9},{1... | collective-permute-start | bytes 2359304 | tf_op jit(solution)/shard_map/ppermute | solution.py:249
  153.4 5.2 %collective-permute-done.23.got = bf16[512,768]{1,0:T(8,128)(2,1)S(1)} collective-permute-done((bf16[512,768]{1,0:T(8,128)(2,1)}, bf16[512,768]{1,0:T(8,128)(2,1)S(1)}, u32[]{:S(2)}, u32[]{:S(2)}) %collective-permute-start.23) | collective-permute-done | bytes 786464 | tf_op jit(solution)/shard_map/ppermute | solution.py:243
  158.6 8.3 %collective-permute-done.27.grad_a.hg_prev = bf16[512,768]{1,0:T(8,128)(2,1)S(1)} collective-permute-done((bf16[512,768]{1,0:T(8,128)(2,1)S(1)}, bf16[512,768]{1,0:T(8,128)(2,1)S(1)}, u32[]{:S(2)}, u32[]{:S(2)}) %collective-permute-start.27) | collective-permute-done | bytes 786464 | tf_op jit(solution)/shard_map/ppermute | solution.py:246
  171.0 4.7 %shard_map.86 = (f32[2,4,96,768]{3,2,1,0:T(8,128)S(1)}, bf16[2,4,96,768]{3,2,1,0:T(8,128)(2,1)S(1)}) custom-call(s32[4]{0:T(128)S(1)} %pad_add_fusion.place, bf16[512,1536]{1,0:T(8,128)(2,1)S(1)} %get-tuple-element.148.rows_kept.rows_sent.act_a.rows_a, bf16[512,1536]{1,0:T(8,128)(2,1)S(1)} %get-tuple-element.142.rows_sent.rows_kept.act_b.rows_b, ...), custom_call_target="tpu_custom_call" | custom-call | flops 1 | bytes 1 | tf_op jit(solution)/shard_map/pallas_call | solution.py:107
  175.8 5.3 %shard_map.87 = (f32[2,4,96,768]{3,2,1,0:T(8,128)S(1)}, bf16[2,4,96,768]{3,2,1,0:T(8,128)(2,1)}) custom-call(s32[4]{0:T(128)S(1)} %pad_add_fusion.place, bf16[512,1536]{1,0:T(8,128)(2,1)S(1)} %get-tuple-element.148.rows_kept.rows_sent.act_a.rows_a, bf16[512,1536]{1,0:T(8,128)(2,1)S(1)} %get-tuple-element.142.rows_sent.rows_kept.act_b.rows_b, ...), custom_call_target="tpu_custom_call" | custom-call | flops 1 | bytes 1 | tf_op jit(solution)/shard_map/pallas_call | solution.py:107
  184.4 4.6 %shard_map.89 = (f32[2,4,96,768]{3,2,1,0:T(8,128)S(1)}, bf16[2,4,96,768]{3,2,1,0:T(8,128)(2,1)S(1)}) custom-call(s32[4]{0:T(128)S(1)} %pad_add_fusion.place, bf16[512,1536]{1,0:T(8,128)(2,1)S(1)} %get-tuple-element.148.rows_kept.rows_sent.act_a.rows_a, bf16[512,1536]{1,0:T(8,128)(2,1)S(1)} %get-tuple-element.142.rows_sent.rows_kept.act_b.rows_b, ...), custom_call_target="tpu_custom_call" | custom-call | flops 1 | bytes 1 | tf_op jit(solution)/shard_map/pallas_call | solution.py:107
  192.6 13.6 %shard_map.90 = (bf16[512,1536]{1,0:T(8,128)(2,1)S(1)}, bf16[512,1536]{1,0:T(8,128)(2,1)S(1)}) custom-call(s32[4]{0:T(128)S(1)} %pad_add_fusion.place, bf16[512,768]{1,0:T(8,128)(2,1)S(1)} %collective-permute-done.28.grad_b.hg_next, bf16[512,768]{1,0:T(8,128)(2,1)S(1)} %get-tuple-element.101.grad_b.grad_a.hg_b, ...), custom_call_target="tpu_custom_call" | custom-call | flops 1 | bytes 1 | tf_op jit(solution)/shard_map/pallas_call | solution.py:107
  215.3 5.6 %collective-permute-done.38 = bf16[96,768]{1,0:T(8,128)(2,1)S(1)} collective-permute-done((bf16[96,768]{1,0:T(8,128)(2,1)S(1)}, bf16[96,768]{1,0:T(8,128)(2,1)S(1)}, u32[]{:S(2)}, u32[]{:S(2)}) %collective-permute-start.38) | collective-permute-done | bytes 147488 | tf_op jit(solution)/shard_map/ppermute | solution.py:243
  220.9 3.6 %collective-permute-done.39 = bf16[96,768]{1,0:T(8,128)(2,1)S(1)} collective-permute-done((bf16[96,768]{1,0:T(8,128)(2,1)S(1)}, bf16[96,768]{1,0:T(8,128)(2,1)S(1)}, u32[]{:S(2)}, u32[]{:S(2)}) %collective-permute-start.39) | collective-permute-done | bytes 147488 | tf_op jit(solution)/shard_map/ppermute | solution.py:243
  226.2 5.6 %shard_map.93 = bf16[2,512,1536]{2,1,0:T(8,128)(2,1)} custom-call(s32[4]{0:T(128)S(1)} %pad_add_fusion.place, bf16[2,512,768]{2,1,0:T(8,128)(2,1)S(1)} %get-tuple-element.87.gated, bf16[512,768]{1,0:T(8,128)(2,1)S(1)} %collective-permute-done.23.got, bf16[1536,768]{1,0:T(8,128)(2,1)S(1)} %bitcast.66, bf16[2,512,1536]{2,1,0:T(8,128)(2,1)S(1)} %copy-done), custom_call_target="tpu_custom_call" | custom-call | flops 1 | bytes 1 | tf_op jit(solution)/shard_map/pallas_call | solution.py:107
  236.9 5.7 %collective-permute-done.42.refs_0_ = bf16[2,96,768]{2,1,0:T(8,128)(2,1)S(1)} collective-permute-done((bf16[2,96,768]{2,1,0:T(8,128)(2,1)S(1)}, bf16[2,96,768]{2,1,0:T(8,128)(2,1)S(1)}, u32[]{:S(2)}, u32[]{:S(2)}) %collective-permute-start.42) | collective-permute-done | bytes 294944 | tf_op jit(solution)/shard_map/ppermute | solution.py:243
  242.6 12.1 %collective-permute-done.43.refs_1_ = bf16[2,96,768]{2,1,0:T(8,128)(2,1)S(1)} collective-permute-done((bf16[2,96,768]{2,1,0:T(8,128)(2,1)S(1)}, bf16[2,96,768]{2,1,0:T(8,128)(2,1)S(1)}, u32[]{:S(2)}, u32[]{:S(2)}) %collective-permute-start.43) | collective-permute-done | bytes 294944 | tf_op jit(solution)/shard_map/ppermute | solution.py:243
  254.7 7.3 %collective-permute-done.44.refs_2_ = bf16[2,96,768]{2,1,0:T(8,128)(2,1)S(1)} collective-permute-done((bf16[2,96,768]{2,1,0:T(8,128)(2,1)S(1)}, bf16[2,96,768]{2,1,0:T(8,128)(2,1)S(1)}, u32[]{:S(2)}, u32[]{:S(2)}) %collective-permute-start.44) | collective-permute-done | bytes 294944 | tf_op jit(solution)/shard_map/ppermute | solution.py:243
  267.9 5.0 %collective-permute-done.47 = bf16[96,768]{1,0:T(8,128)(2,1)S(1)} collective-permute-done((bf16[96,768]{1,0:T(8,128)(2,1)S(1)}, bf16[96,768]{1,0:T(8,128)(2,1)S(1)}, u32[]{:S(2)}, u32[]{:S(2)}) %collective-permute-start.47) | collective-permute-done | bytes 147488 | tf_op jit(solution)/shard_map/ppermute | solution.py:243
  (124 shorter events, 77.9 us)
Async XLA Ops:
  10.5 35.5 %collective-permute-start.1 = (bf16[512,1536]{1,0:T(8,128)(2,1)}, bf16[512,1536]{1,0:T(8,128)(2,1)S(1)}, u32[]{:S(2)}, u32[]{:S(2)}) collective-permute-start(bf16[512,1536]{1,0:T(8,128)(2,1)} %dynamic-slice_bitcast_fusion.1), channel_id=1, source_target_pairs={{0,2},{1,3},{2,0},{3,1},{4,6},{5,7},{6,4},{7,5},{8,10},{9,11},{10,... | collective-permute-start | bytes 4718600 | tf_op jit(solution)/shard_map/ppermute | solution.py:243
  12.0 12.4 %collective-permute-start.4 = (bf16[2,48,768]{2,1,0:T(8,128)(2,1)S(1)}, bf16[2,48,768]{2,1,0:T(8,128)(2,1)S(1)}, u32[]{:S(2)}, u32[]{:S(2)}) collective-permute-start(bf16[2,48,768]{2,1,0:T(8,128)(2,1)S(1)} %pad_maximum_fusion.10), channel_id=1, source_target_pairs={{0,12},{1,13},{2,14},{3,15},{4,8},{5,9},{6,10},{7,11},{8,4},{9,5},... | collective-permute-start | bytes 442376 | tf_op jit(solution)/shard_map/ppermute | solution.py:243
  24.5 16.3 %collective-permute-start.8 = (bf16[4,2,48,768]{3,2,1,0:T(8,128)(2,1)S(1)}, bf16[4,2,48,768]{3,2,1,0:T(8,128)(2,1)S(1)}, u32[]{:S(2)}, u32[]{:S(2)}) collective-permute-start(bf16[4,2,48,768]{3,2,1,0:T(8,128)(2,1)S(1)} %pad_maximum_fusion.5), channel_id=1, source_target_pairs={{0,16},{16,0},{1,17},{17,1},{2,18},{18,2},{3,19},{19,3},{4,20},{20... | collective-permute-start | bytes 1769480 | tf_op jit(solution)/shard_map/ppermute | solution.py:269
  26.1 12.9 %collective-permute-start.7 = (bf16[2,48,768]{2,1,0:T(8,128)(2,1)S(1)}, bf16[2,48,768]{2,1,0:T(8,128)(2,1)S(1)}, u32[]{:S(2)}, u32[]{:S(2)}) collective-permute-start(bf16[2,48,768]{2,1,0:T(8,128)(2,1)S(1)} %pad_maximum_fusion.9), channel_id=1, source_target_pairs={{0,12},{1,13},{2,14},{3,15},{4,8},{5,9},{6,10},{7,11},{8,4},{9,5},... | collective-permute-start | bytes 442376 | tf_op jit(solution)/shard_map/ppermute | solution.py:243
  27.3 12.1 %collective-permute-start.6 = (bf16[2,48,768]{2,1,0:T(8,128)(2,1)S(1)}, bf16[2,48,768]{2,1,0:T(8,128)(2,1)}, u32[]{:S(2)}, u32[]{:S(2)}) collective-permute-start(bf16[2,48,768]{2,1,0:T(8,128)(2,1)S(1)} %pad_maximum_fusion.9), channel_id=1, source_target_pairs={{0,8},{1,9},{2,10},{3,11},{4,12},{5,13},{6,14},{7,15},{8,0},{9,1},... | collective-permute-start | bytes 442376 | tf_op jit(solution)/shard_map/ppermute | solution.py:243
  40.9 14.1 %collective-permute-start.9 = (bf16[4,2,48,768]{3,2,1,0:T(8,128)(2,1)S(1)}, bf16[4,2,48,768]{3,2,1,0:T(8,128)(2,1)S(1)}, u32[]{:S(2)}, u32[]{:S(2)}) collective-permute-start(bf16[4,2,48,768]{3,2,1,0:T(8,128)(2,1)S(1)} %pad_maximum_fusion.6), channel_id=1, source_target_pairs={{0,16},{16,0},{1,17},{17,1},{2,18},{18,2},{3,19},{19,3},{4,20},{20... | collective-permute-start | bytes 1769480 | tf_op jit(solution)/shard_map/ppermute | solution.py:269
  41.7 21.6 %collective-permute-start.11 = (bf16[2,4,2,48,768]{4,3,2,1,0:T(8,128)(2,1)S(1)}, bf16[2,4,2,48,768]{4,3,2,1,0:T(8,128)(2,1)S(1)}, u32[]{:S(2)}, u32[]{:S(2)}) collective-permute-start(bf16[2,4,2,48,768]{4,3,2,1,0:T(8,128)(2,1)S(1)} %pad_maximum_fusion.1.kept), channel_id=1, source_target_pairs={{0,1},{1,0},{2,3},{3,2},{4,5},{5,4},{6,7},{7,6},{8,9},{9,8},{10,11... | collective-permute-start | bytes 3538952 | tf_op jit(solution)/shard_map/ppermute | solution.py:243
  46.0 12.0 %collective-permute-start.14 = (bf16[2,48,768]{2,1,0:T(8,128)(2,1)S(1)}, bf16[2,48,768]{2,1,0:T(8,128)(2,1)S(1)}, u32[]{:S(2)}, u32[]{:S(2)}) collective-permute-start(bf16[2,48,768]{2,1,0:T(8,128)(2,1)S(1)} %pad_maximum_fusion.11), channel_id=1, source_target_pairs={{0,12},{1,13},{2,14},{3,15},{4,8},{5,9},{6,10},{7,11},{8,4},{9,5},... | collective-permute-start | bytes 442376 | tf_op jit(solution)/shard_map/ppermute | solution.py:243
  55.2 48.0 %collective-permute-start.10 = (bf16[2,4,2,48,768]{4,3,2,1,0:T(8,128)(2,1)S(1)}, bf16[2,4,2,48,768]{4,3,2,1,0:T(8,128)(2,1)S(1)}, u32[]{:S(2)}, u32[]{:S(2)}) collective-permute-start(bf16[2,4,2,48,768]{4,3,2,1,0:T(8,128)(2,1)S(1)} %pad_maximum_fusion.2.kept), channel_id=1, source_target_pairs={{0,1},{1,0},{2,3},{3,2},{4,5},{5,4},{6,7},{7,6},{8,9},{9,8},{10,11... | collective-permute-start | bytes 3538952 | tf_op jit(solution)/shard_map/ppermute | solution.py:243
  58.1 51.7 %collective-permute-start.15 = (bf16[4,2,48,768]{3,2,1,0:T(8,128)(2,1)S(1)}, bf16[4,2,48,768]{3,2,1,0:T(8,128)(2,1)S(1)}, u32[]{:S(2)}, u32[]{:S(2)}) collective-permute-start(bf16[4,2,48,768]{3,2,1,0:T(8,128)(2,1)S(1)} %pad_maximum_fusion.7), channel_id=1, source_target_pairs={{0,16},{16,0},{1,17},{17,1},{2,18},{18,2},{3,19},{19,3},{4,20},{20... | collective-permute-start | bytes 1769480 | tf_op jit(solution)/shard_map/ppermute | solution.py:269
  59.7 66.2 %collective-permute-start.24 = (bf16[512,1536]{1,0:T(8,128)(2,1)S(1)}, bf16[512,1536]{1,0:T(8,128)(2,1)S(1)}, u32[]{:S(2)}, u32[]{:S(2)}) collective-permute-start(bf16[512,1536]{1,0:T(8,128)(2,1)S(1)} %dynamic-slice_bitcast_fusion), channel_id=1, source_target_pairs={{0,2},{1,3},{2,0},{3,1},{4,6},{5,7},{6,4},{7,5},{8,10},{9,11},{10,... | collective-permute-start | bytes 4718600 | tf_op jit(solution)/shard_map/ppermute | solution.py:243
  69.1 41.3 %collective-permute-start.16 = (bf16[512,768]{1,0:T(8,128)(2,1)S(1)}, bf16[512,768]{1,0:T(8,128)(2,1)S(1)}, u32[]{:S(2)}, u32[]{:S(2)}) collective-permute-start(bf16[512,768]{1,0:T(8,128)(2,1)S(1)} %get-tuple-element.76), channel_id=1, source_target_pairs={{0,4},{1,5},{2,6},{3,7},{4,8},{5,9},{6,10},{7,11},{8,12},{9,13},{1... | collective-permute-start | bytes 2359304 | tf_op jit(solution)/shard_map/ppermute | solution.py:246
  76.9 17.5 %collective-permute-start.19 = (bf16[2,48,768]{2,1,0:T(8,128)(2,1)S(1)}, bf16[2,48,768]{2,1,0:T(8,128)(2,1)S(1)}, u32[]{:S(2)}, u32[]{:S(2)}) collective-permute-start(bf16[2,48,768]{2,1,0:T(8,128)(2,1)S(1)} %pad_maximum_fusion.12), channel_id=1, source_target_pairs={{0,8},{1,9},{2,10},{3,11},{4,12},{5,13},{6,14},{7,15},{8,0},{9,1},... | collective-permute-start | bytes 442376 | tf_op jit(solution)/shard_map/ppermute | solution.py:243
  107.7 18.1 %collective-permute-start.22 = (bf16[512,768]{1,0:T(8,128)(2,1)S(1)}, bf16[512,768]{1,0:T(8,128)(2,1)S(1)}, u32[]{:S(2)}, u32[]{:S(2)}) collective-permute-start(bf16[512,768]{1,0:T(8,128)(2,1)S(1)} %get-tuple-element.84), channel_id=1, source_target_pairs={{4,0},{5,1},{6,2},{7,3},{8,4},{9,5},{10,6},{11,7},{12,8},{13,9},{1... | collective-permute-start | bytes 2359304 | tf_op jit(solution)/shard_map/ppermute | solution.py:249
  109.9 12.0 %collective-permute-start.21 = (bf16[4,2,48,768]{3,2,1,0:T(8,128)(2,1)S(1)}, bf16[4,2,48,768]{3,2,1,0:T(8,128)(2,1)S(1)}, u32[]{:S(2)}, u32[]{:S(2)}) collective-permute-start(bf16[4,2,48,768]{3,2,1,0:T(8,128)(2,1)S(1)} %pad_maximum_fusion.8), channel_id=1, source_target_pairs={{0,16},{16,0},{1,17},{17,1},{2,18},{18,2},{3,19},{19,3},{4,20},{20... | collective-permute-start | bytes 1769480 | tf_op jit(solution)/shard_map/ppermute | solution.py:269
  110.4 15.6 %collective-permute-start.17 = (bf16[2,4,2,48,768]{4,3,2,1,0:T(8,128)(2,1)S(1)}, bf16[2,4,2,48,768]{4,3,2,1,0:T(8,128)(2,1)S(1)}, u32[]{:S(2)}, u32[]{:S(2)}) collective-permute-start(bf16[2,4,2,48,768]{4,3,2,1,0:T(8,128)(2,1)S(1)} %pad_maximum_fusion.3.kept), channel_id=1, source_target_pairs={{0,1},{1,0},{2,3},{3,2},{4,5},{5,4},{6,7},{7,6},{8,9},{9,8},{10,11... | collective-permute-start | bytes 3538952 | tf_op jit(solution)/shard_map/ppermute | solution.py:243
  125.8 13.8 %collective-permute-start.25 = (bf16[2,4,2,48,768]{4,3,2,1,0:T(8,128)(2,1)S(1)}, bf16[2,4,2,48,768]{4,3,2,1,0:T(8,128)(2,1)S(1)}, u32[]{:S(2)}, u32[]{:S(2)}) collective-permute-start(bf16[2,4,2,48,768]{4,3,2,1,0:T(8,128)(2,1)S(1)} %pad_maximum_fusion.4.kept), channel_id=1, source_target_pairs={{0,1},{1,0},{2,3},{3,2},{4,5},{5,4},{6,7},{7,6},{8,9},{9,8},{10,11... | collective-permute-start | bytes 3538952 | tf_op jit(solution)/shard_map/ppermute | solution.py:243
  137.4 14.4 %collective-permute-start.26 = (bf16[2,4,96,768]{3,2,1,0:T(8,128)(2,1)S(1)}, bf16[2,4,96,768]{3,2,1,0:T(8,128)(2,1)S(1)}, u32[]{:S(2)}, u32[]{:S(2)}) collective-permute-start(bf16[2,4,96,768]{3,2,1,0:T(8,128)(2,1)S(1)} %get-tuple-element.96), channel_id=1, source_target_pairs={{0,1},{1,0},{2,3},{3,2},{4,5},{5,4},{6,7},{7,6},{8,9},{9,8},{10,11... | collective-permute-start | bytes 3538952 | tf_op jit(solution)/shard_map/ppermute | solution.py:243
  138.0 20.6 %collective-permute-start.23 = (bf16[512,768]{1,0:T(8,128)(2,1)}, bf16[512,768]{1,0:T(8,128)(2,1)S(1)}, u32[]{:S(2)}, u32[]{:S(2)}) collective-permute-start(bf16[512,768]{1,0:T(8,128)(2,1)} %get-tuple-element.88), channel_id=1, source_target_pairs={{0,2},{1,3},{2,0},{3,1},{4,6},{5,7},{6,4},{7,5},{8,10},{9,11},{10,... | collective-permute-start | bytes 2359304 | tf_op jit(solution)/shard_map/ppermute | solution.py:243
  145.8 21.1 %collective-permute-start.27 = (bf16[512,768]{1,0:T(8,128)(2,1)S(1)}, bf16[512,768]{1,0:T(8,128)(2,1)S(1)}, u32[]{:S(2)}, u32[]{:S(2)}) collective-permute-start(bf16[512,768]{1,0:T(8,128)(2,1)S(1)} %get-tuple-element.101.grad_b.grad_a.hg_b), channel_id=1, source_target_pairs={{0,4},{1,5},{2,6},{3,7},{4,8},{5,9},{6,10},{7,11},{8,12},{9,13},{1... | collective-permute-start | bytes 2359304 | tf_op jit(solution)/shard_map/ppermute | solution.py:246
  147.7 21.1 %collective-permute-start.28 = (bf16[512,768]{1,0:T(8,128)(2,1)S(1)}, bf16[512,768]{1,0:T(8,128)(2,1)S(1)}, u32[]{:S(2)}, u32[]{:S(2)}) collective-permute-start(bf16[512,768]{1,0:T(8,128)(2,1)S(1)} %get-tuple-element.108.grad_a.grad_b.hg_a), channel_id=1, source_target_pairs={{4,0},{5,1},{6,2},{7,3},{8,4},{9,5},{10,6},{11,7},{12,8},{13,9},{1... | collective-permute-start | bytes 2359304 | tf_op jit(solution)/shard_map/ppermute | solution.py:249
  152.9 17.4 %collective-permute-start.29 = (bf16[4,96,768]{2,1,0:T(8,128)(2,1)S(1)}, bf16[4,96,768]{2,1,0:T(8,128)(2,1)S(1)}, u32[]{:S(2)}, u32[]{:S(2)}) collective-permute-start(bf16[4,96,768]{2,1,0:T(8,128)(2,1)S(1)} %get-tuple-element.99), channel_id=1, source_target_pairs={{0,2},{1,3},{2,0},{3,1},{4,6},{5,7},{6,4},{7,5},{8,10},{9,11},{10,... | collective-permute-start | bytes 1769480 | tf_op jit(solution)/shard_map/ppermute | solution.py:243
  181.1 25.2 %collective-permute-start.35 = (bf16[2,4,96,768]{3,2,1,0:T(8,128)(2,1)}, bf16[2,4,96,768]{3,2,1,0:T(8,128)(2,1)S(1)}, u32[]{:S(2)}, u32[]{:S(2)}) collective-permute-start(bf16[2,4,96,768]{3,2,1,0:T(8,128)(2,1)} %get-tuple-element.117), channel_id=1, source_target_pairs={{0,1},{1,0},{2,3},{3,2},{4,5},{5,4},{6,7},{7,6},{8,9},{9,8},{10,11... | collective-permute-start | bytes 3538952 | tf_op jit(solution)/shard_map/ppermute | solution.py:243
  182.6 23.7 %collective-permute-start.31 = (bf16[4,96,768]{2,1,0:T(8,128)(2,1)S(1)}, bf16[4,96,768]{2,1,0:T(8,128)(2,1)S(1)}, u32[]{:S(2)}, u32[]{:S(2)}) collective-permute-start(bf16[4,96,768]{2,1,0:T(8,128)(2,1)S(1)} %get-tuple-element.112), channel_id=1, source_target_pairs={{0,2},{1,3},{2,0},{3,1},{4,6},{5,7},{6,4},{7,5},{8,10},{9,11},{10,... | collective-permute-start | bytes 1769480 | tf_op jit(solution)/shard_map/ppermute | solution.py:243
  189.0 42.8 %collective-permute-start.41 = (bf16[2,4,96,768]{3,2,1,0:T(8,128)(2,1)S(1)}, bf16[2,4,96,768]{3,2,1,0:T(8,128)(2,1)S(1)}, u32[]{:S(2)}, u32[]{:S(2)}) collective-permute-start(bf16[2,4,96,768]{3,2,1,0:T(8,128)(2,1)S(1)} %get-tuple-element.129), channel_id=1, source_target_pairs={{0,1},{1,0},{2,3},{3,2},{4,5},{5,4},{6,7},{7,6},{8,9},{9,8},{10,11... | collective-permute-start | bytes 3538952 | tf_op jit(solution)/shard_map/ppermute | solution.py:243
  189.1 17.2 %collective-permute-start.33 = (bf16[96,768]{1,0:T(8,128)(2,1)S(1)}, bf16[96,768]{1,0:T(8,128)(2,1)S(1)}, u32[]{:S(2)}, u32[]{:S(2)}) collective-permute-start(bf16[96,768]{1,0:T(8,128)(2,1)S(1)} %get-tuple-element.114), channel_id=1, source_target_pairs={{0,8},{1,9},{2,10},{3,11},{4,12},{5,13},{6,14},{7,15},{8,0},{9,1},... | collective-permute-start | bytes 442376 | tf_op jit(solution)/shard_map/ppermute | solution.py:243
  190.9 15.4 %collective-permute-start.34 = (bf16[96,768]{1,0:T(8,128)(2,1)S(1)}, bf16[96,768]{1,0:T(8,128)(2,1)S(1)}, u32[]{:S(2)}, u32[]{:S(2)}) collective-permute-start(bf16[96,768]{1,0:T(8,128)(2,1)S(1)} %get-tuple-element.115), channel_id=1, source_target_pairs={{0,12},{1,13},{2,14},{3,15},{4,8},{5,9},{6,10},{7,11},{8,4},{9,5},... | collective-permute-start | bytes 442376 | tf_op jit(solution)/shard_map/ppermute | solution.py:243
  207.4 17.2 %collective-permute-start.36 = (bf16[4,96,768]{2,1,0:T(8,128)(2,1)S(1)}, bf16[4,96,768]{2,1,0:T(8,128)(2,1)S(1)}, u32[]{:S(2)}, u32[]{:S(2)}) collective-permute-start(bf16[4,96,768]{2,1,0:T(8,128)(2,1)S(1)} %get-tuple-element.123), channel_id=1, source_target_pairs={{0,2},{1,3},{2,0},{3,1},{4,6},{5,7},{6,4},{7,5},{8,10},{9,11},{10,... | collective-permute-start | bytes 1769480 | tf_op jit(solution)/shard_map/ppermute | solution.py:243
  210.3 14.3 %collective-permute-start.39 = (bf16[96,768]{1,0:T(8,128)(2,1)S(1)}, bf16[96,768]{1,0:T(8,128)(2,1)S(1)}, u32[]{:S(2)}, u32[]{:S(2)}) collective-permute-start(bf16[96,768]{1,0:T(8,128)(2,1)S(1)} %get-tuple-element.126), channel_id=1, source_target_pairs={{0,12},{1,13},{2,14},{3,15},{4,8},{5,9},{6,10},{7,11},{8,4},{9,5},... | collective-permute-start | bytes 442376 | tf_op jit(solution)/shard_map/ppermute | solution.py:243
  224.6 49.5 %collective-permute-start.40 = (bf16[512,1536]{1,0:T(8,128)(2,1)S(1)}, bf16[512,1536]{1,0:T(8,128)(2,1)S(1)}, u32[]{:S(2)}, u32[]{:S(2)}) collective-permute-start(bf16[512,1536]{1,0:T(8,128)(2,1)S(1)} %get-tuple-element.127), channel_id=1, source_target_pairs={{0,2},{1,3},{2,0},{3,1},{4,6},{5,7},{6,4},{7,5},{8,10},{9,11},{10,... | collective-permute-start | bytes 4718600 | tf_op jit(solution)/shard_map/ppermute | solution.py:243
  232.6 22.0 %collective-permute-start.43 = (bf16[2,96,768]{2,1,0:T(8,128)(2,1)S(1)}, bf16[2,96,768]{2,1,0:T(8,128)(2,1)S(1)}, u32[]{:S(2)}, u32[]{:S(2)}) collective-permute-start(bf16[2,96,768]{2,1,0:T(8,128)(2,1)S(1)} %get-tuple-element.133), channel_id=1, source_target_pairs={{0,8},{1,9},{2,10},{3,11},{4,12},{5,13},{6,14},{7,15},{8,0},{9,1},... | collective-permute-start | bytes 884744 | tf_op jit(solution)/shard_map/ppermute | solution.py:243
  234.6 27.4 %collective-permute-start.44 = (bf16[2,96,768]{2,1,0:T(8,128)(2,1)S(1)}, bf16[2,96,768]{2,1,0:T(8,128)(2,1)S(1)}, u32[]{:S(2)}, u32[]{:S(2)}) collective-permute-start(bf16[2,96,768]{2,1,0:T(8,128)(2,1)S(1)} %get-tuple-element.134), channel_id=1, source_target_pairs={{0,12},{1,13},{2,14},{3,15},{4,8},{5,9},{6,10},{7,11},{8,4},{9,5},... | collective-permute-start | bytes 884744 | tf_op jit(solution)/shard_map/ppermute | solution.py:243
  (21 other events, 169.7 us)

commit v3 on v2

--- a/solution.py
+++ b/solution.py
@@ -6,6 +6,7 @@
 from jax.sharding import PartitionSpec as P
 
 L = 8192
+LONG = 10**10
 
 
 def from_behind(block, axis, distance):
@@ -98,12 +99,12 @@
     return lax.optimization_barrier((values, earlier))[0]
 
 
-def call(kernel, outs, place, *args, grid=(), ins=None, out_specs=None, scratch=()):
+def call(kernel, outs, place, *args, grid=(), ins=None, out_specs=None, scratch=(), work=1):
     whole = pl.BlockSpec(memory_space=pltpu.VMEM)
     ins = [whole] * len(args) if ins is None else ins
     outs = [jax.ShapeDtypeStruct(shape, dtype) for shape, dtype in outs]
     out_specs = [whole] * len(outs) if out_specs is None else out_specs
-    light = pl.CostEstimate(flops=1, bytes_accessed=1, transcendentals=0)
+    light = pl.CostEstimate(flops=work, bytes_accessed=1, transcendentals=0)
     return pl.pallas_call(
         kernel,
         grid=grid,
@@ -141,11 +142,16 @@
     kept[...] = dot(rows_kept[...], weight)
 
 
-def gated_kernel(place, near_a, near_b, act_a, act_b, tap, from_prev, from_next, hidden, gated, sent):
+def own_tap_kernel(place, near_a, near_b, act_a, act_b, tap, sum_a, sum_b):
+    weight = tap[...]
+    sum_a[...] = near_a[...] + dot(act_a[...], weight)
+    sum_b[...] = near_b[...] + dot(act_b[...], weight)
+
+
+def gated_kernel(place, near_a, near_b, from_prev, from_next, hidden, gated, sent):
     x = place[1]
-    weight = tap[...]
-    hidden[0] = near_a[...] + dot(act_a[...], weight) + from_prev[...].astype(jnp.float32)
-    hidden[1] = near_b[...] + dot(act_b[...], weight) + from_next[...].astype(jnp.float32)
+    hidden[0] = near_a[...] + from_prev[...].astype(jnp.float32)
+    hidden[1] = near_b[...] + from_next[...].astype(jnp.float32)
     gated[...] = act(hidden[...])
     sent[...] = gated[1 - x]
 
@@ -170,28 +176,11 @@
     sent[...] = (mine[1 - x] + got[1 - x].astype(jnp.float32)).astype(jnp.bfloat16)
 
 
-def first_z_kernel(place, mine, got, kept, *sent):
-    z = place[0]
-    kept[...] = mine[:, z] + got[:, z].astype(jnp.float32)
-    for k, out in enumerate(sent, 1):
-        out[...] = (mine[:, z ^ k] + got[:, z ^ k].astype(jnp.float32)).astype(jnp.bfloat16)
-
-
 def then_z_kernel(place, mine, got, kept, *sent):
     z = place[0]
     kept[...] = mine[z] + got[z].astype(jnp.float32)
     for k, out in enumerate(sent, 1):
         out[...] = (mine[z ^ k] + got[z ^ k].astype(jnp.float32)).astype(jnp.bfloat16)
-
-
-def then_x_kernel(place, mine, *refs):
-    x = place[1]
-    got, kept, sent = refs[:-2], refs[-2], refs[-1]
-    for index, out in ((x, kept), (1 - x, sent)):
-        total = mine[index]
-        for term in got:
-            total = total + term[index].astype(jnp.float32)
-        out[...] = total.astype(out.dtype)
 
 
 def input_grad_kernel(place, hg_next, hg_b, hg_a, hg_prev, w0, w1, w2, in_a, in_b, cot_a, cot_b, kept, sent):
@@ -281,34 +270,43 @@
     column_0 = along_z(0)
     column_2 = along_z(2, column_0)
     half_0 = over_y(column_0)
-    column_1 = along_z(1, column_2, half_0, in_got)
-    half_2 = over_y(column_2, half_0)
     in_a, in_b = ordered(pick(inputs, x), in_got)
     act_a, act_b = act(in_a), act(in_b)
+    column_1 = along_z(1, column_2, half_0, act_a, act_b)
+    half_2 = over_y(column_2, half_0)
     w0 = placed(place, half_0, swap(half_0, 1))
     to_next, near_b = tap_sums(act_b, act_a, w0)
     from_prev = up(to_next)
-    column_p = along_z(3, column_1, half_2, to_next)
     cot_got = swap(after(pick(cotangent, 1 - x), in_got, column_1), 2)
     half_1 = over_y(column_1, half_2)
-    w2 = placed(place, half_2, swap(half_2, 1))
+    piece_p = after(jnp.stack([shard[3], shard_x[3]]), column_1, half_2, to_next)
+    column_p = [swap(piece_p, 12), swap(piece_p, 8)]
+    w2 = placed(place, half_2, swap(after(half_2, to_next), 1))
+    column_p = jnp.stack([piece_p, swap(after(piece_p, w2), 4)] + column_p[::-1])
     to_prev, near_a = tap_sums(act_a, act_b, after(w2, to_next))
     from_next = down(to_prev)
     half_p = over_y(column_p, half_1, to_prev)
-    w1 = placed(place, half_1, swap(after(half_1, from_prev), 1))
+    w1 = placed(place, half_1, swap(half_1, 1))
+    near_a, near_b = call(
+        own_tap_kernel,
+        [((local_len, hid), f32)] * 2,
+        place, near_a, near_b, act_a, act_b, w1,
+        grid=(hid // tile,),
+        ins=[block((local_len, tile), 0, 1)] * 2
+        + [block((local_len, chans), 0, 0)] * 2
+        + [block((chans, tile), 0, 1)],
+        out_specs=[block((local_len, tile), 0, 1)] * 2,
+    )
     hidden, gated, gated_sent = call(
         gated_kernel,
         [((2, local_len, hid), f32), ((2, local_len, hid), bf16), ((local_len, hid), bf16)],
-        place, near_a, near_b, act_a, act_b, after(w1, half_p), from_prev, from_next,
+        place, near_a, near_b, from_prev, after(from_next, near_a),
         grid=(hid // tile,),
-        ins=[block((local_len, tile), 0, 1)] * 2
-        + [block((local_len, chans), 0, 0)] * 2
-        + [block((chans, tile), 0, 1)]
-        + [block((local_len, tile), 0, 1)] * 2,
+        ins=[block((local_len, tile), 0, 1)] * 4,
         out_specs=[block((2, local_len, tile), 0, 0, 1)] * 2 + [block((local_len, tile), 0, 1)],
     )
     gated_got = swap(gated_sent, 2)
-    def term(rows_a, rows_b, grad_a, grad_b):
+    def term(rows_a, rows_b, grad_a, grad_b, work=1):
         cols = 4 * share
         part = (2, depth, share, hid)
         mine, theirs = call(
@@ -319,6 +317,7 @@
             ins=[block((local_len, cols), 0, 1)] * 2 + [block((local_len, hid), 0, 0)] * 2,
             out_specs=[block((2, 1, share, hid), 0, 1, 0, 0)] * 2,
             scratch=[pltpu.VMEM((2, 2, share, hid), f32)],
+            work=work,
         )
         return mine, swap(theirs, 1)
 
@@ -341,27 +340,12 @@
         )
         return [kept] + [swap(value, 4 * k) for k, value in enumerate(sent, 1)]
 
-    def z_first(mine, got):
-        kept, *sent = call(
-            first_z_kernel,
-            [((2, share, hid), f32)] + [((2, share, hid), bf16)] * (depth - 1),
-            place, mine, got,
-        )
-        return [kept] + [swap(value, 4 * k) for k, value in enumerate(sent, 1)]
-
-    def then_x(kept, *got):
-        kept, sent = call(
-            then_x_kernel, [((share, hid), f32), ((share, hid), bf16)], place, kept, *got
-        )
-        return [kept, swap(sent, 2)]
-
     def total(parts):
         return sum(part.astype(f32) for part in parts)
 
     cot_a, cot_b = ordered(pick(cotangent, x), cot_got)
     term_p = term(cot_a, cot_b, gated[0], gated[1])
-    grad_p = x_first(*term_p)
-    wp = placed(place, half_p, swap(after(half_p, from_prev, from_next), 1))
+    wp = placed(place, half_p, swap(after(half_p, from_prev, from_next, near_a, near_b), 1))
     hg_a, hg_b = call(
         hidden_grad_kernel,
         [((local_len, hid), bf16)] * 2,
@@ -371,29 +355,39 @@
         + [block((local_len, chans), 0, 0)] * 2
         + [block((chans, tile), 0, 1)],
         out_specs=[block((local_len, tile), 0, 1)] * 2,
+        work=LONG,
     )
     hg_prev, hg_next = up(hg_b), down(hg_a)
-    grad_p = then_z(after(grad_p[0], hg_prev, hg_next, gated_got), grad_p[1])
+    grad_p = x_first(after(term_p[0], hg_a, gated_got), term_p[1])
     term_1 = term(act_a, act_b, hg_a, after(hg_b, grad_p[0]))
-    term_0 = term(act_a, act_b, hg_b, after(hg_next, term_1[0]))
-    grad_1 = x_first(after(term_1[0], term_0[0]), term_1[1])
+    term_0 = term(act_a, act_b, hg_b, after(hg_next, term_1[0], hg_prev), LONG)
+    grad_1 = x_first(after(term_1[0], term_0[0], grad_p[1]), term_1[1])
     term_2 = term(act_a, act_b, hg_prev, after(hg_a, grad_1[0]))
-    input_kept, input_sent = call(
-        input_grad_kernel,
-        [((local_len, chans), bf16)] * 2,
-        place, hg_next, hg_b, hg_a, after(hg_prev, term_2[0]), w0, w1, w2, in_a, in_b, cot_a, cot_b,
-        grid=(steps,),
-        ins=[block((local_len, hid), 0, 0)] * 4
-        + [block((tile, hid), 1, 0)] * 3
-        + [block((local_len, tile), 0, 1)] * 4,
-        out_specs=[block((local_len, tile), 0, 1)] * 2,
-    )
-    grad_0 = x_first(after(term_0[0], input_sent, grad_1[1], grad_p), term_0[1])
-    grad_1 = then_z(after(grad_1[0], grad_0[0]), grad_1[1])
+    grad_p = then_z(after(grad_p[0], term_2[0]), grad_p[1])
+
+    def input_grads(part, *earlier):
+        cols = [block((local_len, tile), 0, 1)]
+        first = part * steps // 2
+        late = pl.BlockSpec((local_len, tile), lambda i: (0, i + first))
+        taps = pl.BlockSpec((tile, hid), lambda i: (i + first, 0))
+        return call(
+            input_grad_kernel,
+            [((local_len, chans // 2), bf16)] * 2,
+            place, hg_next, hg_b, hg_a, after(hg_prev, *earlier), w0, w1, w2, in_a, in_b, cot_a, cot_b,
+            grid=(steps // 2,),
+            ins=[block((local_len, hid), 0, 0)] * 4 + [taps] * 3 + [late] * 4,
+            out_specs=cols * 2,
+        )
+
+    grad_0 = x_first(after(term_0[0], grad_p[0]), term_0[1])
+    kept_0, sent_0 = input_grads(0, grad_0[0])
+    grad_1 = then_z(after(grad_1[0], sent_0, grad_p), grad_1[1])
+    grad_2 = x_first(after(term_2[0], grad_1[0]), term_2[1])
+    kept_1, sent_1 = input_grads(1, grad_2[0])
     (outputs,) = call(
         outputs_kernel,
         [(inputs.shape, bf16)],
-        place, gated, after(gated_got, grad_1[0]), wp, inputs,
+        place, gated, after(gated_got, sent_1), wp, inputs,
         grid=(steps,),
         ins=[
             block((2, local_len, hid), 0, 0, 0),
@@ -403,10 +397,12 @@
         ],
         out_specs=[block((2, local_len, tile), 0, 0, 1)],
     )
-    grad_2 = z_first(after(term_2[0], outputs, grad_0[1], grad_1), term_2[1])
-    input_got = swap(after(input_sent, grad_0, grad_1), 2)
-    grad_2 = then_x(after(grad_2[0], outputs), *grad_2[1:])
-    grad_0 = then_z(after(grad_0[0], grad_2[0]), grad_0[1])
+    grad_0 = then_z(after(grad_0[0], outputs, grad_1), grad_0[1])
+    got_0 = swap(after(sent_0, grad_0[0]), 2)
+    grad_2 = then_z(after(grad_2[0], grad_0), grad_2[1])
+    got_1 = swap(after(sent_1, grad_2[0]), 2)
+    input_kept = jnp.concatenate([kept_0, kept_1], axis=1)
+    input_got = jnp.concatenate([got_0, got_1], axis=1)
     conv_grad = jnp.stack([total(grad_0), total(grad_1), total(grad_2)], axis=1)
     return (
         outputs,

time: 281 us -> 253 us (0.900)
  waiting for transfers between devices: 130 us -> 101 us
  other arithmetic: 9.88 us -> 16.7 us
  starting transfers between devices: 65.4 us -> 59.8 us
  Pallas kernels: 66.6 us -> 69.7 us
    ppermute x41 -> x42, waiting for transfers between devices: 99.5 us -> 67.7 us  [swap(): return lax.ppermute(value, 'seq', [(i, i ^ bits) for i in everyone])]
    ppermute x41 -> x42, starting transfers between devices: 47.9 us -> 42.7 us  [swap(): return lax.ppermute(value, 'seq', [(i, i ^ bits) for i in everyone])]
    pallas_call x22 -> x24, Pallas kernels: 66.6 us -> 69.7 us  [call(): pl.pallas_call(kernel, grid=grid, out_shape=outs, in_specs=[pl.BlockSpec(...]
  transfers between devices with their start and end apart: 49 -> 50, of which waited for: 25 -> 26; matrix products, arithmetic and copies ran while one was open for 3% -> 6% of each run, Pallas kernels for 22% -> 28%
where the time goes in v3:
time: 253 us; the launch traced here: 250 us
  waiting for transfers between devices  101 us (40%)
  Pallas kernels  69.7 us (28%)
  starting transfers between devices  59.8 us (24%)
  other arithmetic  16.7 us (7%)
    pallas_call x24, Pallas kernels, call(): pl.pallas_call(kernel, grid=grid, out_shape=outs, in_specs=[pl.BlockSpec(...  69.7 us
    ppermute x42, waiting for transfers between devices, swap(): return lax.ppermute(value, 'seq', [(i, i ^ bits) for i in everyone])  67.7 us
    ppermute x42, starting transfers between devices, swap(): return lax.ppermute(value, 'seq', [(i, i ^ bits) for i in everyone])  42.7 us
    ppermute x4, waiting for transfers between devices, over_y(): return jnp.stack([column, lax.ppermute(column, 'groups', [(0, 1), (1, 0)])])  18.8 us
    ppermute x2, waiting for transfers between devices, up(): lax.ppermute(value, 'seq', [(i, i + 4) for i in everyone if i + 4 in ever...  7.29 us
    ppermute x2, waiting for transfers between devices, down(): lax.ppermute(value, 'seq', [(i + 4, i) for i in everyone if i + 4 in ever...  6.78 us
    ppermute x2, starting transfers between devices, down(): lax.ppermute(value, 'seq', [(i + 4, i) for i in everyone if i + 4 in ever...  6.55 us
    ppermute x2, starting transfers between devices, up(): lax.ppermute(value, 'seq', [(i, i + 4) for i in everyone if i + 4 in ever...  5.31 us
  transfers between devices with their start and end apart: 50, of which 26 were waited for; matrix products, arithmetic and copies ran while one was open for 6% of the time, Pallas kernels for 28%

profile of v3, /device:TPU:16, one launch (start us, length us, event | category | flops | bytes accessed | tf_op | source)
XLA Modules:
  0.0 249.7 jit_solution(4566556502877977457)
XLA Ops:
  4.7 5.7 %collective-permute-done = bf16[4,48,768]{2,1,0:T(8,128)(2,1)S(1)} collective-permute-done((bf16[4,48,768]{2,1,0:T(8,128)(2,1)S(1)}, bf16[4,48,768]{2,1,0:T(8,128)(2,1)S(1)}, u32[]{:S(2)}, u32[]{:S(2)}) %collective-permute-start) | collective-permute-done | bytes 294944 | tf_op jit(solution)/shard_map/ppermute | solution.py:232
  12.6 3.5 %collective-permute-start.3 = (bf16[2,48,768]{2,1,0:T(8,128)(2,1)S(1)}, bf16[2,48,768]{2,1,0:T(8,128)(2,1)S(1)}, u32[]{:S(2)}, u32[]{:S(2)}) collective-permute-start(bf16[2,48,768]{2,1,0:T(8,128)(2,1)S(1)} %pad_maximum_fusion.12), channel_id=1, source_target_pairs={{0,8},{1,9},{2,10},{3,11},{4,12},{5,13},{6,14},{7,15},{8,0},{9,1},... | collective-permute-start | bytes 442376 | tf_op jit(solution)/shard_map/ppermute | solution.py:232
  16.1 8.4 %collective-permute-done.4 = bf16[2,48,768]{2,1,0:T(8,128)(2,1)S(1)} collective-permute-done((bf16[2,48,768]{2,1,0:T(8,128)(2,1)S(1)}, bf16[2,48,768]{2,1,0:T(8,128)(2,1)S(1)}, u32[]{:S(2)}, u32[]{:S(2)}) %collective-permute-start.4) | collective-permute-done | bytes 147488 | tf_op jit(solution)/shard_map/ppermute | solution.py:232
  27.3 4.3 %collective-permute-start.6 = (bf16[2,48,768]{2,1,0:T(8,128)(2,1)S(1)}, bf16[2,48,768]{2,1,0:T(8,128)(2,1)}, u32[]{:S(2)}, u32[]{:S(2)}) collective-permute-start(bf16[2,48,768]{2,1,0:T(8,128)(2,1)S(1)} %pad_maximum_fusion.11), channel_id=1, source_target_pairs={{0,8},{1,9},{2,10},{3,11},{4,12},{5,13},{6,14},{7,15},{8,0},{9,1},... | collective-permute-start | bytes 442376 | tf_op jit(solution)/shard_map/ppermute | solution.py:232
  31.6 7.5 %collective-permute-done.7 = bf16[2,48,768]{2,1,0:T(8,128)(2,1)} collective-permute-done((bf16[2,48,768]{2,1,0:T(8,128)(2,1)S(1)}, bf16[2,48,768]{2,1,0:T(8,128)(2,1)}, u32[]{:S(2)}, u32[]{:S(2)}) %collective-permute-start.7) | collective-permute-done | bytes 147488 | tf_op jit(solution)/shard_map/ppermute | solution.py:232
  45.8 4.8 %fusion.11 = (bf16[512,1536]{1,0:T(8,128)(2,1)S(1)}, bf16[512,1536]{1,0:T(8,128)(2,1)}, bf16[512,1536]{1,0:T(8,128)(2,1)S(1)}, bf16[512,1536]{1,0:T(8,128)(2,1)}) fusion(bf16[512,1536]{1,0:T(8,128)(2,1)} %collective-permute-done.1, bf16[2,512,1536]{2,1,0:T(8,128)(2,1)S(1)} %copy-done.2, s32[]{:T(128)S(6)} %select_n.79, pred[]{:T(512)S(6)} %eq.5), kind=kLoop, calls=%fused_computation.19 | loop fusion | flops 17301504 | bytes 9437189 | tf_op jit(solution)/shard_map/convert_element_type | solution.py:95
  51.1 3.5 %collective-permute-start.13 = (bf16[2,48,768]{2,1,0:T(8,128)(2,1)S(1)}, bf16[2,48,768]{2,1,0:T(8,128)(2,1)}, u32[]{:S(2)}, u32[]{:S(2)}) collective-permute-start(bf16[2,48,768]{2,1,0:T(8,128)(2,1)S(1)} %pad_maximum_fusion.13), channel_id=1, source_target_pairs={{0,8},{1,9},{2,10},{3,11},{4,12},{5,13},{6,14},{7,15},{8,0},{9,1},... | collective-permute-start | bytes 442376 | tf_op jit(solution)/shard_map/ppermute | solution.py:232
  54.6 4.3 %collective-permute-done.9 = bf16[4,2,48,768]{3,2,1,0:T(8,128)(2,1)} collective-permute-done((bf16[4,2,48,768]{3,2,1,0:T(8,128)(2,1)}, bf16[4,2,48,768]{3,2,1,0:T(8,128)(2,1)}, u32[]{:S(2)}, u32[]{:S(2)}) %collective-permute-start.9) | collective-permute-done | bytes 589856 | tf_op jit(solution)/shard_map/ppermute | solution.py:258
  68.1 3.8 %shard_map.76 = (bf16[512,768]{1,0:T(8,128)(2,1)S(1)}, f32[512,768]{1,0:T(8,128)S(1)}) custom-call(s32[4]{0:T(128)S(1)} %pad_add_fusion.place, bf16[512,1536]{1,0:T(8,128)(2,1)S(1)} %get-tuple-element.158.rows_sent.rows_kept.act_b.rows_b, bf16[512,1536]{1,0:T(8,128)(2,1)S(1)} %get-tuple-element.164.rows_kept.rows_sent.act_a.rows_a, ...), custom_call_target="tpu_custom_call" | custom-call | flops 1 | bytes 1 | tf_op jit(solution)/shard_map/pallas_call | solution.py:108
  71.9 7.3 %collective-permute-done.15 = bf16[4,2,48,768]{3,2,1,0:T(8,128)(2,1)S(1)} collective-permute-done((bf16[4,2,48,768]{3,2,1,0:T(8,128)(2,1)S(1)}, bf16[4,2,48,768]{3,2,1,0:T(8,128)(2,1)S(1)}, u32[]{:S(2)}, u32[]{:S(2)}) %collective-permute-start.15) | collective-permute-done | bytes 589856 | tf_op jit(solution)/shard_map/ppermute | solution.py:258
  80.7 4.1 %collective-permute-start.22 = (bf16[2,48,768]{2,1,0:T(8,128)(2,1)S(1)}, bf16[2,48,768]{2,1,0:T(8,128)(2,1)S(1)}, u32[]{:S(2)}, u32[]{:S(2)}) collective-permute-start(bf16[2,48,768]{2,1,0:T(8,128)(2,1)S(1)} %pad_maximum_fusion.14), channel_id=1, source_target_pairs={{0,8},{1,9},{2,10},{3,11},{4,12},{5,13},{6,14},{7,15},{8,0},{9,1},... | collective-permute-start | bytes 442376 | tf_op jit(solution)/shard_map/ppermute | solution.py:232
  85.6 3.8 %shard_map.78 = (bf16[512,768]{1,0:T(8,128)(2,1)S(1)}, f32[512,768]{1,0:T(8,128)S(1)}) custom-call(s32[4]{0:T(128)S(1)} %pad_add_fusion.place, bf16[512,1536]{1,0:T(8,128)(2,1)S(1)} %get-tuple-element.164.rows_kept.rows_sent.act_a.rows_a, bf16[512,1536]{1,0:T(8,128)(2,1)S(1)} %get-tuple-element.158.rows_sent.rows_kept.act_b.rows_b, ...), custom_call_target="tpu_custom_call" | custom-call | flops 1 | bytes 1 | tf_op jit(solution)/shard_map/pallas_call | solution.py:108
  94.3 3.9 %collective-permute-start.18 = (bf16[512,768]{1,0:T(8,128)(2,1)S(1)}, bf16[512,768]{1,0:T(8,128)(2,1)S(1)}, u32[]{:S(2)}, u32[]{:S(2)}) collective-permute-start(bf16[512,768]{1,0:T(8,128)(2,1)S(1)} %get-tuple-element.93), channel_id=1, source_target_pairs={{4,0},{5,1},{6,2},{7,3},{8,4},{9,5},{10,6},{11,7},{12,8},{13,9},{1... | collective-permute-start | bytes 2359304 | tf_op jit(solution)/shard_map/ppermute | solution.py:238
  100.6 4.0 %shard_map.80 = (f32[512,768]{1,0:T(8,128)S(1)}, f32[512,768]{1,0:T(8,128)S(1)}) custom-call(s32[4]{0:T(128)S(1)} %pad_add_fusion.place, f32[512,768]{1,0:T(8,128)S(1)} %get-tuple-element.87.near_a, f32[512,768]{1,0:T(8,128)S(1)} %get-tuple-element.88.near_b, bf16[512,1536]{1,0:T(8,128)(2,1)S(1)} %get-tuple-element.164.rows_kept.rows_sent.act_a.rows_a, ...), custom_call_target="tpu_custom_call" | custom-call | flops 1 | bytes 1 | tf_op jit(solution)/shard_map/pallas_call | solution.py:108
  104.6 7.2 %collective-permute-done.24 = bf16[4,2,48,768]{3,2,1,0:T(8,128)(2,1)S(1)} collective-permute-done((bf16[4,2,48,768]{3,2,1,0:T(8,128)(2,1)S(1)}, bf16[4,2,48,768]{3,2,1,0:T(8,128)(2,1)S(1)}, u32[]{:S(2)}, u32[]{:S(2)}) %collective-permute-start.24) | collective-permute-done | bytes 589856 | tf_op jit(solution)/shard_map/ppermute | solution.py:258
  116.6 3.6 %shard_map.81 = (f32[2,512,768]{2,1,0:T(8,128)S(1)}, bf16[2,512,768]{2,1,0:T(8,128)(2,1)S(1)}, bf16[512,768]{1,0:T(8,128)(2,1)S(1)}) custom-call(s32[4]{0:T(128)S(1)} %pad_add_fusion.place, f32[512,768]{1,0:T(8,128)S(1)} %get-tuple-element.91.near_a, f32[512,768]{1,0:T(8,128)S(1)} %get-tuple-element.92.near_b, ...), custom_call_target="tpu_custom_call" | custom-call | flops 1 | bytes 1 | tf_op jit(solution)/shard_map/pallas_call | solution.py:108
  121.4 4.6 %shard_map.83 = (f32[2,4,96,768]{3,2,1,0:T(8,128)S(1)}, bf16[2,4,96,768]{3,2,1,0:T(8,128)(2,1)S(1)}) custom-call(s32[4]{0:T(128)S(1)} %pad_add_fusion.place, bf16[512,1536]{1,0:T(8,128)(2,1)S(1)} %get-tuple-element.163.rows_a.cot_a, bf16[512,1536]{1,0:T(8,128)(2,1)S(1)} %get-tuple-element.162.rows_b.cot_b, bf16[512,768]{1,0:T(8,128)(2,1)S(1)} %get-tuple-element.169.grad_a, ...), custom_call_target="tpu_custom_call" | custom-call | flops 1 | bytes 1 | tf_op jit(solution)/shard_map/pallas_call | solution.py:108
  127.1 5.4 %shard_map.84 = (bf16[512,768]{1,0:T(8,128)(2,1)S(1)}, bf16[512,768]{1,0:T(8,128)(2,1)S(1)}) custom-call(s32[4]{0:T(128)S(1)} %pad_add_fusion.place, f32[2,512,768]{2,1,0:T(8,128)S(1)} %get-tuple-element.97.hidden, bf16[512,1536]{1,0:T(8,128)(2,1)S(1)} %get-tuple-element.163.rows_a.cot_a, bf16[512,1536]{1,0:T(8,128)(2,1)S(1)} %get-tuple-element.162.rows_b.cot_b, ...), custom_call_target="tpu_custom_call" | custom-call | flops 10000000000 | bytes 1 | tf_op jit(solution)/shard_map/pallas_call | solution.py:108
  142.4 4.6 %shard_map.86 = (f32[2,4,96,768]{3,2,1,0:T(8,128)S(1)}, bf16[2,4,96,768]{3,2,1,0:T(8,128)(2,1)S(1)}) custom-call(s32[4]{0:T(128)S(1)} %pad_add_fusion.place, bf16[512,1536]{1,0:T(8,128)(2,1)S(1)} %get-tuple-element.164.rows_kept.rows_sent.act_a.rows_a, bf16[512,1536]{1,0:T(8,128)(2,1)S(1)} %get-tuple-element.158.rows_sent.rows_kept.act_b.rows_b, ...), custom_call_target="tpu_custom_call" | custom-call | flops 1 | bytes 1 | tf_op jit(solution)/shard_map/pallas_call | solution.py:108
  147.1 7.0 %collective-permute-done.27.grad_a.hg_prev = bf16[512,768]{1,0:T(8,128)(2,1)S(1)} collective-permute-done((bf16[512,768]{1,0:T(8,128)(2,1)S(1)}, bf16[512,768]{1,0:T(8,128)(2,1)S(1)}, u32[]{:S(2)}, u32[]{:S(2)}) %collective-permute-start.27) | collective-permute-done | bytes 786464 | tf_op jit(solution)/shard_map/ppermute | solution.py:235
  157.5 4.6 %shard_map.87 = (f32[2,4,96,768]{3,2,1,0:T(8,128)S(1)}, bf16[2,4,96,768]{3,2,1,0:T(8,128)(2,1)S(1)}) custom-call(s32[4]{0:T(128)S(1)} %pad_add_fusion.place, bf16[512,1536]{1,0:T(8,128)(2,1)S(1)} %get-tuple-element.164.rows_kept.rows_sent.act_a.rows_a, bf16[512,1536]{1,0:T(8,128)(2,1)S(1)} %get-tuple-element.158.rows_sent.rows_kept.act_b.rows_b, ...), custom_call_target="tpu_custom_call" | custom-call | flops 10000000000 | bytes 1 | tf_op jit(solution)/shard_map/pallas_call | solution.py:108
  163.3 4.7 %shard_map.89 = (f32[2,4,96,768]{3,2,1,0:T(8,128)S(1)}, bf16[2,4,96,768]{3,2,1,0:T(8,128)(2,1)S(1)}) custom-call(s32[4]{0:T(128)S(1)} %pad_add_fusion.place, bf16[512,1536]{1,0:T(8,128)(2,1)S(1)} %get-tuple-element.164.rows_kept.rows_sent.act_a.rows_a, bf16[512,1536]{1,0:T(8,128)(2,1)S(1)} %get-tuple-element.158.rows_sent.rows_kept.act_b.rows_b, ...), custom_call_target="tpu_custom_call" | custom-call | flops 1 | bytes 1 | tf_op jit(solution)/shard_map/pallas_call | solution.py:108
  174.1 3.5 %collective-permute-done.32 = bf16[96,768]{1,0:T(8,128)(2,1)S(1)} collective-permute-done((bf16[96,768]{1,0:T(8,128)(2,1)S(1)}, bf16[96,768]{1,0:T(8,128)(2,1)S(1)}, u32[]{:S(2)}, u32[]{:S(2)}) %collective-permute-start.32) | collective-permute-done | bytes 147488 | tf_op jit(solution)/shard_map/ppermute | solution.py:232
  177.6 7.1 %shard_map.92 = (bf16[512,768]{1,0:T(8,128)(2,1)S(1)}, bf16[512,768]{1,0:T(8,128)(2,1)S(1)}) custom-call(s32[4]{0:T(128)S(1)} %pad_add_fusion.place, bf16[512,768]{1,0:T(8,128)(2,1)S(1)} %collective-permute-done.26.grad_b.hg_next, bf16[512,768]{1,0:T(8,128)(2,1)S(1)} %get-tuple-element.110.grad_b.grad_a.hg_b, ...), custom_call_target="tpu_custom_call" | custom-call | flops 1 | bytes 1 | tf_op jit(solution)/shard_map/pallas_call | solution.py:108
  184.7 3.5 %collective-permute-done.34 = bf16[96,768]{1,0:T(8,128)(2,1)S(1)} collective-permute-done((bf16[96,768]{1,0:T(8,128)(2,1)S(1)}, bf16[96,768]{1,0:T(8,128)(2,1)S(1)}, u32[]{:S(2)}, u32[]{:S(2)}) %collective-permute-start.34) | collective-permute-done | bytes 147488 | tf_op jit(solution)/shard_map/ppermute | solution.py:232
  195.0 7.1 %shard_map.95 = (bf16[512,768]{1,0:T(8,128)(2,1)S(1)}, bf16[512,768]{1,0:T(8,128)(2,1)S(1)}) custom-call(s32[4]{0:T(128)S(1)} %pad_add_fusion.place, bf16[512,768]{1,0:T(8,128)(2,1)S(1)} %collective-permute-done.26.grad_b.hg_next, bf16[512,768]{1,0:T(8,128)(2,1)S(1)} %get-tuple-element.110.grad_b.grad_a.hg_b, ...), custom_call_target="tpu_custom_call" | custom-call | flops 1 | bytes 1 | tf_op jit(solution)/shard_map/pallas_call | solution.py:108
  202.1 5.6 %shard_map.96 = bf16[2,512,1536]{2,1,0:T(8,128)(2,1)} custom-call(s32[4]{0:T(128)S(1)} %pad_add_fusion.place, bf16[2,512,768]{2,1,0:T(8,128)(2,1)S(1)} %get-tuple-element.95.gated, bf16[512,768]{1,0:T(8,128)(2,1)S(1)} %collective-permute-done.19.got, bf16[1536,768]{1,0:T(8,128)(2,1)S(1)} %bitcast.69, bf16[2,512,1536]{2,1,0:T(8,128)(2,1)S(1)} %copy-done.3), custom_call_target="tpu_custom_call" | custom-call | flops 1 | bytes 1 | tf_op jit(solution)/shard_map/pallas_call | solution.py:108
  215.2 4.8 %collective-permute-done.43 = bf16[96,768]{1,0:T(8,128)(2,1)S(1)} collective-permute-done((bf16[96,768]{1,0:T(8,128)(2,1)S(1)}, bf16[96,768]{1,0:T(8,128)(2,1)S(1)}, u32[]{:S(2)}, u32[]{:S(2)}) %collective-permute-start.43) | collective-permute-done | bytes 147488 | tf_op jit(solution)/shard_map/ppermute | solution.py:232
  220.0 3.8 %collective-permute-done.44 = bf16[96,768]{1,0:T(8,128)(2,1)S(1)} collective-permute-done((bf16[96,768]{1,0:T(8,128)(2,1)S(1)}, bf16[96,768]{1,0:T(8,128)(2,1)S(1)}, u32[]{:S(2)}, u32[]{:S(2)}) %collective-permute-start.44) | collective-permute-done | bytes 147488 | tf_op jit(solution)/shard_map/ppermute | solution.py:232
  231.9 4.1 %collective-permute-done.48 = bf16[96,768]{1,0:T(8,128)(2,1)S(1)} collective-permute-done((bf16[96,768]{1,0:T(8,128)(2,1)S(1)}, bf16[96,768]{1,0:T(8,128)(2,1)S(1)}, u32[]{:S(2)}, u32[]{:S(2)}) %collective-permute-start.48) | collective-permute-done | bytes 147488 | tf_op jit(solution)/shard_map/ppermute | solution.py:232
  236.0 3.7 %collective-permute-done.49 = bf16[96,768]{1,0:T(8,128)(2,1)S(1)} collective-permute-done((bf16[96,768]{1,0:T(8,128)(2,1)S(1)}, bf16[96,768]{1,0:T(8,128)(2,1)S(1)}, u32[]{:S(2)}, u32[]{:S(2)}) %collective-permute-start.49) | collective-permute-done | bytes 147488 | tf_op jit(solution)/shard_map/ppermute | solution.py:232
  240.7 6.4 %collective-permute-done.46 = bf16[512,768]{1,0:T(8,128)(2,1)S(1)} collective-permute-done((bf16[512,768]{1,0:T(8,128)(2,1)S(1)}, bf16[512,768]{1,0:T(8,128)(2,1)S(1)}, u32[]{:S(2)}, u32[]{:S(2)}) %collective-permute-start.46) | collective-permute-done | bytes 786464 | tf_op jit(solution)/shard_map/ppermute | solution.py:232
  (130 shorter events, 88.4 us)
Async XLA Ops:
  10.5 35.4 %collective-permute-start.1 = (bf16[512,1536]{1,0:T(8,128)(2,1)S(1)}, bf16[512,1536]{1,0:T(8,128)(2,1)}, u32[]{:S(2)}, u32[]{:S(2)}) collective-permute-start(bf16[512,1536]{1,0:T(8,128)(2,1)S(1)} %dynamic-slice_bitcast_fusion.1), channel_id=1, source_target_pairs={{0,2},{1,3},{2,0},{3,1},{4,6},{5,7},{6,4},{7,5},{8,10},{9,11},{10,... | collective-permute-start | bytes 4718600 | tf_op jit(solution)/shard_map/ppermute | solution.py:232
  24.5 17.2 %collective-permute-start.8 = (bf16[4,2,48,768]{3,2,1,0:T(8,128)(2,1)S(1)}, bf16[4,2,48,768]{3,2,1,0:T(8,128)(2,1)S(1)}, u32[]{:S(2)}, u32[]{:S(2)}) collective-permute-start(bf16[4,2,48,768]{3,2,1,0:T(8,128)(2,1)S(1)} %pad_maximum_fusion.7), channel_id=1, source_target_pairs={{0,16},{16,0},{1,17},{17,1},{2,18},{18,2},{3,19},{19,3},{4,20},{20... | collective-permute-start | bytes 1769480 | tf_op jit(solution)/shard_map/ppermute | solution.py:258
  26.1 13.0 %collective-permute-start.7 = (bf16[2,48,768]{2,1,0:T(8,128)(2,1)S(1)}, bf16[2,48,768]{2,1,0:T(8,128)(2,1)}, u32[]{:S(2)}, u32[]{:S(2)}) collective-permute-start(bf16[2,48,768]{2,1,0:T(8,128)(2,1)S(1)} %pad_maximum_fusion.11), channel_id=1, source_target_pairs={{0,12},{1,13},{2,14},{3,15},{4,8},{5,9},{6,10},{7,11},{8,4},{9,5},... | collective-permute-start | bytes 442376 | tf_op jit(solution)/shard_map/ppermute | solution.py:232
  42.8 23.4 %collective-permute-start.10 = (bf16[2,4,2,48,768]{4,3,2,1,0:T(8,128)(2,1)}, bf16[2,4,2,48,768]{4,3,2,1,0:T(8,128)(2,1)}, u32[]{:S(2)}, u32[]{:S(2)}) collective-permute-start(bf16[2,4,2,48,768]{4,3,2,1,0:T(8,128)(2,1)} %pad_maximum_fusion.3.kept), channel_id=1, source_target_pairs={{0,1},{1,0},{2,3},{3,2},{4,5},{5,4},{6,7},{7,6},{8,9},{9,8},{10,11... | collective-permute-start | bytes 3538952 | tf_op jit(solution)/shard_map/ppermute | solution.py:232
  42.8 16.1 %collective-permute-start.9 = (bf16[4,2,48,768]{3,2,1,0:T(8,128)(2,1)}, bf16[4,2,48,768]{3,2,1,0:T(8,128)(2,1)}, u32[]{:S(2)}, u32[]{:S(2)}) collective-permute-start(bf16[4,2,48,768]{3,2,1,0:T(8,128)(2,1)} %pad_maximum_fusion.8), channel_id=1, source_target_pairs={{0,16},{16,0},{1,17},{17,1},{2,18},{18,2},{3,19},{19,3},{4,20},{20... | collective-permute-start | bytes 1769480 | tf_op jit(solution)/shard_map/ppermute | solution.py:258
  50.6 12.8 %collective-permute-start.14 = (bf16[2,48,768]{2,1,0:T(8,128)(2,1)S(1)}, bf16[2,48,768]{2,1,0:T(8,128)(2,1)}, u32[]{:S(2)}, u32[]{:S(2)}) collective-permute-start(bf16[2,48,768]{2,1,0:T(8,128)(2,1)S(1)} %pad_maximum_fusion.13), channel_id=1, source_target_pairs={{0,12},{1,13},{2,14},{3,15},{4,8},{5,9},{6,10},{7,11},{8,4},{9,5},... | collective-permute-start | bytes 442376 | tf_op jit(solution)/shard_map/ppermute | solution.py:232
  64.6 14.6 %collective-permute-start.15 = (bf16[4,2,48,768]{3,2,1,0:T(8,128)(2,1)S(1)}, bf16[4,2,48,768]{3,2,1,0:T(8,128)(2,1)S(1)}, u32[]{:S(2)}, u32[]{:S(2)}) collective-permute-start(bf16[4,2,48,768]{3,2,1,0:T(8,128)(2,1)S(1)} %pad_maximum_fusion.9), channel_id=1, source_target_pairs={{0,16},{16,0},{1,17},{17,1},{2,18},{18,2},{3,19},{19,3},{4,20},{20... | collective-permute-start | bytes 1769480 | tf_op jit(solution)/shard_map/ppermute | solution.py:258
  71.9 12.9 %collective-permute-start.11 = (bf16[2,4,2,48,768]{4,3,2,1,0:T(8,128)(2,1)S(1)}, bf16[2,4,2,48,768]{4,3,2,1,0:T(8,128)(2,1)S(1)}, u32[]{:S(2)}, u32[]{:S(2)}) collective-permute-start(bf16[2,4,2,48,768]{4,3,2,1,0:T(8,128)(2,1)S(1)} %pad_maximum_fusion.4.kept), channel_id=1, source_target_pairs={{0,1},{1,0},{2,3},{3,2},{4,5},{5,4},{6,7},{7,6},{8,9},{9,8},{10,11... | collective-permute-start | bytes 3538952 | tf_op jit(solution)/shard_map/ppermute | solution.py:232
  79.3 20.6 %collective-permute-start.16 = (bf16[2,4,2,48,768]{4,3,2,1,0:T(8,128)(2,1)S(1)}, bf16[2,4,2,48,768]{4,3,2,1,0:T(8,128)(2,1)S(1)}, u32[]{:S(2)}, u32[]{:S(2)}) collective-permute-start(bf16[2,4,2,48,768]{4,3,2,1,0:T(8,128)(2,1)S(1)} %pad_maximum_fusion.5.kept), channel_id=1, source_target_pairs={{0,1},{1,0},{2,3},{3,2},{4,5},{5,4},{6,7},{7,6},{8,9},{9,8},{10,11... | collective-permute-start | bytes 3538952 | tf_op jit(solution)/shard_map/ppermute | solution.py:232
  79.6 36.8 %collective-permute-start.20 = (bf16[512,1536]{1,0:T(8,128)(2,1)S(1)}, bf16[512,1536]{1,0:T(8,128)(2,1)S(1)}, u32[]{:S(2)}, u32[]{:S(2)}) collective-permute-start(bf16[512,1536]{1,0:T(8,128)(2,1)S(1)} %dynamic-slice_bitcast_fusion), channel_id=1, source_target_pairs={{0,2},{1,3},{2,0},{3,1},{4,6},{5,7},{6,4},{7,5},{8,10},{9,11},{10,... | collective-permute-start | bytes 4718600 | tf_op jit(solution)/shard_map/ppermute | solution.py:232
  80.7 13.6 %collective-permute-start.22 = (bf16[2,48,768]{2,1,0:T(8,128)(2,1)S(1)}, bf16[2,48,768]{2,1,0:T(8,128)(2,1)S(1)}, u32[]{:S(2)}, u32[]{:S(2)}) collective-permute-start(bf16[2,48,768]{2,1,0:T(8,128)(2,1)S(1)} %pad_maximum_fusion.14), channel_id=1, source_target_pairs={{0,8},{1,9},{2,10},{3,11},{4,12},{5,13},{6,14},{7,15},{8,0},{9,1},... | collective-permute-start | bytes 442376 | tf_op jit(solution)/shard_map/ppermute | solution.py:232
  85.5 12.8 %collective-permute-start.21 = (bf16[2,48,768]{2,1,0:T(8,128)(2,1)S(1)}, bf16[2,48,768]{2,1,0:T(8,128)(2,1)S(1)}, u32[]{:S(2)}, u32[]{:S(2)}) collective-permute-start(bf16[2,48,768]{2,1,0:T(8,128)(2,1)S(1)} %pad_maximum_fusion.14), channel_id=1, source_target_pairs={{0,4},{1,5},{2,6},{3,7},{4,0},{5,1},{6,2},{7,3},{8,12},{9,13},{10,... | collective-permute-start | bytes 442376 | tf_op jit(solution)/shard_map/ppermute | solution.py:232
  92.4 19.9 %collective-permute-start.17 = (bf16[512,768]{1,0:T(8,128)(2,1)S(1)}, bf16[512,768]{1,0:T(8,128)(2,1)S(1)}, u32[]{:S(2)}, u32[]{:S(2)}) collective-permute-start(bf16[512,768]{1,0:T(8,128)(2,1)S(1)} %get-tuple-element.84), channel_id=1, source_target_pairs={{0,4},{1,5},{2,6},{3,7},{4,8},{5,9},{6,10},{7,11},{8,12},{9,13},{1... | collective-permute-start | bytes 2359304 | tf_op jit(solution)/shard_map/ppermute | solution.py:235
  94.3 21.4 %collective-permute-start.18 = (bf16[512,768]{1,0:T(8,128)(2,1)S(1)}, bf16[512,768]{1,0:T(8,128)(2,1)S(1)}, u32[]{:S(2)}, u32[]{:S(2)}) collective-permute-start(bf16[512,768]{1,0:T(8,128)(2,1)S(1)} %get-tuple-element.93), channel_id=1, source_target_pairs={{4,0},{5,1},{6,2},{7,3},{8,4},{9,5},{10,6},{11,7},{12,8},{13,9},{1... | collective-permute-start | bytes 2359304 | tf_op jit(solution)/shard_map/ppermute | solution.py:238
  98.3 13.5 %collective-permute-start.24 = (bf16[4,2,48,768]{3,2,1,0:T(8,128)(2,1)S(1)}, bf16[4,2,48,768]{3,2,1,0:T(8,128)(2,1)S(1)}, u32[]{:S(2)}, u32[]{:S(2)}) collective-permute-start(bf16[4,2,48,768]{3,2,1,0:T(8,128)(2,1)S(1)} %pad_maximum_fusion.10), channel_id=1, source_target_pairs={{0,16},{16,0},{1,17},{17,1},{2,18},{18,2},{3,19},{19,3},{4,20},{20... | collective-permute-start | bytes 1769480 | tf_op jit(solution)/shard_map/ppermute | solution.py:258
  120.3 19.4 %collective-permute-start.19 = (bf16[512,768]{1,0:T(8,128)(2,1)S(1)}, bf16[512,768]{1,0:T(8,128)(2,1)S(1)}, u32[]{:S(2)}, u32[]{:S(2)}) collective-permute-start(bf16[512,768]{1,0:T(8,128)(2,1)S(1)} %get-tuple-element.96), channel_id=1, source_target_pairs={{0,2},{1,3},{2,0},{3,1},{4,6},{5,7},{6,4},{7,5},{8,10},{9,11},{10,... | collective-permute-start | bytes 2359304 | tf_op jit(solution)/shard_map/ppermute | solution.py:232
  126.1 13.5 %collective-permute-start.28 = (bf16[2,4,96,768]{3,2,1,0:T(8,128)(2,1)S(1)}, bf16[2,4,96,768]{3,2,1,0:T(8,128)(2,1)S(1)}, u32[]{:S(2)}, u32[]{:S(2)}) collective-permute-start(bf16[2,4,96,768]{3,2,1,0:T(8,128)(2,1)S(1)} %get-tuple-element.108), channel_id=1, source_target_pairs={{0,1},{1,0},{2,3},{3,2},{4,5},{5,4},{6,7},{7,6},{8,9},{9,8},{10,11... | collective-permute-start | bytes 3538952 | tf_op jit(solution)/shard_map/ppermute | solution.py:232
  132.5 21.6 %collective-permute-start.27 = (bf16[512,768]{1,0:T(8,128)(2,1)S(1)}, bf16[512,768]{1,0:T(8,128)(2,1)S(1)}, u32[]{:S(2)}, u32[]{:S(2)}) collective-permute-start(bf16[512,768]{1,0:T(8,128)(2,1)S(1)} %get-tuple-element.110.grad_b.grad_a.hg_b), channel_id=1, source_target_pairs={{0,4},{1,5},{2,6},{3,7},{4,8},{5,9},{6,10},{7,11},{8,12},{9,13},{1... | collective-permute-start | bytes 2359304 | tf_op jit(solution)/shard_map/ppermute | solution.py:235
  135.9 21.5 %collective-permute-start.26 = (bf16[512,768]{1,0:T(8,128)(2,1)S(1)}, bf16[512,768]{1,0:T(8,128)(2,1)S(1)}, u32[]{:S(2)}, u32[]{:S(2)}) collective-permute-start(bf16[512,768]{1,0:T(8,128)(2,1)S(1)} %get-tuple-element.118.grad_a.grad_b.hg_a), channel_id=1, source_target_pairs={{4,0},{5,1},{6,2},{7,3},{8,4},{9,5},{10,6},{11,7},{12,8},{13,9},{1... | collective-permute-start | bytes 2359304 | tf_op jit(solution)/shard_map/ppermute | solution.py:238
  140.7 21.5 %collective-permute-start.29 = (bf16[4,96,768]{2,1,0:T(8,128)(2,1)S(1)}, bf16[4,96,768]{2,1,0:T(8,128)(2,1)S(1)}, u32[]{:S(2)}, u32[]{:S(2)}) collective-permute-start(bf16[4,96,768]{2,1,0:T(8,128)(2,1)S(1)} %get-tuple-element.114), channel_id=1, source_target_pairs={{0,2},{1,3},{2,0},{3,1},{4,6},{5,7},{6,4},{7,5},{8,10},{9,11},{10,... | collective-permute-start | bytes 1769480 | tf_op jit(solution)/shard_map/ppermute | solution.py:232
  147.1 15.1 %collective-permute-start.30 = (bf16[2,4,96,768]{3,2,1,0:T(8,128)(2,1)S(1)}, bf16[2,4,96,768]{3,2,1,0:T(8,128)(2,1)S(1)}, u32[]{:S(2)}, u32[]{:S(2)}) collective-permute-start(bf16[2,4,96,768]{3,2,1,0:T(8,128)(2,1)S(1)} %get-tuple-element.116), channel_id=1, source_target_pairs={{0,1},{1,0},{2,3},{3,2},{4,5},{5,4},{6,7},{7,6},{8,9},{9,8},{10,11... | collective-permute-start | bytes 3538952 | tf_op jit(solution)/shard_map/ppermute | solution.py:232
  167.9 20.9 %collective-permute-start.36 = (bf16[2,4,96,768]{3,2,1,0:T(8,128)(2,1)S(1)}, bf16[2,4,96,768]{3,2,1,0:T(8,128)(2,1)S(1)}, u32[]{:S(2)}, u32[]{:S(2)}) collective-permute-start(bf16[2,4,96,768]{3,2,1,0:T(8,128)(2,1)S(1)} %get-tuple-element.134), channel_id=1, source_target_pairs={{0,1},{1,0},{2,3},{3,2},{4,5},{5,4},{6,7},{7,6},{8,9},{9,8},{10,11... | collective-permute-start | bytes 3538952 | tf_op jit(solution)/shard_map/ppermute | solution.py:232
  168.5 19.7 %collective-permute-start.35 = (bf16[4,96,768]{2,1,0:T(8,128)(2,1)S(1)}, bf16[4,96,768]{2,1,0:T(8,128)(2,1)S(1)}, u32[]{:S(2)}, u32[]{:S(2)}) collective-permute-start(bf16[4,96,768]{2,1,0:T(8,128)(2,1)S(1)} %get-tuple-element.131), channel_id=1, source_target_pairs={{0,2},{1,3},{2,0},{3,1},{4,6},{5,7},{6,4},{7,5},{8,10},{9,11},{10,... | collective-permute-start | bytes 1769480 | tf_op jit(solution)/shard_map/ppermute | solution.py:232
  172.0 35.7 %collective-permute-start.40 = (bf16[4,96,768]{2,1,0:T(8,128)(2,1)S(1)}, bf16[4,96,768]{2,1,0:T(8,128)(2,1)S(1)}, u32[]{:S(2)}, u32[]{:S(2)}) collective-permute-start(bf16[4,96,768]{2,1,0:T(8,128)(2,1)S(1)} %get-tuple-element.145), channel_id=1, source_target_pairs={{0,2},{1,3},{2,0},{3,1},{4,6},{5,7},{6,4},{7,5},{8,10},{9,11},{10,... | collective-permute-start | bytes 1769480 | tf_op jit(solution)/shard_map/ppermute | solution.py:232
  189.9 33.9 %collective-permute-start.45 = (bf16[4,96,768]{2,1,0:T(8,128)(2,1)S(1)}, bf16[4,96,768]{2,1,0:T(8,128)(2,1)S(1)}, u32[]{:S(2)}, u32[]{:S(2)}) collective-permute-start(bf16[4,96,768]{2,1,0:T(8,128)(2,1)S(1)} %get-tuple-element.152), channel_id=1, source_target_pairs={{0,2},{1,3},{2,0},{3,1},{4,6},{5,7},{6,4},{7,5},{8,10},{9,11},{10,... | collective-permute-start | bytes 1769480 | tf_op jit(solution)/shard_map/ppermute | solution.py:232
  191.5 16.2 %collective-permute-start.37 = (bf16[96,768]{1,0:T(8,128)(2,1)S(1)}, bf16[96,768]{1,0:T(8,128)(2,1)S(1)}, u32[]{:S(2)}, u32[]{:S(2)}) collective-permute-start(bf16[96,768]{1,0:T(8,128)(2,1)S(1)} %get-tuple-element.141), channel_id=1, source_target_pairs={{0,4},{1,5},{2,6},{3,7},{4,0},{5,1},{6,2},{7,3},{8,12},{9,13},{10,... | collective-permute-start | bytes 442376 | tf_op jit(solution)/shard_map/ppermute | solution.py:232
  191.5 16.2 %collective-permute-start.38 = (bf16[96,768]{1,0:T(8,128)(2,1)S(1)}, bf16[96,768]{1,0:T(8,128)(2,1)S(1)}, u32[]{:S(2)}, u32[]{:S(2)}) collective-permute-start(bf16[96,768]{1,0:T(8,128)(2,1)S(1)} %get-tuple-element.142), channel_id=1, source_target_pairs={{0,8},{1,9},{2,10},{3,11},{4,12},{5,13},{6,14},{7,15},{8,0},{9,1},... | collective-permute-start | bytes 442376 | tf_op jit(solution)/shard_map/ppermute | solution.py:232
  193.5 14.2 %collective-permute-start.39 = (bf16[96,768]{1,0:T(8,128)(2,1)S(1)}, bf16[96,768]{1,0:T(8,128)(2,1)S(1)}, u32[]{:S(2)}, u32[]{:S(2)}) collective-permute-start(bf16[96,768]{1,0:T(8,128)(2,1)S(1)} %get-tuple-element.143), channel_id=1, source_target_pairs={{0,12},{1,13},{2,14},{3,15},{4,8},{5,9},{6,10},{7,11},{8,4},{9,5},... | collective-permute-start | bytes 442376 | tf_op jit(solution)/shard_map/ppermute | solution.py:232
  210.4 13.4 %collective-permute-start.44 = (bf16[96,768]{1,0:T(8,128)(2,1)S(1)}, bf16[96,768]{1,0:T(8,128)(2,1)S(1)}, u32[]{:S(2)}, u32[]{:S(2)}) collective-permute-start(bf16[96,768]{1,0:T(8,128)(2,1)S(1)} %get-tuple-element.150), channel_id=1, source_target_pairs={{0,12},{1,13},{2,14},{3,15},{4,8},{5,9},{6,10},{7,11},{8,4},{9,5},... | collective-permute-start | bytes 442376 | tf_op jit(solution)/shard_map/ppermute | solution.py:232
  212.7 28.0 %collective-permute-start.41 = (bf16[512,768]{1,0:T(8,128)(2,1)S(1)}, bf16[512,768]{1,0:T(8,128)(2,1)S(1)}, u32[]{:S(2)}, u32[]{:S(2)}) collective-permute-start(bf16[512,768]{1,0:T(8,128)(2,1)S(1)} %get-tuple-element.147), channel_id=1, source_target_pairs={{0,2},{1,3},{2,0},{3,1},{4,6},{5,7},{6,4},{7,5},{8,10},{9,11},{10,... | collective-permute-start | bytes 2359304 | tf_op jit(solution)/shard_map/ppermute | solution.py:232
  224.5 22.7 %collective-permute-start.46 = (bf16[512,768]{1,0:T(8,128)(2,1)S(1)}, bf16[512,768]{1,0:T(8,128)(2,1)S(1)}, u32[]{:S(2)}, u32[]{:S(2)}) collective-permute-start(bf16[512,768]{1,0:T(8,128)(2,1)S(1)} %get-tuple-element.154), channel_id=1, source_target_pairs={{0,2},{1,3},{2,0},{3,1},{4,6},{5,7},{6,4},{7,5},{8,10},{9,11},{10,... | collective-permute-start | bytes 2359304 | tf_op jit(solution)/shard_map/ppermute | solution.py:232
  226.8 12.9 %collective-permute-start.49 = (bf16[96,768]{1,0:T(8,128)(2,1)S(1)}, bf16[96,768]{1,0:T(8,128)(2,1)S(1)}, u32[]{:S(2)}, u32[]{:S(2)}) collective-permute-start(bf16[96,768]{1,0:T(8,128)(2,1)S(1)} %get-tuple-element.157), channel_id=1, source_target_pairs={{0,12},{1,13},{2,14},{3,15},{4,8},{5,9},{6,10},{7,11},{8,4},{9,5},... | collective-permute-start | bytes 442376 | tf_op jit(solution)/shard_map/ppermute | solution.py:232
  (23 other events, 218.2 us)

commit v4 on v3

--- a/solution.py
+++ b/solution.py
@@ -121,6 +121,9 @@
     return pl.BlockSpec(shape, lambda i: tuple(i if d else 0 for d in index))
 
 
+RESIDENT = pl.BlockSpec(memory_space=pltpu.VMEM)
+
+
 def place_kernel(place, kept, got, out):
     z, x, core, y = place[0], place[1], place[2], place[3]
     for dy in range(kept.shape[0]):
@@ -165,6 +168,21 @@
 def term_kernel(place, rows_a, rows_b, grad_a, grad_b, mine, theirs, product):
     core = place[2]
     sums = t_dot(rows_a[...], grad_a[...]) + t_dot(rows_b[...], grad_b[...])
+    product[...] = sums.reshape(product.shape)
+    mine[:, 0] = product[:, core]
+    theirs[:, 0] = product[:, 1 - core].astype(theirs.dtype)
+
+
+def turn_kernel(place, rows_a, rows_b, out):
+    half = rows_a.shape[0]
+    out[:, :half] = rows_a[...].T
+    out[:, half:] = rows_b[...].T
+
+
+def turned_term_kernel(place, turned, grad_a, grad_b, mine, theirs, product):
+    core = place[2]
+    half = grad_a.shape[0]
+    sums = dot(turned[:, :half], grad_a[...]) + dot(turned[:, half:], grad_b[...])
     product[...] = sums.reshape(product.shape)
     mine[:, 0] = product[:, core]
     theirs[:, 0] = product[:, 1 - core].astype(theirs.dtype)
@@ -249,12 +267,13 @@
     shard_x = swap(shard, 2)
     in_got = swap(after(pick(inputs, 1 - x), shard_x), 2)
 
-    def along_z(k, *earlier):
-        piece = after(jnp.stack([shard[k], shard_x[k]]), *earlier)
+    def along_z(piece):
         return jnp.stack([piece] + [swap(piece, 4 * d) for d in range(1, depth)])
 
-    def over_y(column, *earlier):
-        column = after(column, *earlier)
+    def column(k):
+        return jnp.stack([shard[k], shard_x[k]])
+
+    def over_y(column):
         return jnp.stack([column, lax.ppermute(column, "groups", [(0, 1), (1, 0)])])
 
     def tap_sums(rows_sent, rows_kept, tap):
@@ -263,29 +282,29 @@
             [((local_len, hid), bf16), ((local_len, hid), f32)],
             place, rows_sent, rows_kept, tap,
             grid=(hid // tile,),
-            ins=[block((local_len, chans), 0, 0)] * 2 + [block((chans, tile), 0, 1)],
+            ins=[RESIDENT] * 2 + [block((chans, tile), 0, 1)],
             out_specs=[block((local_len, tile), 0, 1)] * 2,
         )
 
-    column_0 = along_z(0)
-    column_2 = along_z(2, column_0)
+    column_0 = along_z(column(0))
+    column_2 = along_z(after(column(2), column_0))
     half_0 = over_y(column_0)
     in_a, in_b = ordered(pick(inputs, x), in_got)
     act_a, act_b = act(in_a), act(in_b)
-    column_1 = along_z(1, column_2, half_0, act_a, act_b)
-    half_2 = over_y(column_2, half_0)
+    column_1 = along_z(after(column(1), column_2, half_0, (act_a, act_b)))
+    half_2 = over_y(after(column_2, half_0))
     w0 = placed(place, half_0, swap(half_0, 1))
+    cot_got = swap(after(pick(cotangent, 1 - x), in_got, column_1), 2)
     to_next, near_b = tap_sums(act_b, act_a, w0)
     from_prev = up(to_next)
-    cot_got = swap(after(pick(cotangent, 1 - x), in_got, column_1), 2)
-    half_1 = over_y(column_1, half_2)
-    piece_p = after(jnp.stack([shard[3], shard_x[3]]), column_1, half_2, to_next)
-    column_p = [swap(piece_p, 12), swap(piece_p, 8)]
     w2 = placed(place, half_2, swap(after(half_2, to_next), 1))
-    column_p = jnp.stack([piece_p, swap(after(piece_p, w2), 4)] + column_p[::-1])
+    half_1 = over_y(after(column_1, half_2))
     to_prev, near_a = tap_sums(act_a, act_b, after(w2, to_next))
     from_next = down(to_prev)
-    half_p = over_y(column_p, half_1, to_prev)
+    piece_p = after(column(3), column_1, half_2, to_next)
+    column_p = [swap(piece_p, 12), swap(piece_p, 8)]
+    column_p = jnp.stack([piece_p, swap(after(piece_p, w2), 4)] + column_p[::-1])
+    half_p = over_y(after(column_p, half_1, to_prev))
     w1 = placed(place, half_1, swap(half_1, 1))
     near_a, near_b = call(
         own_tap_kernel,
@@ -293,9 +312,10 @@
         place, near_a, near_b, act_a, act_b, w1,
         grid=(hid // tile,),
         ins=[block((local_len, tile), 0, 1)] * 2
-        + [block((local_len, chans), 0, 0)] * 2
+        + [RESIDENT] * 2
         + [block((chans, tile), 0, 1)],
         out_specs=[block((local_len, tile), 0, 1)] * 2,
+        work=1,
     )
     hidden, gated, gated_sent = call(
         gated_kernel,
@@ -306,15 +326,28 @@
         out_specs=[block((2, local_len, tile), 0, 0, 1)] * 2 + [block((local_len, tile), 0, 1)],
     )
     gated_got = swap(gated_sent, 2)
-    def term(rows_a, rows_b, grad_a, grad_b, work=1):
+
+    def turned(rows_a, rows_b):
+        cols = 4 * share
+        return call(
+            turn_kernel,
+            [((chans, 2 * local_len), bf16)],
+            place, rows_a, rows_b,
+            grid=(depth,),
+            ins=[block((local_len, cols), 0, 1)] * 2,
+            out_specs=[block((cols, 2 * local_len), 1, 0)],
+        )[0]
+
+    def term(lhs, grad_a, grad_b, work=1):
         cols = 4 * share
         part = (2, depth, share, hid)
+        one = len(lhs) == 1
         mine, theirs = call(
-            term_kernel,
+            turned_term_kernel if one else term_kernel,
             [(part, f32), (part, bf16)],
-            place, rows_a, rows_b, grad_a, grad_b,
+            place, *lhs, grad_a, grad_b,
             grid=(depth,),
-            ins=[block((local_len, cols), 0, 1)] * 2 + [block((local_len, hid), 0, 0)] * 2,
+            ins=([block((cols, 2 * local_len), 1, 0)] if one else [block((local_len, cols), 0, 1)] * 2) + [RESIDENT] * 2,
             out_specs=[block((2, 1, share, hid), 0, 1, 0, 0)] * 2,
             scratch=[pltpu.VMEM((2, 2, share, hid), f32)],
             work=work,
@@ -344,28 +377,22 @@
         return sum(part.astype(f32) for part in parts)
 
     cot_a, cot_b = ordered(pick(cotangent, x), cot_got)
-    term_p = term(cot_a, cot_b, gated[0], gated[1])
-    wp = placed(place, half_p, swap(after(half_p, from_prev, from_next, near_a, near_b), 1))
+    wp = placed(place, half_p, swap(after(half_p, from_prev, from_next, (near_a, near_b)), 1))
+    term_p = term((cot_a, cot_b), gated[0], gated[1], 1)
     hg_a, hg_b = call(
         hidden_grad_kernel,
         [((local_len, hid), bf16)] * 2,
         place, hidden, cot_a, cot_b, after(wp, term_p[0]),
         grid=(hid // tile,),
         ins=[block((2, local_len, tile), 0, 0, 1)]
-        + [block((local_len, chans), 0, 0)] * 2
+        + [RESIDENT] * 2
         + [block((chans, tile), 0, 1)],
         out_specs=[block((local_len, tile), 0, 1)] * 2,
         work=LONG,
     )
     hg_prev, hg_next = up(hg_b), down(hg_a)
-    grad_p = x_first(after(term_p[0], hg_a, gated_got), term_p[1])
-    term_1 = term(act_a, act_b, hg_a, after(hg_b, grad_p[0]))
-    term_0 = term(act_a, act_b, hg_b, after(hg_next, term_1[0], hg_prev), LONG)
-    grad_1 = x_first(after(term_1[0], term_0[0], grad_p[1]), term_1[1])
-    term_2 = term(act_a, act_b, hg_prev, after(hg_a, grad_1[0]))
-    grad_p = then_z(after(grad_p[0], term_2[0]), grad_p[1])
-
-    def input_grads(part, *earlier):
+
+    def input_grads(part, earlier):
         cols = [block((local_len, tile), 0, 1)]
         first = part * steps // 2
         late = pl.BlockSpec((local_len, tile), lambda i: (0, i + first))
@@ -373,40 +400,52 @@
         return call(
             input_grad_kernel,
             [((local_len, chans // 2), bf16)] * 2,
-            place, hg_next, hg_b, hg_a, after(hg_prev, *earlier), w0, w1, w2, in_a, in_b, cot_a, cot_b,
+            place, hg_next, hg_b, hg_a, after(hg_prev, earlier), w0, w1, w2, in_a, in_b, cot_a, cot_b,
             grid=(steps // 2,),
-            ins=[block((local_len, hid), 0, 0)] * 4 + [taps] * 3 + [late] * 4,
+            ins=[RESIDENT] * 4 + [taps] * 3 + [late] * 4,
             out_specs=cols * 2,
         )
 
+    grad_p = x_first(after(term_p[0], hg_a, gated_got), term_p[1])
+    acted = (turned(act_a, after(act_b, grad_p[0])),)
+    term_1 = term(acted, hg_a, after(hg_b, grad_p[0]), 1)
+
+    def finished(got):
+        return call(
+            outputs_kernel,
+            [(inputs.shape, bf16)],
+            place, gated, got, wp, inputs,
+            grid=(steps,),
+            ins=[
+                block((2, local_len, hid), 0, 0, 0),
+                block((local_len, hid), 0, 0),
+                block((tile, hid), 1, 0),
+                block((2, local_len, tile), 0, 0, 1),
+            ],
+            out_specs=[block((2, local_len, tile), 0, 0, 1)],
+        )[0]
+
+    term_0 = term(acted, hg_b, after(hg_next, term_1[0], hg_prev), LONG)
+    grad_1 = x_first(after(term_1[0], term_0[0], grad_p[1]), term_1[1])
+    term_2 = term(acted, hg_prev, after(hg_a, grad_1[0]), 1)
+    grad_p = then_z(after(grad_p[0], term_2[0]), grad_p[1])
     grad_0 = x_first(after(term_0[0], grad_p[0]), term_0[1])
     kept_0, sent_0 = input_grads(0, grad_0[0])
     grad_1 = then_z(after(grad_1[0], sent_0, grad_p), grad_1[1])
     grad_2 = x_first(after(term_2[0], grad_1[0]), term_2[1])
     kept_1, sent_1 = input_grads(1, grad_2[0])
-    (outputs,) = call(
-        outputs_kernel,
-        [(inputs.shape, bf16)],
-        place, gated, after(gated_got, sent_1), wp, inputs,
-        grid=(steps,),
-        ins=[
-            block((2, local_len, hid), 0, 0, 0),
-            block((local_len, hid), 0, 0),
-            block((tile, hid), 1, 0),
-            block((2, local_len, tile), 0, 0, 1),
-        ],
-        out_specs=[block((2, local_len, tile), 0, 0, 1)],
-    )
-    grad_0 = then_z(after(grad_0[0], outputs, grad_1), grad_0[1])
-    got_0 = swap(after(sent_0, grad_0[0]), 2)
-    grad_2 = then_z(after(grad_2[0], grad_0), grad_2[1])
+    got_0 = swap(sent_0, 2)
+    grad_0 = then_z(after(grad_0[0], sent_1, grad_1), grad_0[1])
+    outputs = finished(after(gated_got, got_0))
+    grad_2 = then_z(after(grad_2[0], grad_0[0], grad_0, outputs), grad_2[1])
     got_1 = swap(after(sent_1, grad_2[0]), 2)
     input_kept = jnp.concatenate([kept_0, kept_1], axis=1)
     input_got = jnp.concatenate([got_0, got_1], axis=1)
+    input_grad = jnp.stack(ordered(input_kept, input_got))
     conv_grad = jnp.stack([total(grad_0), total(grad_1), total(grad_2)], axis=1)
     return (
         outputs,
-        jnp.stack(ordered(input_kept, input_got)),
+        input_grad,
         conv_grad * scale,
         total(grad_p) * scale,
     )

time: 253 us -> 251 us (level)
  waiting for transfers between devices: 101 us -> 89.6 us
  starting transfers between devices: 59.8 us -> 67.8 us
    ppermute x42, waiting for transfers between devices: 67.7 us -> 56.3 us  [swap(): return lax.ppermute(value, 'seq', [(i, i ^ bits) for i in everyone])]
    ppermute x42, starting transfers between devices: 42.7 us -> 47.8 us  [swap(): return lax.ppermute(value, 'seq', [(i, i ^ bits) for i in everyone])]
    ppermute x4, starting transfers between devices: 5.26 us -> 7.85 us  [over_y(): return jnp.stack([column, lax.ppermute(column, 'groups', [(0, 1), (1, 0)])])]
    pallas_call x24 -> x25, Pallas kernels: 69.7 us -> 70.4 us  [call(): pl.pallas_call(kernel, grid=grid, out_shape=outs, in_specs=[pl.BlockSpec(...]
  transfers between devices with their start and end apart: 50 -> 50, of which waited for: 26 -> 30; matrix products, arithmetic and copies ran while one was open for 6% -> 6% of each run, Pallas kernels for 28% -> 28%
where the time goes in v4:
time: 251 us; the launch traced here: 249 us
  waiting for transfers between devices  89.6 us (36%)
  Pallas kernels  70.4 us (28%)
  starting transfers between devices  67.8 us (27%)
  other arithmetic  17.8 us (7%)
    pallas_call x25, Pallas kernels, call(): pl.pallas_call(kernel, grid=grid, out_shape=outs, in_specs=[pl.BlockSpec(...  70.4 us
    ppermute x42, waiting for transfers between devices, swap(): return lax.ppermute(value, 'seq', [(i, i ^ bits) for i in everyone])  56.3 us
    ppermute x42, starting transfers between devices, swap(): return lax.ppermute(value, 'seq', [(i, i ^ bits) for i in everyone])  47.8 us
    ppermute x4, waiting for transfers between devices, over_y(): return jnp.stack([column, lax.ppermute(column, 'groups', [(0, 1), (1, 0)])])  20.6 us
    ppermute x4, starting transfers between devices, over_y(): return jnp.stack([column, lax.ppermute(column, 'groups', [(0, 1), (1, 0)])])  7.85 us
    ppermute x2, waiting for transfers between devices, down(): lax.ppermute(value, 'seq', [(i + 4, i) for i in everyone if i + 4 in ever...  7.22 us
    ppermute x2, starting transfers between devices, up(): lax.ppermute(value, 'seq', [(i, i + 4) for i in everyone if i + 4 in ever...  6.31 us
    ppermute x2, starting transfers between devices, down(): lax.ppermute(value, 'seq', [(i + 4, i) for i in everyone if i + 4 in ever...  5.91 us
  transfers between devices with their start and end apart: 50, of which 30 were waited for; matrix products, arithmetic and copies ran while one was open for 6% of the time, Pallas kernels for 28%

profile of v4, /device:TPU:16, one launch (start us, length us, event | category | flops | bytes accessed | tf_op | source)
XLA Modules:
  0.0 249.0 jit_solution(7155750360682023937)
XLA Ops:
  4.7 5.7 %collective-permute-done = bf16[4,48,768]{2,1,0:T(8,128)(2,1)S(1)} collective-permute-done((bf16[4,48,768]{2,1,0:T(8,128)(2,1)S(1)}, bf16[4,48,768]{2,1,0:T(8,128)(2,1)S(1)}, u32[]{:S(2)}, u32[]{:S(2)}) %collective-permute-start) | collective-permute-done | bytes 294944 | tf_op jit(solution)/shard_map/ppermute | solution.py:250
  15.6 4.9 %collective-permute-done.3 = bf16[2,48,768]{2,1,0:T(8,128)(2,1)S(1)} collective-permute-done((bf16[2,48,768]{2,1,0:T(8,128)(2,1)S(1)}, bf16[2,48,768]{2,1,0:T(8,128)(2,1)S(1)}, u32[]{:S(2)}, u32[]{:S(2)}) %collective-permute-start.3) | collective-permute-done | bytes 147488 | tf_op jit(solution)/shard_map/ppermute | solution.py:250
  21.3 5.7 %collective-permute-done.4 = bf16[2,48,768]{2,1,0:T(8,128)(2,1)S(1)} collective-permute-done((bf16[2,48,768]{2,1,0:T(8,128)(2,1)S(1)}, bf16[2,48,768]{2,1,0:T(8,128)(2,1)S(1)}, u32[]{:S(2)}, u32[]{:S(2)}) %collective-permute-start.4) | collective-permute-done | bytes 147488 | tf_op jit(solution)/shard_map/ppermute | solution.py:250
  30.4 3.4 %collective-permute-start.5 = (bf16[2,48,768]{2,1,0:T(8,128)(2,1)S(1)}, bf16[2,48,768]{2,1,0:T(8,128)(2,1)}, u32[]{:S(2)}, u32[]{:S(2)}) collective-permute-start(bf16[2,48,768]{2,1,0:T(8,128)(2,1)S(1)} %pad_maximum_fusion.11), channel_id=1, source_target_pairs={{0,4},{1,5},{2,6},{3,7},{4,0},{5,1},{6,2},{7,3},{8,12},{9,13},{10,... | collective-permute-start | bytes 442376 | tf_op jit(solution)/shard_map/ppermute | solution.py:250
  33.8 5.7 %collective-permute-done.7 = bf16[2,48,768]{2,1,0:T(8,128)(2,1)} collective-permute-done((bf16[2,48,768]{2,1,0:T(8,128)(2,1)S(1)}, bf16[2,48,768]{2,1,0:T(8,128)(2,1)}, u32[]{:S(2)}, u32[]{:S(2)}) %collective-permute-start.7) | collective-permute-done | bytes 147488 | tf_op jit(solution)/shard_map/ppermute | solution.py:250
  45.8 4.8 %fusion.11 = (bf16[512,1536]{1,0:T(8,128)(2,1)S(1)}, bf16[512,1536]{1,0:T(8,128)(2,1)}, bf16[512,1536]{1,0:T(8,128)(2,1)S(1)}, bf16[512,1536]{1,0:T(8,128)(2,1)}) fusion(bf16[512,1536]{1,0:T(8,128)(2,1)} %collective-permute-done.1, bf16[2,512,1536]{2,1,0:T(8,128)(2,1)S(1)} %copy-done.2, s32[]{:T(128)S(6)} %select_n.79, pred[]{:T(512)S(6)} %eq.5), kind=kLoop, calls=%fused_computation.19 | loop fusion | flops 17301504 | bytes 9437189 | tf_op jit(solution)/shard_map/convert_element_type | solution.py:95
  51.1 3.9 %collective-permute-start.13 = (bf16[2,48,768]{2,1,0:T(8,128)(2,1)S(1)}, bf16[2,48,768]{2,1,0:T(8,128)(2,1)}, u32[]{:S(2)}, u32[]{:S(2)}) collective-permute-start(bf16[2,48,768]{2,1,0:T(8,128)(2,1)S(1)} %pad_maximum_fusion.13), channel_id=1, source_target_pairs={{0,8},{1,9},{2,10},{3,11},{4,12},{5,13},{6,14},{7,15},{8,0},{9,1},... | collective-permute-start | bytes 442376 | tf_op jit(solution)/shard_map/ppermute | solution.py:250
  54.9 5.1 %collective-permute-done.9 = bf16[4,2,48,768]{3,2,1,0:T(8,128)(2,1)} collective-permute-done((bf16[4,2,48,768]{3,2,1,0:T(8,128)(2,1)}, bf16[4,2,48,768]{3,2,1,0:T(8,128)(2,1)}, u32[]{:S(2)}, u32[]{:S(2)}) %collective-permute-start.9) | collective-permute-done | bytes 589856 | tf_op jit(solution)/shard_map/ppermute | solution.py:277
  68.9 3.8 %shard_map.76 = (bf16[512,768]{1,0:T(8,128)(2,1)S(1)}, f32[512,768]{1,0:T(8,128)S(1)}) custom-call(s32[4]{0:T(128)S(1)} %pad_add_fusion.place, bf16[512,1536]{1,0:T(8,128)(2,1)S(1)} %get-tuple-element.110.rows_sent.rows_kept.act_b.rows_b, bf16[512,1536]{1,0:T(8,128)(2,1)S(1)} %get-tuple-element.164.rows_kept.rows_sent.act_a.rows_a, ...), custom_call_target="tpu_custom_call" | custom-call | flops 1 | bytes 1 | tf_op jit(solution)/shard_map/pallas_call | solution.py:108
  72.7 7.3 %collective-permute-done.15 = bf16[4,2,48,768]{3,2,1,0:T(8,128)(2,1)S(1)} collective-permute-done((bf16[4,2,48,768]{3,2,1,0:T(8,128)(2,1)S(1)}, bf16[4,2,48,768]{3,2,1,0:T(8,128)(2,1)S(1)}, u32[]{:S(2)}, u32[]{:S(2)}) %collective-permute-start.15) | collective-permute-done | bytes 589856 | tf_op jit(solution)/shard_map/ppermute | solution.py:277
  82.3 4.3 %collective-permute-start.22 = (bf16[2,48,768]{2,1,0:T(8,128)(2,1)S(1)}, bf16[2,48,768]{2,1,0:T(8,128)(2,1)S(1)}, u32[]{:S(2)}, u32[]{:S(2)}) collective-permute-start(bf16[2,48,768]{2,1,0:T(8,128)(2,1)S(1)} %pad_maximum_fusion.14), channel_id=1, source_target_pairs={{0,8},{1,9},{2,10},{3,11},{4,12},{5,13},{6,14},{7,15},{8,0},{9,1},... | collective-permute-start | bytes 442376 | tf_op jit(solution)/shard_map/ppermute | solution.py:250
  87.4 3.8 %shard_map.78 = (bf16[512,768]{1,0:T(8,128)(2,1)S(1)}, f32[512,768]{1,0:T(8,128)S(1)}) custom-call(s32[4]{0:T(128)S(1)} %pad_add_fusion.place, bf16[512,1536]{1,0:T(8,128)(2,1)S(1)} %get-tuple-element.164.rows_kept.rows_sent.act_a.rows_a, bf16[512,1536]{1,0:T(8,128)(2,1)S(1)} %get-tuple-element.110.rows_sent.rows_kept.act_b.rows_b, ...), custom_call_target="tpu_custom_call" | custom-call | flops 1 | bytes 1 | tf_op jit(solution)/shard_map/pallas_call | solution.py:108
  95.5 3.6 %collective-permute-start.18 = (bf16[512,768]{1,0:T(8,128)(2,1)S(1)}, bf16[512,768]{1,0:T(8,128)(2,1)S(1)}, u32[]{:S(2)}, u32[]{:S(2)}) collective-permute-start(bf16[512,768]{1,0:T(8,128)(2,1)S(1)} %get-tuple-element.93), channel_id=1, source_target_pairs={{4,0},{5,1},{6,2},{7,3},{8,4},{9,5},{10,6},{11,7},{12,8},{13,9},{1... | collective-permute-start | bytes 2359304 | tf_op jit(solution)/shard_map/ppermute | solution.py:256
  101.5 4.0 %shard_map.80 = (f32[512,768]{1,0:T(8,128)S(1)}, f32[512,768]{1,0:T(8,128)S(1)}) custom-call(s32[4]{0:T(128)S(1)} %pad_add_fusion.place, f32[512,768]{1,0:T(8,128)S(1)} %get-tuple-element.87.near_a, f32[512,768]{1,0:T(8,128)S(1)} %get-tuple-element.88.near_b, bf16[512,1536]{1,0:T(8,128)(2,1)S(1)} %get-tuple-element.164.rows_kept.rows_sent.act_a.rows_a, ...), custom_call_target="tpu_custom_call" | custom-call | flops 1 | bytes 1 | tf_op jit(solution)/shard_map/pallas_call | solution.py:108
  105.5 8.0 %collective-permute-done.24 = bf16[4,2,48,768]{3,2,1,0:T(8,128)(2,1)S(1)} collective-permute-done((bf16[4,2,48,768]{3,2,1,0:T(8,128)(2,1)S(1)}, bf16[4,2,48,768]{3,2,1,0:T(8,128)(2,1)S(1)}, u32[]{:S(2)}, u32[]{:S(2)}) %collective-permute-start.24) | collective-permute-done | bytes 589856 | tf_op jit(solution)/shard_map/ppermute | solution.py:277
  113.8 3.6 %collective-permute-done.18.from_next = bf16[512,768]{1,0:T(8,128)(2,1)S(1)} collective-permute-done((bf16[512,768]{1,0:T(8,128)(2,1)S(1)}, bf16[512,768]{1,0:T(8,128)(2,1)S(1)}, u32[]{:S(2)}, u32[]{:S(2)}) %collective-permute-start.18) | collective-permute-done | bytes 786464 | tf_op jit(solution)/shard_map/ppermute | solution.py:256
  117.6 3.6 %shard_map.81 = (f32[2,512,768]{2,1,0:T(8,128)S(1)}, bf16[2,512,768]{2,1,0:T(8,128)(2,1)S(1)}, bf16[512,768]{1,0:T(8,128)(2,1)S(1)}) custom-call(s32[4]{0:T(128)S(1)} %pad_add_fusion.place, f32[512,768]{1,0:T(8,128)S(1)} %get-tuple-element.91.near_a, f32[512,768]{1,0:T(8,128)S(1)} %get-tuple-element.92.near_b, ...), custom_call_target="tpu_custom_call" | custom-call | flops 1 | bytes 1 | tf_op jit(solution)/shard_map/pallas_call | solution.py:108
  123.0 4.7 %shard_map.83 = (f32[2,4,96,768]{3,2,1,0:T(8,128)S(1)}, bf16[2,4,96,768]{3,2,1,0:T(8,128)(2,1)S(1)}) custom-call(s32[4]{0:T(128)S(1)} %pad_add_fusion.place, bf16[512,1536]{1,0:T(8,128)(2,1)S(1)} %get-tuple-element.163.rows_a.cot_a, bf16[512,1536]{1,0:T(8,128)(2,1)S(1)} %get-tuple-element.162.rows_b.cot_b, bf16[512,768]{1,0:T(8,128)(2,1)S(1)} %get-tuple-element.169.grad_a, ...), custom_call_target="tpu_custom_call" | custom-call | flops 1 | bytes 1 | tf_op jit(solution)/shard_map/pallas_call | solution.py:108
  128.7 5.4 %shard_map.84 = (bf16[512,768]{1,0:T(8,128)(2,1)S(1)}, bf16[512,768]{1,0:T(8,128)(2,1)S(1)}) custom-call(s32[4]{0:T(128)S(1)} %pad_add_fusion.place, f32[2,512,768]{2,1,0:T(8,128)S(1)} %get-tuple-element.97.hidden, bf16[512,1536]{1,0:T(8,128)(2,1)S(1)} %get-tuple-element.163.rows_a.cot_a, bf16[512,1536]{1,0:T(8,128)(2,1)S(1)} %get-tuple-element.162.rows_b.cot_b, ...), custom_call_target="tpu_custom_call" | custom-call | flops 10000000000 | bytes 1 | tf_op jit(solution)/shard_map/pallas_call | solution.py:108
  134.1 3.7 %collective-permute-start.27 = (bf16[512,768]{1,0:T(8,128)(2,1)S(1)}, bf16[512,768]{1,0:T(8,128)(2,1)S(1)}, u32[]{:S(2)}, u32[]{:S(2)}) collective-permute-start(bf16[512,768]{1,0:T(8,128)(2,1)S(1)} %get-tuple-element.111.grad_b.grad_a.hg_b), channel_id=1, source_target_pairs={{0,4},{1,5},{2,6},{3,7},{4,8},{5,9},{6,10},{7,11},{8,12},{9,13},{1... | collective-permute-start | bytes 2359304 | tf_op jit(solution)/shard_map/ppermute | solution.py:253
  146.0 4.2 %shard_map.87 = (f32[2,4,96,768]{3,2,1,0:T(8,128)S(1)}, bf16[2,4,96,768]{3,2,1,0:T(8,128)(2,1)S(1)}) custom-call(s32[4]{0:T(128)S(1)} %pad_add_fusion.place, bf16[1536,1024]{1,0:T(8,128)(2,1)S(1)} %shard_map.86.turned, bf16[512,768]{1,0:T(8,128)(2,1)S(1)} %get-tuple-element.119.grad_a.grad_b.hg_a, bf16[512,768]{1,0:T(8,128)(2,1)S(1)} %get-tuple-element.111.grad_b.grad_a.hg_b), custom_call_target="tpu_custom_call" | custom-call | flops 1 | bytes 1 | tf_op jit(solution)/shard_map/pallas_call | solution.py:108
  150.3 5.4 %collective-permute-done.27.grad_a.hg_prev = bf16[512,768]{1,0:T(8,128)(2,1)S(1)} collective-permute-done((bf16[512,768]{1,0:T(8,128)(2,1)S(1)}, bf16[512,768]{1,0:T(8,128)(2,1)S(1)}, u32[]{:S(2)}, u32[]{:S(2)}) %collective-permute-start.27) | collective-permute-done | bytes 786464 | tf_op jit(solution)/shard_map/ppermute | solution.py:253
  155.7 3.6 %collective-permute-done.26.grad_b.hg_next = bf16[512,768]{1,0:T(8,128)(2,1)S(1)} collective-permute-done((bf16[512,768]{1,0:T(8,128)(2,1)S(1)}, bf16[512,768]{1,0:T(8,128)(2,1)S(1)}, u32[]{:S(2)}, u32[]{:S(2)}) %collective-permute-start.26) | collective-permute-done | bytes 786464 | tf_op jit(solution)/shard_map/ppermute | solution.py:256
  159.3 4.2 %shard_map.88 = (f32[2,4,96,768]{3,2,1,0:T(8,128)S(1)}, bf16[2,4,96,768]{3,2,1,0:T(8,128)(2,1)S(1)}) custom-call(s32[4]{0:T(128)S(1)} %pad_add_fusion.place, bf16[1536,1024]{1,0:T(8,128)(2,1)S(1)} %shard_map.86.turned, bf16[512,768]{1,0:T(8,128)(2,1)S(1)} %get-tuple-element.111.grad_b.grad_a.hg_b, bf16[512,768]{1,0:T(8,128)(2,1)S(1)} %collective-permute-done.26.grad_b.hg_next), custom_call_target="tpu_custom_call" | custom-call | flops 10000000000 | bytes 1 | tf_op jit(solution)/shard_map/pallas_call | solution.py:108
  164.8 4.3 %shard_map.90 = (f32[2,4,96,768]{3,2,1,0:T(8,128)S(1)}, bf16[2,4,96,768]{3,2,1,0:T(8,128)(2,1)S(1)}) custom-call(s32[4]{0:T(128)S(1)} %pad_add_fusion.place, bf16[1536,1024]{1,0:T(8,128)(2,1)S(1)} %shard_map.86.turned, bf16[512,768]{1,0:T(8,128)(2,1)S(1)} %collective-permute-done.27.grad_a.hg_prev, bf16[512,768]{1,0:T(8,128)(2,1)S(1)} %get-tuple-element.119.grad_a.grad_b.hg_a), custom_call_target="tpu_custom_call" | custom-call | flops 1 | bytes 1 | tf_op jit(solution)/shard_map/pallas_call | solution.py:108
  175.6 7.0 %shard_map.93 = (bf16[512,768]{1,0:T(8,128)(2,1)S(1)}, bf16[512,768]{1,0:T(8,128)(2,1)S(1)}) custom-call(s32[4]{0:T(128)S(1)} %pad_add_fusion.place, bf16[512,768]{1,0:T(8,128)(2,1)S(1)} %collective-permute-done.26.grad_b.hg_next, bf16[512,768]{1,0:T(8,128)(2,1)S(1)} %get-tuple-element.111.grad_b.grad_a.hg_b, ...), custom_call_target="tpu_custom_call" | custom-call | flops 1 | bytes 1 | tf_op jit(solution)/shard_map/pallas_call | solution.py:108
  185.7 5.9 %collective-permute-done.35 = bf16[96,768]{1,0:T(8,128)(2,1)S(1)} collective-permute-done((bf16[96,768]{1,0:T(8,128)(2,1)S(1)}, bf16[96,768]{1,0:T(8,128)(2,1)S(1)}, u32[]{:S(2)}, u32[]{:S(2)}) %collective-permute-start.35) | collective-permute-done | bytes 147488 | tf_op jit(solution)/shard_map/ppermute | solution.py:250
  202.9 7.1 %shard_map.97 = (bf16[512,768]{1,0:T(8,128)(2,1)S(1)}, bf16[512,768]{1,0:T(8,128)(2,1)S(1)}) custom-call(s32[4]{0:T(128)S(1)} %pad_add_fusion.place, bf16[512,768]{1,0:T(8,128)(2,1)S(1)} %collective-permute-done.26.grad_b.hg_next, bf16[512,768]{1,0:T(8,128)(2,1)S(1)} %get-tuple-element.111.grad_b.grad_a.hg_b, ...), custom_call_target="tpu_custom_call" | custom-call | flops 1 | bytes 1 | tf_op jit(solution)/shard_map/pallas_call | solution.py:108
  215.3 5.6 %shard_map.94 = bf16[2,512,1536]{2,1,0:T(8,128)(2,1)} custom-call(s32[4]{0:T(128)S(1)} %pad_add_fusion.place, bf16[2,512,768]{2,1,0:T(8,128)(2,1)S(1)} %get-tuple-element.95.gated, bf16[512,768]{1,0:T(8,128)(2,1)S(1)} %copy-done.5, bf16[1536,768]{1,0:T(8,128)(2,1)S(1)} %bitcast.71, bf16[2,512,1536]{2,1,0:T(8,128)(2,1)S(1)} %copy-done.3), custom_call_target="tpu_custom_call" | custom-call | flops 1 | bytes 1 | tf_op jit(solution)/shard_map/pallas_call | solution.py:108
  233.1 3.2 %collective-permute-done.47 = bf16[96,768]{1,0:T(8,128)(2,1)S(1)} collective-permute-done((bf16[96,768]{1,0:T(8,128)(2,1)S(1)}, bf16[96,768]{1,0:T(8,128)(2,1)S(1)}, u32[]{:S(2)}, u32[]{:S(2)}) %collective-permute-start.47) | collective-permute-done | bytes 147488 | tf_op jit(solution)/shard_map/ppermute | solution.py:250
  236.3 4.9 %collective-permute-done.48 = bf16[96,768]{1,0:T(8,128)(2,1)S(1)} collective-permute-done((bf16[96,768]{1,0:T(8,128)(2,1)S(1)}, bf16[96,768]{1,0:T(8,128)(2,1)S(1)}, u32[]{:S(2)}, u32[]{:S(2)}) %collective-permute-start.48) | collective-permute-done | bytes 147488 | tf_op jit(solution)/shard_map/ppermute | solution.py:250
  241.2 3.7 %collective-permute-done.49 = bf16[96,768]{1,0:T(8,128)(2,1)S(1)} collective-permute-done((bf16[96,768]{1,0:T(8,128)(2,1)S(1)}, bf16[96,768]{1,0:T(8,128)(2,1)S(1)}, u32[]{:S(2)}, u32[]{:S(2)}) %collective-permute-start.49) | collective-permute-done | bytes 147488 | tf_op jit(solution)/shard_map/ppermute | solution.py:250
  (135 shorter events, 93.7 us)
Async XLA Ops:
  10.5 35.4 %collective-permute-start.1 = (bf16[512,1536]{1,0:T(8,128)(2,1)S(1)}, bf16[512,1536]{1,0:T(8,128)(2,1)}, u32[]{:S(2)}, u32[]{:S(2)}) collective-permute-start(bf16[512,1536]{1,0:T(8,128)(2,1)S(1)} %dynamic-slice_bitcast_fusion.1), channel_id=1, source_target_pairs={{0,2},{1,3},{2,0},{3,1},{4,6},{5,7},{6,4},{7,5},{8,10},{9,11},{10,... | collective-permute-start | bytes 4718600 | tf_op jit(solution)/shard_map/ppermute | solution.py:250
  14.0 12.9 %collective-permute-start.4 = (bf16[2,48,768]{2,1,0:T(8,128)(2,1)S(1)}, bf16[2,48,768]{2,1,0:T(8,128)(2,1)S(1)}, u32[]{:S(2)}, u32[]{:S(2)}) collective-permute-start(bf16[2,48,768]{2,1,0:T(8,128)(2,1)S(1)} %get-tuple-element.181), channel_id=1, source_target_pairs={{0,12},{1,13},{2,14},{3,15},{4,8},{5,9},{6,10},{7,11},{8,4},{9,5},... | collective-permute-start | bytes 442376 | tf_op jit(solution)/shard_map/ppermute | solution.py:250
  27.0 14.8 %collective-permute-start.8 = (bf16[4,2,48,768]{3,2,1,0:T(8,128)(2,1)S(1)}, bf16[4,2,48,768]{3,2,1,0:T(8,128)(2,1)}, u32[]{:S(2)}, u32[]{:S(2)}) collective-permute-start(bf16[4,2,48,768]{3,2,1,0:T(8,128)(2,1)S(1)} %get-tuple-element.171), channel_id=1, source_target_pairs={{0,16},{16,0},{1,17},{17,1},{2,18},{18,2},{3,19},{19,3},{4,20},{20... | collective-permute-start | bytes 1769480 | tf_op jit(solution)/shard_map/ppermute | solution.py:277
  44.0 23.0 %collective-permute-start.10 = (bf16[2,4,2,48,768]{4,3,2,1,0:T(8,128)(2,1)}, bf16[2,4,2,48,768]{4,3,2,1,0:T(8,128)(2,1)}, u32[]{:S(2)}, u32[]{:S(2)}) collective-permute-start(bf16[2,4,2,48,768]{4,3,2,1,0:T(8,128)(2,1)} %pad_maximum_fusion.3.kept), channel_id=1, source_target_pairs={{0,1},{1,0},{2,3},{3,2},{4,5},{5,4},{6,7},{7,6},{8,9},{9,8},{10,11... | collective-permute-start | bytes 3538952 | tf_op jit(solution)/shard_map/ppermute | solution.py:250
  44.0 16.1 %collective-permute-start.9 = (bf16[4,2,48,768]{3,2,1,0:T(8,128)(2,1)}, bf16[4,2,48,768]{3,2,1,0:T(8,128)(2,1)}, u32[]{:S(2)}, u32[]{:S(2)}) collective-permute-start(bf16[4,2,48,768]{3,2,1,0:T(8,128)(2,1)} %pad_maximum_fusion.8), channel_id=1, source_target_pairs={{0,16},{16,0},{1,17},{17,1},{2,18},{18,2},{3,19},{19,3},{4,20},{20... | collective-permute-start | bytes 1769480 | tf_op jit(solution)/shard_map/ppermute | solution.py:277
  50.6 12.6 %collective-permute-start.14 = (bf16[2,48,768]{2,1,0:T(8,128)(2,1)S(1)}, bf16[2,48,768]{2,1,0:T(8,128)(2,1)}, u32[]{:S(2)}, u32[]{:S(2)}) collective-permute-start(bf16[2,48,768]{2,1,0:T(8,128)(2,1)S(1)} %pad_maximum_fusion.13), channel_id=1, source_target_pairs={{0,12},{1,13},{2,14},{3,15},{4,8},{5,9},{6,10},{7,11},{8,4},{9,5},... | collective-permute-start | bytes 442376 | tf_op jit(solution)/shard_map/ppermute | solution.py:250
  51.1 12.5 %collective-permute-start.13 = (bf16[2,48,768]{2,1,0:T(8,128)(2,1)S(1)}, bf16[2,48,768]{2,1,0:T(8,128)(2,1)}, u32[]{:S(2)}, u32[]{:S(2)}) collective-permute-start(bf16[2,48,768]{2,1,0:T(8,128)(2,1)S(1)} %pad_maximum_fusion.13), channel_id=1, source_target_pairs={{0,8},{1,9},{2,10},{3,11},{4,12},{5,13},{6,14},{7,15},{8,0},{9,1},... | collective-permute-start | bytes 442376 | tf_op jit(solution)/shard_map/ppermute | solution.py:250
  65.4 14.7 %collective-permute-start.15 = (bf16[4,2,48,768]{3,2,1,0:T(8,128)(2,1)S(1)}, bf16[4,2,48,768]{3,2,1,0:T(8,128)(2,1)S(1)}, u32[]{:S(2)}, u32[]{:S(2)}) collective-permute-start(bf16[4,2,48,768]{3,2,1,0:T(8,128)(2,1)S(1)} %pad_maximum_fusion.9), channel_id=1, source_target_pairs={{0,16},{16,0},{1,17},{17,1},{2,18},{18,2},{3,19},{19,3},{4,20},{20... | collective-permute-start | bytes 1769480 | tf_op jit(solution)/shard_map/ppermute | solution.py:277
  72.6 14.0 %collective-permute-start.11 = (bf16[2,4,2,48,768]{4,3,2,1,0:T(8,128)(2,1)S(1)}, bf16[2,4,2,48,768]{4,3,2,1,0:T(8,128)(2,1)S(1)}, u32[]{:S(2)}, u32[]{:S(2)}) collective-permute-start(bf16[2,4,2,48,768]{4,3,2,1,0:T(8,128)(2,1)S(1)} %pad_maximum_fusion.4.kept), channel_id=1, source_target_pairs={{0,1},{1,0},{2,3},{3,2},{4,5},{5,4},{6,7},{7,6},{8,9},{9,8},{10,11... | collective-permute-start | bytes 3538952 | tf_op jit(solution)/shard_map/ppermute | solution.py:250
  80.2 20.6 %collective-permute-start.16 = (bf16[2,4,2,48,768]{4,3,2,1,0:T(8,128)(2,1)S(1)}, bf16[2,4,2,48,768]{4,3,2,1,0:T(8,128)(2,1)S(1)}, u32[]{:S(2)}, u32[]{:S(2)}) collective-permute-start(bf16[2,4,2,48,768]{4,3,2,1,0:T(8,128)(2,1)S(1)} %pad_maximum_fusion.5.kept), channel_id=1, source_target_pairs={{0,1},{1,0},{2,3},{3,2},{4,5},{5,4},{6,7},{7,6},{8,9},{9,8},{10,11... | collective-permute-start | bytes 3538952 | tf_op jit(solution)/shard_map/ppermute | solution.py:250
  80.4 37.0 %collective-permute-start.20 = (bf16[512,1536]{1,0:T(8,128)(2,1)S(1)}, bf16[512,1536]{1,0:T(8,128)(2,1)S(1)}, u32[]{:S(2)}, u32[]{:S(2)}) collective-permute-start(bf16[512,1536]{1,0:T(8,128)(2,1)S(1)} %dynamic-slice_bitcast_fusion), channel_id=1, source_target_pairs={{0,2},{1,3},{2,0},{3,1},{4,6},{5,7},{6,4},{7,5},{8,10},{9,11},{10,... | collective-permute-start | bytes 4718600 | tf_op jit(solution)/shard_map/ppermute | solution.py:250
  82.3 13.2 %collective-permute-start.22 = (bf16[2,48,768]{2,1,0:T(8,128)(2,1)S(1)}, bf16[2,48,768]{2,1,0:T(8,128)(2,1)S(1)}, u32[]{:S(2)}, u32[]{:S(2)}) collective-permute-start(bf16[2,48,768]{2,1,0:T(8,128)(2,1)S(1)} %pad_maximum_fusion.14), channel_id=1, source_target_pairs={{0,8},{1,9},{2,10},{3,11},{4,12},{5,13},{6,14},{7,15},{8,0},{9,1},... | collective-permute-start | bytes 442376 | tf_op jit(solution)/shard_map/ppermute | solution.py:250
  87.4 11.8 %collective-permute-start.21 = (bf16[2,48,768]{2,1,0:T(8,128)(2,1)S(1)}, bf16[2,48,768]{2,1,0:T(8,128)(2,1)S(1)}, u32[]{:S(2)}, u32[]{:S(2)}) collective-permute-start(bf16[2,48,768]{2,1,0:T(8,128)(2,1)S(1)} %pad_maximum_fusion.14), channel_id=1, source_target_pairs={{0,4},{1,5},{2,6},{3,7},{4,0},{5,1},{6,2},{7,3},{8,12},{9,13},{10,... | collective-permute-start | bytes 442376 | tf_op jit(solution)/shard_map/ppermute | solution.py:250
  92.5 21.2 %collective-permute-start.17 = (bf16[512,768]{1,0:T(8,128)(2,1)S(1)}, bf16[512,768]{1,0:T(8,128)(2,1)S(1)}, u32[]{:S(2)}, u32[]{:S(2)}) collective-permute-start(bf16[512,768]{1,0:T(8,128)(2,1)S(1)} %get-tuple-element.84), channel_id=1, source_target_pairs={{0,4},{1,5},{2,6},{3,7},{4,8},{5,9},{6,10},{7,11},{8,12},{9,13},{1... | collective-permute-start | bytes 2359304 | tf_op jit(solution)/shard_map/ppermute | solution.py:253
  95.5 21.8 %collective-permute-start.18 = (bf16[512,768]{1,0:T(8,128)(2,1)S(1)}, bf16[512,768]{1,0:T(8,128)(2,1)S(1)}, u32[]{:S(2)}, u32[]{:S(2)}) collective-permute-start(bf16[512,768]{1,0:T(8,128)(2,1)S(1)} %get-tuple-element.93), channel_id=1, source_target_pairs={{4,0},{5,1},{6,2},{7,3},{8,4},{9,5},{10,6},{11,7},{12,8},{13,9},{1... | collective-permute-start | bytes 2359304 | tf_op jit(solution)/shard_map/ppermute | solution.py:256
  99.2 14.3 %collective-permute-start.24 = (bf16[4,2,48,768]{3,2,1,0:T(8,128)(2,1)S(1)}, bf16[4,2,48,768]{3,2,1,0:T(8,128)(2,1)S(1)}, u32[]{:S(2)}, u32[]{:S(2)}) collective-permute-start(bf16[4,2,48,768]{3,2,1,0:T(8,128)(2,1)S(1)} %pad_maximum_fusion.10), channel_id=1, source_target_pairs={{0,16},{16,0},{1,17},{17,1},{2,18},{18,2},{3,19},{19,3},{4,20},{20... | collective-permute-start | bytes 1769480 | tf_op jit(solution)/shard_map/ppermute | solution.py:277
  121.2 20.0 %collective-permute-start.19 = (bf16[512,768]{1,0:T(8,128)(2,1)S(1)}, bf16[512,768]{1,0:T(8,128)(2,1)S(1)}, u32[]{:S(2)}, u32[]{:S(2)}) collective-permute-start(bf16[512,768]{1,0:T(8,128)(2,1)S(1)} %get-tuple-element.96), channel_id=1, source_target_pairs={{0,2},{1,3},{2,0},{3,1},{4,6},{5,7},{6,4},{7,5},{8,10},{9,11},{10,... | collective-permute-start | bytes 2359304 | tf_op jit(solution)/shard_map/ppermute | solution.py:250
  127.7 13.5 %collective-permute-start.28 = (bf16[2,4,96,768]{3,2,1,0:T(8,128)(2,1)S(1)}, bf16[2,4,96,768]{3,2,1,0:T(8,128)(2,1)S(1)}, u32[]{:S(2)}, u32[]{:S(2)}) collective-permute-start(bf16[2,4,96,768]{3,2,1,0:T(8,128)(2,1)S(1)} %get-tuple-element.108), channel_id=1, source_target_pairs={{0,1},{1,0},{2,3},{3,2},{4,5},{5,4},{6,7},{7,6},{8,9},{9,8},{10,11... | collective-permute-start | bytes 3538952 | tf_op jit(solution)/shard_map/ppermute | solution.py:250
  134.1 21.6 %collective-permute-start.27 = (bf16[512,768]{1,0:T(8,128)(2,1)S(1)}, bf16[512,768]{1,0:T(8,128)(2,1)S(1)}, u32[]{:S(2)}, u32[]{:S(2)}) collective-permute-start(bf16[512,768]{1,0:T(8,128)(2,1)S(1)} %get-tuple-element.111.grad_b.grad_a.hg_b), channel_id=1, source_target_pairs={{0,4},{1,5},{2,6},{3,7},{4,8},{5,9},{6,10},{7,11},{8,12},{9,13},{1... | collective-permute-start | bytes 2359304 | tf_op jit(solution)/shard_map/ppermute | solution.py:253
  137.8 21.5 %collective-permute-start.26 = (bf16[512,768]{1,0:T(8,128)(2,1)S(1)}, bf16[512,768]{1,0:T(8,128)(2,1)S(1)}, u32[]{:S(2)}, u32[]{:S(2)}) collective-permute-start(bf16[512,768]{1,0:T(8,128)(2,1)S(1)} %get-tuple-element.119.grad_a.grad_b.hg_a), channel_id=1, source_target_pairs={{4,0},{5,1},{6,2},{7,3},{8,4},{9,5},{10,6},{11,7},{12,8},{13,9},{1... | collective-permute-start | bytes 2359304 | tf_op jit(solution)/shard_map/ppermute | solution.py:256
  144.3 19.4 %collective-permute-start.29 = (bf16[4,96,768]{2,1,0:T(8,128)(2,1)S(1)}, bf16[4,96,768]{2,1,0:T(8,128)(2,1)S(1)}, u32[]{:S(2)}, u32[]{:S(2)}) collective-permute-start(bf16[4,96,768]{2,1,0:T(8,128)(2,1)S(1)} %get-tuple-element.115), channel_id=1, source_target_pairs={{0,2},{1,3},{2,0},{3,1},{4,6},{5,7},{6,4},{7,5},{8,10},{9,11},{10,... | collective-permute-start | bytes 1769480 | tf_op jit(solution)/shard_map/ppermute | solution.py:250
  150.2 13.5 %collective-permute-start.30 = (bf16[2,4,96,768]{3,2,1,0:T(8,128)(2,1)S(1)}, bf16[2,4,96,768]{3,2,1,0:T(8,128)(2,1)S(1)}, u32[]{:S(2)}, u32[]{:S(2)}) collective-permute-start(bf16[2,4,96,768]{3,2,1,0:T(8,128)(2,1)S(1)} %get-tuple-element.117), channel_id=1, source_target_pairs={{0,1},{1,0},{2,3},{3,2},{4,5},{5,4},{6,7},{7,6},{8,9},{9,8},{10,11... | collective-permute-start | bytes 3538952 | tf_op jit(solution)/shard_map/ppermute | solution.py:250
  169.0 23.2 %collective-permute-start.37 = (bf16[2,4,96,768]{3,2,1,0:T(8,128)(2,1)S(1)}, bf16[2,4,96,768]{3,2,1,0:T(8,128)(2,1)S(1)}, u32[]{:S(2)}, u32[]{:S(2)}) collective-permute-start(bf16[2,4,96,768]{3,2,1,0:T(8,128)(2,1)S(1)} %get-tuple-element.137), channel_id=1, source_target_pairs={{0,1},{1,0},{2,3},{3,2},{4,5},{5,4},{6,7},{7,6},{8,9},{9,8},{10,11... | collective-permute-start | bytes 3538952 | tf_op jit(solution)/shard_map/ppermute | solution.py:250
  169.6 22.0 %collective-permute-start.36 = (bf16[4,96,768]{2,1,0:T(8,128)(2,1)S(1)}, bf16[4,96,768]{2,1,0:T(8,128)(2,1)S(1)}, u32[]{:S(2)}, u32[]{:S(2)}) collective-permute-start(bf16[4,96,768]{2,1,0:T(8,128)(2,1)S(1)} %get-tuple-element.134), channel_id=1, source_target_pairs={{0,2},{1,3},{2,0},{3,1},{4,6},{5,7},{6,4},{7,5},{8,10},{9,11},{10,... | collective-permute-start | bytes 1769480 | tf_op jit(solution)/shard_map/ppermute | solution.py:250
  171.9 12.0 %collective-permute-start.34 = (bf16[96,768]{1,0:T(8,128)(2,1)S(1)}, bf16[96,768]{1,0:T(8,128)(2,1)S(1)}, u32[]{:S(2)}, u32[]{:S(2)}) collective-permute-start(bf16[96,768]{1,0:T(8,128)(2,1)S(1)} %get-tuple-element.131), channel_id=1, source_target_pairs={{0,8},{1,9},{2,10},{3,11},{4,12},{5,13},{6,14},{7,15},{8,0},{9,1},... | collective-permute-start | bytes 442376 | tf_op jit(solution)/shard_map/ppermute | solution.py:250
  174.8 35.3 %collective-permute-start.41 = (bf16[4,96,768]{2,1,0:T(8,128)(2,1)S(1)}, bf16[4,96,768]{2,1,0:T(8,128)(2,1)S(1)}, u32[]{:S(2)}, u32[]{:S(2)}) collective-permute-start(bf16[4,96,768]{2,1,0:T(8,128)(2,1)S(1)} %get-tuple-element.146), channel_id=1, source_target_pairs={{0,2},{1,3},{2,0},{3,1},{4,6},{5,7},{6,4},{7,5},{8,10},{9,11},{10,... | collective-permute-start | bytes 1769480 | tf_op jit(solution)/shard_map/ppermute | solution.py:250
  182.6 32.6 %collective-permute-start.32 = (bf16[512,768]{1,0:T(8,128)(2,1)S(1)}, bf16[512,768]{1,0:T(8,128)(2,1)S(1)}, u32[]{:S(2)}, u32[]{:S(2)}) collective-permute-start(bf16[512,768]{1,0:T(8,128)(2,1)S(1)} %get-tuple-element.127), channel_id=1, source_target_pairs={{0,2},{1,3},{2,0},{3,1},{4,6},{5,7},{6,4},{7,5},{8,10},{9,11},{10,... | collective-permute-start | bytes 2359304 | tf_op jit(solution)/shard_map/ppermute | solution.py:250
  193.3 33.7 %collective-permute-start.45 = (bf16[4,96,768]{2,1,0:T(8,128)(2,1)S(1)}, bf16[4,96,768]{2,1,0:T(8,128)(2,1)S(1)}, u32[]{:S(2)}, u32[]{:S(2)}) collective-permute-start(bf16[4,96,768]{2,1,0:T(8,128)(2,1)S(1)} %get-tuple-element.152), channel_id=1, source_target_pairs={{0,2},{1,3},{2,0},{3,1},{4,6},{5,7},{6,4},{7,5},{8,10},{9,11},{10,... | collective-permute-start | bytes 1769480 | tf_op jit(solution)/shard_map/ppermute | solution.py:250
  194.4 15.6 %collective-permute-start.39 = (bf16[96,768]{1,0:T(8,128)(2,1)S(1)}, bf16[96,768]{1,0:T(8,128)(2,1)S(1)}, u32[]{:S(2)}, u32[]{:S(2)}) collective-permute-start(bf16[96,768]{1,0:T(8,128)(2,1)S(1)} %get-tuple-element.143), channel_id=1, source_target_pairs={{0,8},{1,9},{2,10},{3,11},{4,12},{5,13},{6,14},{7,15},{8,0},{9,1},... | collective-permute-start | bytes 442376 | tf_op jit(solution)/shard_map/ppermute | solution.py:250
  213.6 12.3 %collective-permute-start.44 = (bf16[96,768]{1,0:T(8,128)(2,1)S(1)}, bf16[96,768]{1,0:T(8,128)(2,1)S(1)}, u32[]{:S(2)}, u32[]{:S(2)}) collective-permute-start(bf16[96,768]{1,0:T(8,128)(2,1)S(1)} %get-tuple-element.150), channel_id=1, source_target_pairs={{0,12},{1,13},{2,14},{3,15},{4,8},{5,9},{6,10},{7,11},{8,4},{9,5},... | collective-permute-start | bytes 442376 | tf_op jit(solution)/shard_map/ppermute | solution.py:250
  227.7 18.7 %collective-permute-start.46 = (bf16[512,768]{1,0:T(8,128)(2,1)S(1)}, bf16[512,768]{1,0:T(8,128)(2,1)S(1)}, u32[]{:S(2)}, u32[]{:S(2)}) collective-permute-start(bf16[512,768]{1,0:T(8,128)(2,1)S(1)} %get-tuple-element.154), channel_id=1, source_target_pairs={{0,2},{1,3},{2,0},{3,1},{4,6},{5,7},{6,4},{7,5},{8,10},{9,11},{10,... | collective-permute-start | bytes 2359304 | tf_op jit(solution)/shard_map/ppermute | solution.py:250
  231.3 13.6 %collective-permute-start.49 = (bf16[96,768]{1,0:T(8,128)(2,1)S(1)}, bf16[96,768]{1,0:T(8,128)(2,1)S(1)}, u32[]{:S(2)}, u32[]{:S(2)}) collective-permute-start(bf16[96,768]{1,0:T(8,128)(2,1)S(1)} %get-tuple-element.157), channel_id=1, source_target_pairs={{0,12},{1,13},{2,14},{3,15},{4,8},{5,9},{6,10},{7,11},{8,4},{9,5},... | collective-permute-start | bytes 442376 | tf_op jit(solution)/shard_map/ppermute | solution.py:250
  (25 other events, 209.4 us)

commit v5 on v4

--- a/solution.py
+++ b/solution.py
@@ -291,13 +291,13 @@
     half_0 = over_y(column_0)
     in_a, in_b = ordered(pick(inputs, x), in_got)
     act_a, act_b = act(in_a), act(in_b)
-    column_1 = along_z(after(column(1), column_2, half_0, (act_a, act_b)))
+    column_1 = along_z(after(column(1), column_2, half_0))
     half_2 = over_y(after(column_2, half_0))
     w0 = placed(place, half_0, swap(half_0, 1))
     cot_got = swap(after(pick(cotangent, 1 - x), in_got, column_1), 2)
     to_next, near_b = tap_sums(act_b, act_a, w0)
     from_prev = up(to_next)
-    w2 = placed(place, half_2, swap(after(half_2, to_next), 1))
+    w2 = placed(place, half_2, swap(after(half_2, to_next, column_1), 1))
     half_1 = over_y(after(column_1, half_2))
     to_prev, near_a = tap_sums(act_a, act_b, after(w2, to_next))
     from_next = down(to_prev)
@@ -320,7 +320,7 @@
     hidden, gated, gated_sent = call(
         gated_kernel,
         [((2, local_len, hid), f32), ((2, local_len, hid), bf16), ((local_len, hid), bf16)],
-        place, near_a, near_b, from_prev, after(from_next, near_a),
+        place, near_a, near_b, from_prev, from_next,
         grid=(hid // tile,),
         ins=[block((local_len, tile), 0, 1)] * 4,
         out_specs=[block((2, local_len, tile), 0, 0, 1)] * 2 + [block((local_len, tile), 0, 1)],
@@ -377,7 +377,7 @@
         return sum(part.astype(f32) for part in parts)
 
     cot_a, cot_b = ordered(pick(cotangent, x), cot_got)
-    wp = placed(place, half_p, swap(after(half_p, from_prev, from_next, (near_a, near_b)), 1))
+    wp = placed(place, half_p, swap(after(half_p, from_prev, from_next, (near_a, near_b), (cot_a, cot_b)), 1))
     term_p = term((cot_a, cot_b), gated[0], gated[1], 1)
     hg_a, hg_b = call(
         hidden_grad_kernel,
@@ -428,7 +428,7 @@
     term_0 = term(acted, hg_b, after(hg_next, term_1[0], hg_prev), LONG)
     grad_1 = x_first(after(term_1[0], term_0[0], grad_p[1]), term_1[1])
     term_2 = term(acted, hg_prev, after(hg_a, grad_1[0]), 1)
-    grad_p = then_z(after(grad_p[0], term_2[0]), grad_p[1])
+    grad_p = then_z(after(grad_p[0], grad_1[0], term_2[0]), grad_p[1])
     grad_0 = x_first(after(term_0[0], grad_p[0]), term_0[1])
     kept_0, sent_0 = input_grads(0, grad_0[0])
     grad_1 = then_z(after(grad_1[0], sent_0, grad_p), grad_1[1])

time: 251 us -> 245 us (0.976)
  starting transfers between devices: 67.8 us -> 61.3 us
  local copies, waits for them, and re-layouts: 2.15 us -> 8.25 us
  other arithmetic: 17.8 us -> 12.9 us
    ppermute x42, starting transfers between devices: 47.8 us -> 41.4 us  [swap(): return lax.ppermute(value, 'seq', [(i, i ^ bits) for i in everyone])]
    ppermute x42, waiting for transfers between devices: 56.3 us -> 60.8 us  [swap(): return lax.ppermute(value, 'seq', [(i, i ^ bits) for i in everyone])]
    ppermute x4, waiting for transfers between devices: 20.6 us -> 17 us  [over_y(): return jnp.stack([column, lax.ppermute(column, 'groups', [(0, 1), (1, 0)])])]
    unnamed x14 -> x18, local copies, waits for them, and re-layouts: 0.38 us -> 2.95 us
  transfers between devices with their start and end apart: 50 -> 50, of which waited for: 30 -> 23; matrix products, arithmetic and copies ran while one was open for 6% -> 6% of each run, Pallas kernels for 28% -> 28%
where the time goes in v5:
time: 245 us; the launch traced here: 243 us
  waiting for transfers between devices  89.8 us (37%)
  Pallas kernels  69.9 us (29%)
  starting transfers between devices  61.3 us (25%)
  other arithmetic  12.9 us (5%)
  local copies, waits for them, and re-layouts  8.25 us (3%)
    pallas_call x25, Pallas kernels, call(): pl.pallas_call(kernel, grid=grid, out_shape=outs, in_specs=[pl.BlockSpec(...  69.9 us
    ppermute x42, waiting for transfers between devices, swap(): return lax.ppermute(value, 'seq', [(i, i ^ bits) for i in everyone])  60.8 us
    ppermute x42, starting transfers between devices, swap(): return lax.ppermute(value, 'seq', [(i, i ^ bits) for i in everyone])  41.4 us
    ppermute x4, waiting for transfers between devices, over_y(): return jnp.stack([column, lax.ppermute(column, 'groups', [(0, 1), (1, 0)])])  17 us
    ppermute x4, starting transfers between devices, over_y(): return jnp.stack([column, lax.ppermute(column, 'groups', [(0, 1), (1, 0)])])  8.05 us
    ppermute x2, starting transfers between devices, down(): lax.ppermute(value, 'seq', [(i + 4, i) for i in everyone if i + 4 in ever...  6.55 us
    ppermute x2, waiting for transfers between devices, up(): lax.ppermute(value, 'seq', [(i, i + 4) for i in everyone if i + 4 in ever...  6.51 us
    ppermute x2, waiting for transfers between devices, down(): lax.ppermute(value, 'seq', [(i + 4, i) for i in everyone if i + 4 in ever...  5.56 us
  transfers between devices with their start and end apart: 50, of which 23 were waited for; matrix products, arithmetic and copies ran while one was open for 6% of the time, Pallas kernels for 28%

profile of v5, /device:TPU:16, one launch (start us, length us, event | category | flops | bytes accessed | tf_op | source)
XLA Modules:
  0.0 243.3 jit_solution(5605129740320910444)
XLA Ops:
  3.9 6.6 %collective-permute-done = bf16[4,48,768]{2,1,0:T(8,128)(2,1)S(1)} collective-permute-done((bf16[4,48,768]{2,1,0:T(8,128)(2,1)S(1)}, bf16[4,48,768]{2,1,0:T(8,128)(2,1)S(1)}, u32[]{:S(2)}, u32[]{:S(2)}) %collective-permute-start) | collective-permute-done | bytes 294944 | tf_op jit(solution)/shard_map/ppermute | solution.py:250
  14.7 2.7 %dynamic-slice_bitcast_fusion.1 = bf16[512,1536]{1,0:T(8,128)(2,1)} fusion(bf16[2,512,1536]{2,1,0:T(8,128)(2,1)} %inputs.1, s32[]{:T(128)S(6)} %select_n.80), kind=kLoop, calls=%fused_computation.28 | loop fusion | bytes 3145732 | tf_op jit(solution)/shard_map/jit(dynamic_index_in_dim)/squeeze | solution.py:259
  20.6 5.7 %collective-permute-done.4 = bf16[2,48,768]{2,1,0:T(8,128)(2,1)S(1)} collective-permute-done((bf16[2,48,768]{2,1,0:T(8,128)(2,1)S(1)}, bf16[2,48,768]{2,1,0:T(8,128)(2,1)S(1)}, u32[]{:S(2)}, u32[]{:S(2)}) %collective-permute-start.4) | collective-permute-done | bytes 147488 | tf_op jit(solution)/shard_map/ppermute | solution.py:250
  26.4 3.2 %collective-permute-start.8 = (bf16[4,2,48,768]{3,2,1,0:T(8,128)(2,1)S(1)}, bf16[4,2,48,768]{3,2,1,0:T(8,128)(2,1)S(1)}, u32[]{:S(2)}, u32[]{:S(2)}) collective-permute-start(bf16[4,2,48,768]{3,2,1,0:T(8,128)(2,1)S(1)} %get-tuple-element.169), channel_id=1, source_target_pairs={{0,16},{16,0},{1,17},{17,1},{2,18},{18,2},{3,19},{19,3},{4,20},{20... | collective-permute-start | bytes 1769480 | tf_op jit(solution)/shard_map/ppermute | solution.py:277
  29.8 3.4 %collective-permute-start.5 = (bf16[2,48,768]{2,1,0:T(8,128)(2,1)S(1)}, bf16[2,48,768]{2,1,0:T(8,128)(2,1)S(1)}, u32[]{:S(2)}, u32[]{:S(2)}) collective-permute-start(bf16[2,48,768]{2,1,0:T(8,128)(2,1)S(1)} %pad_maximum_fusion.11), channel_id=1, source_target_pairs={{0,4},{1,5},{2,6},{3,7},{4,0},{5,1},{6,2},{7,3},{8,12},{9,13},{10,... | collective-permute-start | bytes 442376 | tf_op jit(solution)/shard_map/ppermute | solution.py:250
  33.2 5.8 %collective-permute-done.7 = bf16[2,48,768]{2,1,0:T(8,128)(2,1)S(1)} collective-permute-done((bf16[2,48,768]{2,1,0:T(8,128)(2,1)S(1)}, bf16[2,48,768]{2,1,0:T(8,128)(2,1)S(1)}, u32[]{:S(2)}, u32[]{:S(2)}) %collective-permute-start.7) | collective-permute-done | bytes 147488 | tf_op jit(solution)/shard_map/ppermute | solution.py:250
  47.9 6.7 %collective-permute-done.13 = bf16[2,48,768]{2,1,0:T(8,128)(2,1)} collective-permute-done((bf16[2,48,768]{2,1,0:T(8,128)(2,1)S(1)}, bf16[2,48,768]{2,1,0:T(8,128)(2,1)}, u32[]{:S(2)}, u32[]{:S(2)}) %collective-permute-start.13) | collective-permute-done | bytes 147488 | tf_op jit(solution)/shard_map/ppermute | solution.py:250
  63.5 3.8 %shard_map.76 = (bf16[512,768]{1,0:T(8,128)(2,1)S(1)}, f32[512,768]{1,0:T(8,128)S(1)}) custom-call(s32[4]{0:T(128)S(1)} %pad_add_fusion.place, bf16[512,1536]{1,0:T(8,128)(2,1)S(1)} %get-tuple-element.108.rows_sent.rows_kept.act_b.rows_b, bf16[512,1536]{1,0:T(8,128)(2,1)S(1)} %get-tuple-element.162.rows_kept.rows_sent.act_a.rows_a, ...), custom_call_target="tpu_custom_call" | custom-call | flops 1 | bytes 1 | tf_op jit(solution)/shard_map/pallas_call | solution.py:108
  67.4 5.5 %collective-permute-done.15 = bf16[4,2,48,768]{3,2,1,0:T(8,128)(2,1)S(1)} collective-permute-done((bf16[4,2,48,768]{3,2,1,0:T(8,128)(2,1)S(1)}, bf16[4,2,48,768]{3,2,1,0:T(8,128)(2,1)S(1)}, u32[]{:S(2)}, u32[]{:S(2)}) %collective-permute-start.15) | collective-permute-done | bytes 589856 | tf_op jit(solution)/shard_map/ppermute | solution.py:277
  77.5 3.8 %shard_map.78 = (bf16[512,768]{1,0:T(8,128)(2,1)S(1)}, f32[512,768]{1,0:T(8,128)S(1)}) custom-call(s32[4]{0:T(128)S(1)} %pad_add_fusion.place, bf16[512,1536]{1,0:T(8,128)(2,1)S(1)} %get-tuple-element.162.rows_kept.rows_sent.act_a.rows_a, bf16[512,1536]{1,0:T(8,128)(2,1)S(1)} %get-tuple-element.108.rows_sent.rows_kept.act_b.rows_b, ...), custom_call_target="tpu_custom_call" | custom-call | flops 1 | bytes 1 | tf_op jit(solution)/shard_map/pallas_call | solution.py:108
  81.3 3.4 %collective-permute-start.17 = (bf16[512,768]{1,0:T(8,128)(2,1)S(1)}, bf16[512,768]{1,0:T(8,128)(2,1)S(1)}, u32[]{:S(2)}, u32[]{:S(2)}) collective-permute-start(bf16[512,768]{1,0:T(8,128)(2,1)S(1)} %get-tuple-element.83), channel_id=1, source_target_pairs={{0,4},{1,5},{2,6},{3,7},{4,8},{5,9},{6,10},{7,11},{8,12},{9,13},{1... | collective-permute-start | bytes 2359304 | tf_op jit(solution)/shard_map/ppermute | solution.py:253
  85.4 4.0 %shard_map.80 = (f32[512,768]{1,0:T(8,128)S(1)}, f32[512,768]{1,0:T(8,128)S(1)}) custom-call(s32[4]{0:T(128)S(1)} %pad_add_fusion.place, f32[512,768]{1,0:T(8,128)S(1)} %get-tuple-element.87.near_a, f32[512,768]{1,0:T(8,128)S(1)} %get-tuple-element.88.near_b, bf16[512,1536]{1,0:T(8,128)(2,1)S(1)} %get-tuple-element.162.rows_kept.rows_sent.act_a.rows_a, ...), custom_call_target="tpu_custom_call" | custom-call | flops 1 | bytes 1 | tf_op jit(solution)/shard_map/pallas_call | solution.py:108
  97.2 9.2 %collective-permute-done.24 = bf16[4,2,48,768]{3,2,1,0:T(8,128)(2,1)S(1)} collective-permute-done((bf16[4,2,48,768]{3,2,1,0:T(8,128)(2,1)S(1)}, bf16[4,2,48,768]{3,2,1,0:T(8,128)(2,1)S(1)}, u32[]{:S(2)}, u32[]{:S(2)}) %collective-permute-start.24) | collective-permute-done | bytes 589856 | tf_op jit(solution)/shard_map/ppermute | solution.py:277
  106.5 3.6 %collective-permute-done.18.from_next = bf16[512,768]{1,0:T(8,128)(2,1)S(1)} collective-permute-done((bf16[512,768]{1,0:T(8,128)(2,1)S(1)}, bf16[512,768]{1,0:T(8,128)(2,1)S(1)}, u32[]{:S(2)}, u32[]{:S(2)}) %collective-permute-start.18) | collective-permute-done | bytes 786464 | tf_op jit(solution)/shard_map/ppermute | solution.py:256
  110.1 3.6 %shard_map.81 = (f32[2,512,768]{2,1,0:T(8,128)S(1)}, bf16[2,512,768]{2,1,0:T(8,128)(2,1)S(1)}, bf16[512,768]{1,0:T(8,128)(2,1)S(1)}) custom-call(s32[4]{0:T(128)S(1)} %pad_add_fusion.place, f32[512,768]{1,0:T(8,128)S(1)} %get-tuple-element.90.near_a, f32[512,768]{1,0:T(8,128)S(1)} %get-tuple-element.91.near_b, ...), custom_call_target="tpu_custom_call" | custom-call | flops 1 | bytes 1 | tf_op jit(solution)/shard_map/pallas_call | solution.py:108
  115.5 4.7 %shard_map.83 = (f32[2,4,96,768]{3,2,1,0:T(8,128)S(1)}, bf16[2,4,96,768]{3,2,1,0:T(8,128)(2,1)S(1)}) custom-call(s32[4]{0:T(128)S(1)} %pad_add_fusion.place, bf16[512,1536]{1,0:T(8,128)(2,1)S(1)} %get-tuple-element.161.rows_a.cot_a, bf16[512,1536]{1,0:T(8,128)(2,1)S(1)} %get-tuple-element.160.rows_b.cot_b, bf16[512,768]{1,0:T(8,128)(2,1)S(1)} %get-tuple-element.167.grad_a, ...), custom_call_target="tpu_custom_call" | custom-call | flops 1 | bytes 1 | tf_op jit(solution)/shard_map/pallas_call | solution.py:108
  122.0 5.4 %shard_map.84 = (bf16[512,768]{1,0:T(8,128)(2,1)S(1)}, bf16[512,768]{1,0:T(8,128)(2,1)S(1)}) custom-call(s32[4]{0:T(128)S(1)} %pad_add_fusion.place, f32[2,512,768]{2,1,0:T(8,128)S(1)} %copy-done.4, bf16[512,1536]{1,0:T(8,128)(2,1)S(1)} %get-tuple-element.161.rows_a.cot_a, bf16[512,1536]{1,0:T(8,128)(2,1)S(1)} %get-tuple-element.160.rows_b.cot_b, ...), custom_call_target="tpu_custom_call" | custom-call | flops 10000000000 | bytes 1 | tf_op jit(solution)/shard_map/pallas_call | solution.py:108
  129.3 4.1 %collective-permute-start.26 = (bf16[512,768]{1,0:T(8,128)(2,1)S(1)}, bf16[512,768]{1,0:T(8,128)(2,1)S(1)}, u32[]{:S(2)}, u32[]{:S(2)}) collective-permute-start(bf16[512,768]{1,0:T(8,128)(2,1)S(1)} %get-tuple-element.117.grad_a.grad_b.hg_a), channel_id=1, source_target_pairs={{4,0},{5,1},{6,2},{7,3},{8,4},{9,5},{10,6},{11,7},{12,8},{13,9},{1... | collective-permute-start | bytes 2359304 | tf_op jit(solution)/shard_map/ppermute | solution.py:256
  138.4 4.2 %shard_map.87 = (f32[2,4,96,768]{3,2,1,0:T(8,128)S(1)}, bf16[2,4,96,768]{3,2,1,0:T(8,128)(2,1)S(1)}) custom-call(s32[4]{0:T(128)S(1)} %pad_add_fusion.place, bf16[1536,1024]{1,0:T(8,128)(2,1)S(1)} %shard_map.86.turned, bf16[512,768]{1,0:T(8,128)(2,1)S(1)} %get-tuple-element.117.grad_a.grad_b.hg_a, bf16[512,768]{1,0:T(8,128)(2,1)S(1)} %get-tuple-element.109.grad_b.grad_a.hg_b), custom_call_target="tpu_custom_call" | custom-call | flops 1 | bytes 1 | tf_op jit(solution)/shard_map/pallas_call | solution.py:108
  142.7 6.5 %collective-permute-done.27.grad_a.hg_prev = bf16[512,768]{1,0:T(8,128)(2,1)S(1)} collective-permute-done((bf16[512,768]{1,0:T(8,128)(2,1)S(1)}, bf16[512,768]{1,0:T(8,128)(2,1)S(1)}, u32[]{:S(2)}, u32[]{:S(2)}) %collective-permute-start.27) | collective-permute-done | bytes 786464 | tf_op jit(solution)/shard_map/ppermute | solution.py:253
  151.1 4.9 %shard_map.88 = (f32[2,4,96,768]{3,2,1,0:T(8,128)S(1)}, bf16[2,4,96,768]{3,2,1,0:T(8,128)(2,1)}) custom-call(s32[4]{0:T(128)S(1)} %pad_add_fusion.place, bf16[1536,1024]{1,0:T(8,128)(2,1)S(1)} %shard_map.86.turned, bf16[512,768]{1,0:T(8,128)(2,1)S(1)} %get-tuple-element.109.grad_b.grad_a.hg_b, bf16[512,768]{1,0:T(8,128)(2,1)S(1)} %collective-permute-done.26.grad_b.hg_next), custom_call_target="tpu_custom_call" | custom-call | flops 10000000000 | bytes 1 | tf_op jit(solution)/shard_map/pallas_call | solution.py:108
  157.1 4.3 %shard_map.90 = (f32[2,4,96,768]{3,2,1,0:T(8,128)S(1)}, bf16[2,4,96,768]{3,2,1,0:T(8,128)(2,1)S(1)}) custom-call(s32[4]{0:T(128)S(1)} %pad_add_fusion.place, bf16[1536,1024]{1,0:T(8,128)(2,1)S(1)} %shard_map.86.turned, bf16[512,768]{1,0:T(8,128)(2,1)S(1)} %collective-permute-done.27.grad_a.hg_prev, bf16[512,768]{1,0:T(8,128)(2,1)S(1)} %get-tuple-element.117.grad_a.grad_b.hg_a), custom_call_target="tpu_custom_call" | custom-call | flops 1 | bytes 1 | tf_op jit(solution)/shard_map/pallas_call | solution.py:108
  164.2 3.2 %collective-permute-start.34 = (bf16[96,768]{1,0:T(8,128)(2,1)S(1)}, bf16[96,768]{1,0:T(8,128)(2,1)S(1)}, u32[]{:S(2)}, u32[]{:S(2)}) collective-permute-start(bf16[96,768]{1,0:T(8,128)(2,1)S(1)} %get-tuple-element.129), channel_id=1, source_target_pairs={{0,8},{1,9},{2,10},{3,11},{4,12},{5,13},{6,14},{7,15},{8,0},{9,1},... | collective-permute-start | bytes 442376 | tf_op jit(solution)/shard_map/ppermute | solution.py:250
  171.3 7.0 %shard_map.93 = (bf16[512,768]{1,0:T(8,128)(2,1)S(1)}, bf16[512,768]{1,0:T(8,128)(2,1)S(1)}) custom-call(s32[4]{0:T(128)S(1)} %pad_add_fusion.place, bf16[512,768]{1,0:T(8,128)(2,1)S(1)} %collective-permute-done.26.grad_b.hg_next, bf16[512,768]{1,0:T(8,128)(2,1)S(1)} %get-tuple-element.109.grad_b.grad_a.hg_b, ...), custom_call_target="tpu_custom_call" | custom-call | flops 1 | bytes 1 | tf_op jit(solution)/shard_map/pallas_call | solution.py:108
  180.2 7.3 %collective-permute-done.35 = bf16[96,768]{1,0:T(8,128)(2,1)S(1)} collective-permute-done((bf16[96,768]{1,0:T(8,128)(2,1)S(1)}, bf16[96,768]{1,0:T(8,128)(2,1)S(1)}, u32[]{:S(2)}, u32[]{:S(2)}) %collective-permute-start.35) | collective-permute-done | bytes 147488 | tf_op jit(solution)/shard_map/ppermute | solution.py:250
  191.6 5.0 %collective-permute-done.38 = bf16[96,768]{1,0:T(8,128)(2,1)S(1)} collective-permute-done((bf16[96,768]{1,0:T(8,128)(2,1)S(1)}, bf16[96,768]{1,0:T(8,128)(2,1)S(1)}, u32[]{:S(2)}, u32[]{:S(2)}) %collective-permute-start.38) | collective-permute-done | bytes 147488 | tf_op jit(solution)/shard_map/ppermute | solution.py:250
  196.6 7.1 %shard_map.97 = (bf16[512,768]{1,0:T(8,128)(2,1)S(1)}, bf16[512,768]{1,0:T(8,128)(2,1)S(1)}) custom-call(s32[4]{0:T(128)S(1)} %pad_add_fusion.place, bf16[512,768]{1,0:T(8,128)(2,1)S(1)} %collective-permute-done.26.grad_b.hg_next, bf16[512,768]{1,0:T(8,128)(2,1)S(1)} %get-tuple-element.109.grad_b.grad_a.hg_b, ...), custom_call_target="tpu_custom_call" | custom-call | flops 1 | bytes 1 | tf_op jit(solution)/shard_map/pallas_call | solution.py:108
  210.0 5.6 %shard_map.94 = bf16[2,512,1536]{2,1,0:T(8,128)(2,1)} custom-call(s32[4]{0:T(128)S(1)} %pad_add_fusion.place, bf16[2,512,768]{2,1,0:T(8,128)(2,1)S(1)} %get-tuple-element.93.gated, bf16[512,768]{1,0:T(8,128)(2,1)S(1)} %collective-permute-done.19.got, bf16[1536,768]{1,0:T(8,128)(2,1)S(1)} %bitcast.71, bf16[2,512,1536]{2,1,0:T(8,128)(2,1)S(1)} %copy-done), custom_call_target="tpu_custom_call" | custom-call | flops 1 | bytes 1 | tf_op jit(solution)/shard_map/pallas_call | solution.py:108
  217.3 3.9 %collective-permute-done.44 = bf16[96,768]{1,0:T(8,128)(2,1)S(1)} collective-permute-done((bf16[96,768]{1,0:T(8,128)(2,1)S(1)}, bf16[96,768]{1,0:T(8,128)(2,1)S(1)}, u32[]{:S(2)}, u32[]{:S(2)}) %collective-permute-start.44) | collective-permute-done | bytes 147488 | tf_op jit(solution)/shard_map/ppermute | solution.py:250
  227.1 3.2 %collective-permute-done.47 = bf16[96,768]{1,0:T(8,128)(2,1)S(1)} collective-permute-done((bf16[96,768]{1,0:T(8,128)(2,1)S(1)}, bf16[96,768]{1,0:T(8,128)(2,1)S(1)}, u32[]{:S(2)}, u32[]{:S(2)}) %collective-permute-start.47) | collective-permute-done | bytes 147488 | tf_op jit(solution)/shard_map/ppermute | solution.py:250
  230.3 4.9 %collective-permute-done.48 = bf16[96,768]{1,0:T(8,128)(2,1)S(1)} collective-permute-done((bf16[96,768]{1,0:T(8,128)(2,1)S(1)}, bf16[96,768]{1,0:T(8,128)(2,1)S(1)}, u32[]{:S(2)}, u32[]{:S(2)}) %collective-permute-start.48) | collective-permute-done | bytes 147488 | tf_op jit(solution)/shard_map/ppermute | solution.py:250
  235.2 3.7 %collective-permute-done.49 = bf16[96,768]{1,0:T(8,128)(2,1)S(1)} collective-permute-done((bf16[96,768]{1,0:T(8,128)(2,1)S(1)}, bf16[96,768]{1,0:T(8,128)(2,1)S(1)}, u32[]{:S(2)}, u32[]{:S(2)}) %collective-permute-start.49) | collective-permute-done | bytes 147488 | tf_op jit(solution)/shard_map/ppermute | solution.py:250
  (139 shorter events, 86.3 us)
Async XLA Ops:
  13.1 13.2 %collective-permute-start.4 = (bf16[2,48,768]{2,1,0:T(8,128)(2,1)S(1)}, bf16[2,48,768]{2,1,0:T(8,128)(2,1)S(1)}, u32[]{:S(2)}, u32[]{:S(2)}) collective-permute-start(bf16[2,48,768]{2,1,0:T(8,128)(2,1)S(1)} %get-tuple-element.179), channel_id=1, source_target_pairs={{0,12},{1,13},{2,14},{3,15},{4,8},{5,9},{6,10},{7,11},{8,4},{9,5},... | collective-permute-start | bytes 442376 | tf_op jit(solution)/shard_map/ppermute | solution.py:250
  17.4 41.4 %collective-permute-start.1 = (bf16[512,1536]{1,0:T(8,128)(2,1)}, bf16[512,1536]{1,0:T(8,128)(2,1)S(1)}, u32[]{:S(2)}, u32[]{:S(2)}) collective-permute-start(bf16[512,1536]{1,0:T(8,128)(2,1)} %dynamic-slice_bitcast_fusion.1), channel_id=1, source_target_pairs={{0,2},{1,3},{2,0},{3,1},{4,6},{5,7},{6,4},{7,5},{8,10},{9,11},{10,... | collective-permute-start | bytes 4718600 | tf_op jit(solution)/shard_map/ppermute | solution.py:250
  26.4 14.8 %collective-permute-start.8 = (bf16[4,2,48,768]{3,2,1,0:T(8,128)(2,1)S(1)}, bf16[4,2,48,768]{3,2,1,0:T(8,128)(2,1)S(1)}, u32[]{:S(2)}, u32[]{:S(2)}) collective-permute-start(bf16[4,2,48,768]{3,2,1,0:T(8,128)(2,1)S(1)} %get-tuple-element.169), channel_id=1, source_target_pairs={{0,16},{16,0},{1,17},{17,1},{2,18},{18,2},{3,19},{19,3},{4,20},{20... | collective-permute-start | bytes 1769480 | tf_op jit(solution)/shard_map/ppermute | solution.py:277
  41.4 14.6 %collective-permute-start.9 = (bf16[4,2,48,768]{3,2,1,0:T(8,128)(2,1)S(1)}, bf16[4,2,48,768]{3,2,1,0:T(8,128)(2,1)}, u32[]{:S(2)}, u32[]{:S(2)}) collective-permute-start(bf16[4,2,48,768]{3,2,1,0:T(8,128)(2,1)S(1)} %pad_maximum_fusion.8), channel_id=1, source_target_pairs={{0,16},{16,0},{1,17},{17,1},{2,18},{18,2},{3,19},{19,3},{4,20},{20... | collective-permute-start | bytes 1769480 | tf_op jit(solution)/shard_map/ppermute | solution.py:277
  43.2 11.5 %collective-permute-start.12 = (bf16[2,48,768]{2,1,0:T(8,128)(2,1)S(1)}, bf16[2,48,768]{2,1,0:T(8,128)(2,1)}, u32[]{:S(2)}, u32[]{:S(2)}) collective-permute-start(bf16[2,48,768]{2,1,0:T(8,128)(2,1)S(1)} %pad_maximum_fusion.13), channel_id=1, source_target_pairs={{0,8},{1,9},{2,10},{3,11},{4,12},{5,13},{6,14},{7,15},{8,0},{9,1},... | collective-permute-start | bytes 442376 | tf_op jit(solution)/shard_map/ppermute | solution.py:250
  57.1 15.8 %collective-permute-start.15 = (bf16[4,2,48,768]{3,2,1,0:T(8,128)(2,1)S(1)}, bf16[4,2,48,768]{3,2,1,0:T(8,128)(2,1)S(1)}, u32[]{:S(2)}, u32[]{:S(2)}) collective-permute-start(bf16[4,2,48,768]{3,2,1,0:T(8,128)(2,1)S(1)} %pad_maximum_fusion.9), channel_id=1, source_target_pairs={{0,16},{16,0},{1,17},{17,1},{2,18},{18,2},{3,19},{19,3},{4,20},{20... | collective-permute-start | bytes 1769480 | tf_op jit(solution)/shard_map/ppermute | solution.py:277
  58.7 36.8 %collective-permute-start.20 = (bf16[512,1536]{1,0:T(8,128)(2,1)}, bf16[512,1536]{1,0:T(8,128)(2,1)}, u32[]{:S(2)}, u32[]{:S(2)}) collective-permute-start(bf16[512,1536]{1,0:T(8,128)(2,1)} %dynamic-slice_bitcast_fusion), channel_id=1, source_target_pairs={{0,2},{1,3},{2,0},{3,1},{4,6},{5,7},{6,4},{7,5},{8,10},{9,11},{10,... | collective-permute-start | bytes 4718600 | tf_op jit(solution)/shard_map/ppermute | solution.py:250
  73.2 16.3 %collective-permute-start.23 = (bf16[2,48,768]{2,1,0:T(8,128)(2,1)S(1)}, bf16[2,48,768]{2,1,0:T(8,128)(2,1)S(1)}, u32[]{:S(2)}, u32[]{:S(2)}) collective-permute-start(bf16[2,48,768]{2,1,0:T(8,128)(2,1)S(1)} %pad_maximum_fusion.14), channel_id=1, source_target_pairs={{0,12},{1,13},{2,14},{3,15},{4,8},{5,9},{6,10},{7,11},{8,4},{9,5},... | collective-permute-start | bytes 442376 | tf_op jit(solution)/shard_map/ppermute | solution.py:250
  73.8 18.1 %collective-permute-start.22 = (bf16[2,48,768]{2,1,0:T(8,128)(2,1)S(1)}, bf16[2,48,768]{2,1,0:T(8,128)(2,1)S(1)}, u32[]{:S(2)}, u32[]{:S(2)}) collective-permute-start(bf16[2,48,768]{2,1,0:T(8,128)(2,1)S(1)} %pad_maximum_fusion.14), channel_id=1, source_target_pairs={{0,8},{1,9},{2,10},{3,11},{4,12},{5,13},{6,14},{7,15},{8,0},{9,1},... | collective-permute-start | bytes 442376 | tf_op jit(solution)/shard_map/ppermute | solution.py:250
  76.9 15.0 %collective-permute-start.21 = (bf16[2,48,768]{2,1,0:T(8,128)(2,1)S(1)}, bf16[2,48,768]{2,1,0:T(8,128)(2,1)S(1)}, u32[]{:S(2)}, u32[]{:S(2)}) collective-permute-start(bf16[2,48,768]{2,1,0:T(8,128)(2,1)S(1)} %pad_maximum_fusion.14), channel_id=1, source_target_pairs={{0,4},{1,5},{2,6},{3,7},{4,0},{5,1},{6,2},{7,3},{8,12},{9,13},{10,... | collective-permute-start | bytes 442376 | tf_op jit(solution)/shard_map/ppermute | solution.py:250
  81.3 25.2 %collective-permute-start.17 = (bf16[512,768]{1,0:T(8,128)(2,1)S(1)}, bf16[512,768]{1,0:T(8,128)(2,1)S(1)}, u32[]{:S(2)}, u32[]{:S(2)}) collective-permute-start(bf16[512,768]{1,0:T(8,128)(2,1)S(1)} %get-tuple-element.83), channel_id=1, source_target_pairs={{0,4},{1,5},{2,6},{3,7},{4,8},{5,9},{6,10},{7,11},{8,12},{9,13},{1... | collective-permute-start | bytes 2359304 | tf_op jit(solution)/shard_map/ppermute | solution.py:253
  89.4 20.7 %collective-permute-start.18 = (bf16[512,768]{1,0:T(8,128)(2,1)S(1)}, bf16[512,768]{1,0:T(8,128)(2,1)S(1)}, u32[]{:S(2)}, u32[]{:S(2)}) collective-permute-start(bf16[512,768]{1,0:T(8,128)(2,1)S(1)} %get-tuple-element.92), channel_id=1, source_target_pairs={{4,0},{5,1},{6,2},{7,3},{8,4},{9,5},{10,6},{11,7},{12,8},{13,9},{1... | collective-permute-start | bytes 2359304 | tf_op jit(solution)/shard_map/ppermute | solution.py:256
  92.0 14.4 %collective-permute-start.24 = (bf16[4,2,48,768]{3,2,1,0:T(8,128)(2,1)S(1)}, bf16[4,2,48,768]{3,2,1,0:T(8,128)(2,1)S(1)}, u32[]{:S(2)}, u32[]{:S(2)}) collective-permute-start(bf16[4,2,48,768]{3,2,1,0:T(8,128)(2,1)S(1)} %pad_maximum_fusion.10), channel_id=1, source_target_pairs={{0,16},{16,0},{1,17},{17,1},{2,18},{18,2},{3,19},{19,3},{4,20},{20... | collective-permute-start | bytes 1769480 | tf_op jit(solution)/shard_map/ppermute | solution.py:277
  113.8 20.0 %collective-permute-start.19 = (bf16[512,768]{1,0:T(8,128)(2,1)S(1)}, bf16[512,768]{1,0:T(8,128)(2,1)S(1)}, u32[]{:S(2)}, u32[]{:S(2)}) collective-permute-start(bf16[512,768]{1,0:T(8,128)(2,1)S(1)} %get-tuple-element.94), channel_id=1, source_target_pairs={{0,2},{1,3},{2,0},{3,1},{4,6},{5,7},{6,4},{7,5},{8,10},{9,11},{10,... | collective-permute-start | bytes 2359304 | tf_op jit(solution)/shard_map/ppermute | solution.py:250
  120.1 13.7 %collective-permute-start.28 = (bf16[2,4,96,768]{3,2,1,0:T(8,128)(2,1)S(1)}, bf16[2,4,96,768]{3,2,1,0:T(8,128)(2,1)S(1)}, u32[]{:S(2)}, u32[]{:S(2)}) collective-permute-start(bf16[2,4,96,768]{3,2,1,0:T(8,128)(2,1)S(1)} %get-tuple-element.106), channel_id=1, source_target_pairs={{0,1},{1,0},{2,3},{3,2},{4,5},{5,4},{6,7},{7,6},{8,9},{9,8},{10,11... | collective-permute-start | bytes 3538952 | tf_op jit(solution)/shard_map/ppermute | solution.py:250
  127.4 21.8 %collective-permute-start.27 = (bf16[512,768]{1,0:T(8,128)(2,1)S(1)}, bf16[512,768]{1,0:T(8,128)(2,1)S(1)}, u32[]{:S(2)}, u32[]{:S(2)}) collective-permute-start(bf16[512,768]{1,0:T(8,128)(2,1)S(1)} %get-tuple-element.109.grad_b.grad_a.hg_b), channel_id=1, source_target_pairs={{0,4},{1,5},{2,6},{3,7},{4,8},{5,9},{6,10},{7,11},{8,12},{9,13},{1... | collective-permute-start | bytes 2359304 | tf_op jit(solution)/shard_map/ppermute | solution.py:253
  129.3 21.8 %collective-permute-start.26 = (bf16[512,768]{1,0:T(8,128)(2,1)S(1)}, bf16[512,768]{1,0:T(8,128)(2,1)S(1)}, u32[]{:S(2)}, u32[]{:S(2)}) collective-permute-start(bf16[512,768]{1,0:T(8,128)(2,1)S(1)} %get-tuple-element.117.grad_a.grad_b.hg_a), channel_id=1, source_target_pairs={{4,0},{5,1},{6,2},{7,3},{8,4},{9,5},{10,6},{11,7},{12,8},{13,9},{1... | collective-permute-start | bytes 2359304 | tf_op jit(solution)/shard_map/ppermute | solution.py:256
  136.8 19.2 %collective-permute-start.29 = (bf16[4,96,768]{2,1,0:T(8,128)(2,1)S(1)}, bf16[4,96,768]{2,1,0:T(8,128)(2,1)S(1)}, u32[]{:S(2)}, u32[]{:S(2)}) collective-permute-start(bf16[4,96,768]{2,1,0:T(8,128)(2,1)S(1)} %get-tuple-element.113), channel_id=1, source_target_pairs={{0,2},{1,3},{2,0},{3,1},{4,6},{5,7},{6,4},{7,5},{8,10},{9,11},{10,... | collective-permute-start | bytes 1769480 | tf_op jit(solution)/shard_map/ppermute | solution.py:250
  142.6 13.4 %collective-permute-start.30 = (bf16[2,4,96,768]{3,2,1,0:T(8,128)(2,1)S(1)}, bf16[2,4,96,768]{3,2,1,0:T(8,128)(2,1)S(1)}, u32[]{:S(2)}, u32[]{:S(2)}) collective-permute-start(bf16[2,4,96,768]{3,2,1,0:T(8,128)(2,1)S(1)} %get-tuple-element.115), channel_id=1, source_target_pairs={{0,1},{1,0},{2,3},{3,2},{4,5},{5,4},{6,7},{7,6},{8,9},{9,8},{10,11... | collective-permute-start | bytes 3538952 | tf_op jit(solution)/shard_map/ppermute | solution.py:250
  161.4 26.8 %collective-permute-start.37 = (bf16[2,4,96,768]{3,2,1,0:T(8,128)(2,1)S(1)}, bf16[2,4,96,768]{3,2,1,0:T(8,128)(2,1)S(1)}, u32[]{:S(2)}, u32[]{:S(2)}) collective-permute-start(bf16[2,4,96,768]{3,2,1,0:T(8,128)(2,1)S(1)} %get-tuple-element.135), channel_id=1, source_target_pairs={{0,1},{1,0},{2,3},{3,2},{4,5},{5,4},{6,7},{7,6},{8,9},{9,8},{10,11... | collective-permute-start | bytes 3538952 | tf_op jit(solution)/shard_map/ppermute | solution.py:250
  161.9 25.6 %collective-permute-start.36 = (bf16[4,96,768]{2,1,0:T(8,128)(2,1)S(1)}, bf16[4,96,768]{2,1,0:T(8,128)(2,1)S(1)}, u32[]{:S(2)}, u32[]{:S(2)}) collective-permute-start(bf16[4,96,768]{2,1,0:T(8,128)(2,1)S(1)} %get-tuple-element.132), channel_id=1, source_target_pairs={{0,2},{1,3},{2,0},{3,1},{4,6},{5,7},{6,4},{7,5},{8,10},{9,11},{10,... | collective-permute-start | bytes 1769480 | tf_op jit(solution)/shard_map/ppermute | solution.py:250
  164.1 14.3 %collective-permute-start.33 = (bf16[96,768]{1,0:T(8,128)(2,1)S(1)}, bf16[96,768]{1,0:T(8,128)(2,1)S(1)}, u32[]{:S(2)}, u32[]{:S(2)}) collective-permute-start(bf16[96,768]{1,0:T(8,128)(2,1)S(1)} %get-tuple-element.128), channel_id=1, source_target_pairs={{0,4},{1,5},{2,6},{3,7},{4,0},{5,1},{6,2},{7,3},{8,12},{9,13},{10,... | collective-permute-start | bytes 442376 | tf_op jit(solution)/shard_map/ppermute | solution.py:250
  164.2 15.7 %collective-permute-start.34 = (bf16[96,768]{1,0:T(8,128)(2,1)S(1)}, bf16[96,768]{1,0:T(8,128)(2,1)S(1)}, u32[]{:S(2)}, u32[]{:S(2)}) collective-permute-start(bf16[96,768]{1,0:T(8,128)(2,1)S(1)} %get-tuple-element.129), channel_id=1, source_target_pairs={{0,8},{1,9},{2,10},{3,11},{4,12},{5,13},{6,14},{7,15},{8,0},{9,1},... | collective-permute-start | bytes 442376 | tf_op jit(solution)/shard_map/ppermute | solution.py:250
  170.7 34.3 %collective-permute-start.41 = (bf16[4,96,768]{2,1,0:T(8,128)(2,1)S(1)}, bf16[4,96,768]{2,1,0:T(8,128)(2,1)S(1)}, u32[]{:S(2)}, u32[]{:S(2)}) collective-permute-start(bf16[4,96,768]{2,1,0:T(8,128)(2,1)S(1)} %get-tuple-element.144), channel_id=1, source_target_pairs={{0,2},{1,3},{2,0},{3,1},{4,6},{5,7},{6,4},{7,5},{8,10},{9,11},{10,... | collective-permute-start | bytes 1769480 | tf_op jit(solution)/shard_map/ppermute | solution.py:250
  178.3 31.7 %collective-permute-start.32 = (bf16[512,768]{1,0:T(8,128)(2,1)S(1)}, bf16[512,768]{1,0:T(8,128)(2,1)S(1)}, u32[]{:S(2)}, u32[]{:S(2)}) collective-permute-start(bf16[512,768]{1,0:T(8,128)(2,1)S(1)} %get-tuple-element.125), channel_id=1, source_target_pairs={{0,2},{1,3},{2,0},{3,1},{4,6},{5,7},{6,4},{7,5},{8,10},{9,11},{10,... | collective-permute-start | bytes 2359304 | tf_op jit(solution)/shard_map/ppermute | solution.py:250
  189.3 32.0 %collective-permute-start.45 = (bf16[4,96,768]{2,1,0:T(8,128)(2,1)S(1)}, bf16[4,96,768]{2,1,0:T(8,128)(2,1)S(1)}, u32[]{:S(2)}, u32[]{:S(2)}) collective-permute-start(bf16[4,96,768]{2,1,0:T(8,128)(2,1)S(1)} %get-tuple-element.150), channel_id=1, source_target_pairs={{0,2},{1,3},{2,0},{3,1},{4,6},{5,7},{6,4},{7,5},{8,10},{9,11},{10,... | collective-permute-start | bytes 1769480 | tf_op jit(solution)/shard_map/ppermute | solution.py:250
  189.9 13.8 %collective-permute-start.39 = (bf16[96,768]{1,0:T(8,128)(2,1)S(1)}, bf16[96,768]{1,0:T(8,128)(2,1)S(1)}, u32[]{:S(2)}, u32[]{:S(2)}) collective-permute-start(bf16[96,768]{1,0:T(8,128)(2,1)S(1)} %get-tuple-element.141), channel_id=1, source_target_pairs={{0,8},{1,9},{2,10},{3,11},{4,12},{5,13},{6,14},{7,15},{8,0},{9,1},... | collective-permute-start | bytes 442376 | tf_op jit(solution)/shard_map/ppermute | solution.py:250
  205.8 11.5 %collective-permute-start.43 = (bf16[96,768]{1,0:T(8,128)(2,1)S(1)}, bf16[96,768]{1,0:T(8,128)(2,1)S(1)}, u32[]{:S(2)}, u32[]{:S(2)}) collective-permute-start(bf16[96,768]{1,0:T(8,128)(2,1)S(1)} %get-tuple-element.147), channel_id=1, source_target_pairs={{0,8},{1,9},{2,10},{3,11},{4,12},{5,13},{6,14},{7,15},{8,0},{9,1},... | collective-permute-start | bytes 442376 | tf_op jit(solution)/shard_map/ppermute | solution.py:250
  207.9 13.3 %collective-permute-start.44 = (bf16[96,768]{1,0:T(8,128)(2,1)S(1)}, bf16[96,768]{1,0:T(8,128)(2,1)S(1)}, u32[]{:S(2)}, u32[]{:S(2)}) collective-permute-start(bf16[96,768]{1,0:T(8,128)(2,1)S(1)} %get-tuple-element.148), channel_id=1, source_target_pairs={{0,12},{1,13},{2,14},{3,15},{4,8},{5,9},{6,10},{7,11},{8,4},{9,5},... | collective-permute-start | bytes 442376 | tf_op jit(solution)/shard_map/ppermute | solution.py:250
  221.9 18.9 %collective-permute-start.46 = (bf16[512,768]{1,0:T(8,128)(2,1)S(1)}, bf16[512,768]{1,0:T(8,128)(2,1)S(1)}, u32[]{:S(2)}, u32[]{:S(2)}) collective-permute-start(bf16[512,768]{1,0:T(8,128)(2,1)S(1)} %get-tuple-element.152), channel_id=1, source_target_pairs={{0,2},{1,3},{2,0},{3,1},{4,6},{5,7},{6,4},{7,5},{8,10},{9,11},{10,... | collective-permute-start | bytes 2359304 | tf_op jit(solution)/shard_map/ppermute | solution.py:250
  223.6 11.6 %collective-permute-start.48 = (bf16[96,768]{1,0:T(8,128)(2,1)S(1)}, bf16[96,768]{1,0:T(8,128)(2,1)S(1)}, u32[]{:S(2)}, u32[]{:S(2)}) collective-permute-start(bf16[96,768]{1,0:T(8,128)(2,1)S(1)} %get-tuple-element.154), channel_id=1, source_target_pairs={{0,8},{1,9},{2,10},{3,11},{4,12},{5,13},{6,14},{7,15},{8,0},{9,1},... | collective-permute-start | bytes 442376 | tf_op jit(solution)/shard_map/ppermute | solution.py:250
  225.2 13.7 %collective-permute-start.49 = (bf16[96,768]{1,0:T(8,128)(2,1)S(1)}, bf16[96,768]{1,0:T(8,128)(2,1)S(1)}, u32[]{:S(2)}, u32[]{:S(2)}) collective-permute-start(bf16[96,768]{1,0:T(8,128)(2,1)S(1)} %get-tuple-element.155), channel_id=1, source_target_pairs={{0,12},{1,13},{2,14},{3,15},{4,8},{5,9},{6,10},{7,11},{8,4},{9,5},... | collective-permute-start | bytes 442376 | tf_op jit(solution)/shard_map/ppermute | solution.py:250
  (27 other events, 202.5 us)

commit v6 on v5

--- a/solution.py
+++ b/solution.py
@@ -382,7 +382,7 @@
     hg_a, hg_b = call(
         hidden_grad_kernel,
         [((local_len, hid), bf16)] * 2,
-        place, hidden, cot_a, cot_b, after(wp, term_p[0]),
+        place, hidden, cot_a, cot_b, wp,
         grid=(hid // tile,),
         ins=[block((2, local_len, tile), 0, 0, 1)]
         + [RESIDENT] * 2

time: 245 us -> 245 us (level)
  no operation moved by 1% of the time
where the time goes in v6:
time: 245 us; the launch traced here: 243 us
  waiting for transfers between devices  89.8 us (37%)
  Pallas kernels  69.9 us (29%)
  starting transfers between devices  61.3 us (25%)
  other arithmetic  12.9 us (5%)
  local copies, waits for them, and re-layouts  8.25 us (3%)
    pallas_call x25, Pallas kernels, call(): pl.pallas_call(kernel, grid=grid, out_shape=outs, in_specs=[pl.BlockSpec(...  69.9 us
    ppermute x42, waiting for transfers between devices, swap(): return lax.ppermute(value, 'seq', [(i, i ^ bits) for i in everyone])  60.8 us
    ppermute x42, starting transfers between devices, swap(): return lax.ppermute(value, 'seq', [(i, i ^ bits) for i in everyone])  41.4 us
    ppermute x4, waiting for transfers between devices, over_y(): return jnp.stack([column, lax.ppermute(column, 'groups', [(0, 1), (1, 0)])])  17 us
    ppermute x4, starting transfers between devices, over_y(): return jnp.stack([column, lax.ppermute(column, 'groups', [(0, 1), (1, 0)])])  8.05 us
    ppermute x2, starting transfers between devices, down(): lax.ppermute(value, 'seq', [(i + 4, i) for i in everyone if i + 4 in ever...  6.55 us
    ppermute x2, waiting for transfers between devices, up(): lax.ppermute(value, 'seq', [(i, i + 4) for i in everyone if i + 4 in ever...  6.51 us
    ppermute x2, waiting for transfers between devices, down(): lax.ppermute(value, 'seq', [(i + 4, i) for i in everyone if i + 4 in ever...  5.56 us
  transfers between devices with their start and end apart: 50, of which 23 were waited for; matrix products, arithmetic and copies ran while one was open for 6% of the time, Pallas kernels for 28%

profile of v6, /device:TPU:16, one launch (start us, length us, event | category | flops | bytes accessed | tf_op | source)
XLA Modules:
  0.0 243.3 jit_solution(16459740427299381598)
XLA Ops:
  3.9 6.6 %collective-permute-done = bf16[4,48,768]{2,1,0:T(8,128)(2,1)S(1)} collective-permute-done((bf16[4,48,768]{2,1,0:T(8,128)(2,1)S(1)}, bf16[4,48,768]{2,1,0:T(8,128)(2,1)S(1)}, u32[]{:S(2)}, u32[]{:S(2)}) %collective-permute-start) | collective-permute-done | bytes 294944 | tf_op jit(solution)/shard_map/ppermute | solution.py:250
  14.7 2.7 %dynamic-slice_bitcast_fusion.1 = bf16[512,1536]{1,0:T(8,128)(2,1)} fusion(bf16[2,512,1536]{2,1,0:T(8,128)(2,1)} %inputs.1, s32[]{:T(128)S(6)} %select_n.80), kind=kLoop, calls=%fused_computation.28 | loop fusion | bytes 3145732 | tf_op jit(solution)/shard_map/jit(dynamic_index_in_dim)/squeeze | solution.py:259
  20.6 5.7 %collective-permute-done.4 = bf16[2,48,768]{2,1,0:T(8,128)(2,1)S(1)} collective-permute-done((bf16[2,48,768]{2,1,0:T(8,128)(2,1)S(1)}, bf16[2,48,768]{2,1,0:T(8,128)(2,1)S(1)}, u32[]{:S(2)}, u32[]{:S(2)}) %collective-permute-start.4) | collective-permute-done | bytes 147488 | tf_op jit(solution)/shard_map/ppermute | solution.py:250
  26.4 3.2 %collective-permute-start.8 = (bf16[4,2,48,768]{3,2,1,0:T(8,128)(2,1)S(1)}, bf16[4,2,48,768]{3,2,1,0:T(8,128)(2,1)S(1)}, u32[]{:S(2)}, u32[]{:S(2)}) collective-permute-start(bf16[4,2,48,768]{3,2,1,0:T(8,128)(2,1)S(1)} %get-tuple-element.167), channel_id=1, source_target_pairs={{0,16},{16,0},{1,17},{17,1},{2,18},{18,2},{3,19},{19,3},{4,20},{20... | collective-permute-start | bytes 1769480 | tf_op jit(solution)/shard_map/ppermute | solution.py:277
  29.8 3.4 %collective-permute-start.5 = (bf16[2,48,768]{2,1,0:T(8,128)(2,1)S(1)}, bf16[2,48,768]{2,1,0:T(8,128)(2,1)S(1)}, u32[]{:S(2)}, u32[]{:S(2)}) collective-permute-start(bf16[2,48,768]{2,1,0:T(8,128)(2,1)S(1)} %pad_maximum_fusion.11), channel_id=1, source_target_pairs={{0,4},{1,5},{2,6},{3,7},{4,0},{5,1},{6,2},{7,3},{8,12},{9,13},{10,... | collective-permute-start | bytes 442376 | tf_op jit(solution)/shard_map/ppermute | solution.py:250
  33.2 5.8 %collective-permute-done.7 = bf16[2,48,768]{2,1,0:T(8,128)(2,1)S(1)} collective-permute-done((bf16[2,48,768]{2,1,0:T(8,128)(2,1)S(1)}, bf16[2,48,768]{2,1,0:T(8,128)(2,1)S(1)}, u32[]{:S(2)}, u32[]{:S(2)}) %collective-permute-start.7) | collective-permute-done | bytes 147488 | tf_op jit(solution)/shard_map/ppermute | solution.py:250
  47.9 6.7 %collective-permute-done.13 = bf16[2,48,768]{2,1,0:T(8,128)(2,1)} collective-permute-done((bf16[2,48,768]{2,1,0:T(8,128)(2,1)S(1)}, bf16[2,48,768]{2,1,0:T(8,128)(2,1)}, u32[]{:S(2)}, u32[]{:S(2)}) %collective-permute-start.13) | collective-permute-done | bytes 147488 | tf_op jit(solution)/shard_map/ppermute | solution.py:250
  63.5 3.8 %shard_map.76 = (bf16[512,768]{1,0:T(8,128)(2,1)S(1)}, f32[512,768]{1,0:T(8,128)S(1)}) custom-call(s32[4]{0:T(128)S(1)} %pad_add_fusion.place, bf16[512,1536]{1,0:T(8,128)(2,1)S(1)} %get-tuple-element.106.rows_sent.rows_kept.act_b.rows_b, bf16[512,1536]{1,0:T(8,128)(2,1)S(1)} %get-tuple-element.160.rows_kept.rows_sent.act_a.rows_a, ...), custom_call_target="tpu_custom_call" | custom-call | flops 1 | bytes 1 | tf_op jit(solution)/shard_map/pallas_call | solution.py:108
  67.4 5.5 %collective-permute-done.15 = bf16[4,2,48,768]{3,2,1,0:T(8,128)(2,1)S(1)} collective-permute-done((bf16[4,2,48,768]{3,2,1,0:T(8,128)(2,1)S(1)}, bf16[4,2,48,768]{3,2,1,0:T(8,128)(2,1)S(1)}, u32[]{:S(2)}, u32[]{:S(2)}) %collective-permute-start.15) | collective-permute-done | bytes 589856 | tf_op jit(solution)/shard_map/ppermute | solution.py:277
  77.5 3.8 %shard_map.78 = (bf16[512,768]{1,0:T(8,128)(2,1)S(1)}, f32[512,768]{1,0:T(8,128)S(1)}) custom-call(s32[4]{0:T(128)S(1)} %pad_add_fusion.place, bf16[512,1536]{1,0:T(8,128)(2,1)S(1)} %get-tuple-element.160.rows_kept.rows_sent.act_a.rows_a, bf16[512,1536]{1,0:T(8,128)(2,1)S(1)} %get-tuple-element.106.rows_sent.rows_kept.act_b.rows_b, ...), custom_call_target="tpu_custom_call" | custom-call | flops 1 | bytes 1 | tf_op jit(solution)/shard_map/pallas_call | solution.py:108
  81.3 3.4 %collective-permute-start.17 = (bf16[512,768]{1,0:T(8,128)(2,1)S(1)}, bf16[512,768]{1,0:T(8,128)(2,1)S(1)}, u32[]{:S(2)}, u32[]{:S(2)}) collective-permute-start(bf16[512,768]{1,0:T(8,128)(2,1)S(1)} %get-tuple-element.82), channel_id=1, source_target_pairs={{0,4},{1,5},{2,6},{3,7},{4,8},{5,9},{6,10},{7,11},{8,12},{9,13},{1... | collective-permute-start | bytes 2359304 | tf_op jit(solution)/shard_map/ppermute | solution.py:253
  85.4 4.0 %shard_map.80 = (f32[512,768]{1,0:T(8,128)S(1)}, f32[512,768]{1,0:T(8,128)S(1)}) custom-call(s32[4]{0:T(128)S(1)} %pad_add_fusion.place, f32[512,768]{1,0:T(8,128)S(1)} %get-tuple-element.86.near_a, f32[512,768]{1,0:T(8,128)S(1)} %get-tuple-element.87.near_b, bf16[512,1536]{1,0:T(8,128)(2,1)S(1)} %get-tuple-element.160.rows_kept.rows_sent.act_a.rows_a, ...), custom_call_target="tpu_custom_call" | custom-call | flops 1 | bytes 1 | tf_op jit(solution)/shard_map/pallas_call | solution.py:108
  97.2 9.2 %collective-permute-done.24 = bf16[4,2,48,768]{3,2,1,0:T(8,128)(2,1)S(1)} collective-permute-done((bf16[4,2,48,768]{3,2,1,0:T(8,128)(2,1)S(1)}, bf16[4,2,48,768]{3,2,1,0:T(8,128)(2,1)S(1)}, u32[]{:S(2)}, u32[]{:S(2)}) %collective-permute-start.24) | collective-permute-done | bytes 589856 | tf_op jit(solution)/shard_map/ppermute | solution.py:277
  106.5 3.6 %collective-permute-done.18.from_next = bf16[512,768]{1,0:T(8,128)(2,1)S(1)} collective-permute-done((bf16[512,768]{1,0:T(8,128)(2,1)S(1)}, bf16[512,768]{1,0:T(8,128)(2,1)S(1)}, u32[]{:S(2)}, u32[]{:S(2)}) %collective-permute-start.18) | collective-permute-done | bytes 786464 | tf_op jit(solution)/shard_map/ppermute | solution.py:256
  110.1 3.6 %shard_map.81 = (f32[2,512,768]{2,1,0:T(8,128)S(1)}, bf16[2,512,768]{2,1,0:T(8,128)(2,1)S(1)}, bf16[512,768]{1,0:T(8,128)(2,1)S(1)}) custom-call(s32[4]{0:T(128)S(1)} %pad_add_fusion.place, f32[512,768]{1,0:T(8,128)S(1)} %get-tuple-element.89.near_a, f32[512,768]{1,0:T(8,128)S(1)} %get-tuple-element.90.near_b, ...), custom_call_target="tpu_custom_call" | custom-call | flops 1 | bytes 1 | tf_op jit(solution)/shard_map/pallas_call | solution.py:108
  115.5 4.7 %shard_map.84 = (f32[2,4,96,768]{3,2,1,0:T(8,128)S(1)}, bf16[2,4,96,768]{3,2,1,0:T(8,128)(2,1)S(1)}) custom-call(s32[4]{0:T(128)S(1)} %pad_add_fusion.place, bf16[512,1536]{1,0:T(8,128)(2,1)S(1)} %get-tuple-element.159.cot_a.rows_a, bf16[512,1536]{1,0:T(8,128)(2,1)S(1)} %get-tuple-element.158.cot_b.rows_b, bf16[512,768]{1,0:T(8,128)(2,1)S(1)} %get-tuple-element.165.grad_a, ...), custom_call_target="tpu_custom_call" | custom-call | flops 1 | bytes 1 | tf_op jit(solution)/shard_map/pallas_call | solution.py:108
  122.0 5.4 %shard_map.83 = (bf16[512,768]{1,0:T(8,128)(2,1)S(1)}, bf16[512,768]{1,0:T(8,128)(2,1)S(1)}) custom-call(s32[4]{0:T(128)S(1)} %pad_add_fusion.place, f32[2,512,768]{2,1,0:T(8,128)S(1)} %copy-done.4, bf16[512,1536]{1,0:T(8,128)(2,1)S(1)} %get-tuple-element.159.cot_a.rows_a, bf16[512,1536]{1,0:T(8,128)(2,1)S(1)} %get-tuple-element.158.cot_b.rows_b, ...), custom_call_target="tpu_custom_call" | custom-call | flops 10000000000 | bytes 1 | tf_op jit(solution)/shard_map/pallas_call | solution.py:108
  129.3 4.1 %collective-permute-start.26 = (bf16[512,768]{1,0:T(8,128)(2,1)S(1)}, bf16[512,768]{1,0:T(8,128)(2,1)S(1)}, u32[]{:S(2)}, u32[]{:S(2)}) collective-permute-start(bf16[512,768]{1,0:T(8,128)(2,1)S(1)} %get-tuple-element.115.grad_a.grad_b.hg_a), channel_id=1, source_target_pairs={{4,0},{5,1},{6,2},{7,3},{8,4},{9,5},{10,6},{11,7},{12,8},{13,9},{1... | collective-permute-start | bytes 2359304 | tf_op jit(solution)/shard_map/ppermute | solution.py:256
  138.4 4.2 %shard_map.87 = (f32[2,4,96,768]{3,2,1,0:T(8,128)S(1)}, bf16[2,4,96,768]{3,2,1,0:T(8,128)(2,1)S(1)}) custom-call(s32[4]{0:T(128)S(1)} %pad_add_fusion.place, bf16[1536,1024]{1,0:T(8,128)(2,1)S(1)} %shard_map.86.turned, bf16[512,768]{1,0:T(8,128)(2,1)S(1)} %get-tuple-element.115.grad_a.grad_b.hg_a, bf16[512,768]{1,0:T(8,128)(2,1)S(1)} %get-tuple-element.107.grad_b.grad_a.hg_b), custom_call_target="tpu_custom_call" | custom-call | flops 1 | bytes 1 | tf_op jit(solution)/shard_map/pallas_call | solution.py:108
  142.7 6.5 %collective-permute-done.27.grad_a.hg_prev = bf16[512,768]{1,0:T(8,128)(2,1)S(1)} collective-permute-done((bf16[512,768]{1,0:T(8,128)(2,1)S(1)}, bf16[512,768]{1,0:T(8,128)(2,1)S(1)}, u32[]{:S(2)}, u32[]{:S(2)}) %collective-permute-start.27) | collective-permute-done | bytes 786464 | tf_op jit(solution)/shard_map/ppermute | solution.py:253
  151.1 4.9 %shard_map.88 = (f32[2,4,96,768]{3,2,1,0:T(8,128)S(1)}, bf16[2,4,96,768]{3,2,1,0:T(8,128)(2,1)}) custom-call(s32[4]{0:T(128)S(1)} %pad_add_fusion.place, bf16[1536,1024]{1,0:T(8,128)(2,1)S(1)} %shard_map.86.turned, bf16[512,768]{1,0:T(8,128)(2,1)S(1)} %get-tuple-element.107.grad_b.grad_a.hg_b, bf16[512,768]{1,0:T(8,128)(2,1)S(1)} %collective-permute-done.26.grad_b.hg_next), custom_call_target="tpu_custom_call" | custom-call | flops 10000000000 | bytes 1 | tf_op jit(solution)/shard_map/pallas_call | solution.py:108
  157.1 4.3 %shard_map.90 = (f32[2,4,96,768]{3,2,1,0:T(8,128)S(1)}, bf16[2,4,96,768]{3,2,1,0:T(8,128)(2,1)S(1)}) custom-call(s32[4]{0:T(128)S(1)} %pad_add_fusion.place, bf16[1536,1024]{1,0:T(8,128)(2,1)S(1)} %shard_map.86.turned, bf16[512,768]{1,0:T(8,128)(2,1)S(1)} %collective-permute-done.27.grad_a.hg_prev, bf16[512,768]{1,0:T(8,128)(2,1)S(1)} %get-tuple-element.115.grad_a.grad_b.hg_a), custom_call_target="tpu_custom_call" | custom-call | flops 1 | bytes 1 | tf_op jit(solution)/shard_map/pallas_call | solution.py:108
  164.2 3.2 %collective-permute-start.34 = (bf16[96,768]{1,0:T(8,128)(2,1)S(1)}, bf16[96,768]{1,0:T(8,128)(2,1)S(1)}, u32[]{:S(2)}, u32[]{:S(2)}) collective-permute-start(bf16[96,768]{1,0:T(8,128)(2,1)S(1)} %get-tuple-element.127), channel_id=1, source_target_pairs={{0,8},{1,9},{2,10},{3,11},{4,12},{5,13},{6,14},{7,15},{8,0},{9,1},... | collective-permute-start | bytes 442376 | tf_op jit(solution)/shard_map/ppermute | solution.py:250
  171.3 7.0 %shard_map.93 = (bf16[512,768]{1,0:T(8,128)(2,1)S(1)}, bf16[512,768]{1,0:T(8,128)(2,1)S(1)}) custom-call(s32[4]{0:T(128)S(1)} %pad_add_fusion.place, bf16[512,768]{1,0:T(8,128)(2,1)S(1)} %collective-permute-done.26.grad_b.hg_next, bf16[512,768]{1,0:T(8,128)(2,1)S(1)} %get-tuple-element.107.grad_b.grad_a.hg_b, ...), custom_call_target="tpu_custom_call" | custom-call | flops 1 | bytes 1 | tf_op jit(solution)/shard_map/pallas_call | solution.py:108
  180.2 7.3 %collective-permute-done.35 = bf16[96,768]{1,0:T(8,128)(2,1)S(1)} collective-permute-done((bf16[96,768]{1,0:T(8,128)(2,1)S(1)}, bf16[96,768]{1,0:T(8,128)(2,1)S(1)}, u32[]{:S(2)}, u32[]{:S(2)}) %collective-permute-start.35) | collective-permute-done | bytes 147488 | tf_op jit(solution)/shard_map/ppermute | solution.py:250
  191.6 5.0 %collective-permute-done.38 = bf16[96,768]{1,0:T(8,128)(2,1)S(1)} collective-permute-done((bf16[96,768]{1,0:T(8,128)(2,1)S(1)}, bf16[96,768]{1,0:T(8,128)(2,1)S(1)}, u32[]{:S(2)}, u32[]{:S(2)}) %collective-permute-start.38) | collective-permute-done | bytes 147488 | tf_op jit(solution)/shard_map/ppermute | solution.py:250
  196.6 7.1 %shard_map.97 = (bf16[512,768]{1,0:T(8,128)(2,1)S(1)}, bf16[512,768]{1,0:T(8,128)(2,1)S(1)}) custom-call(s32[4]{0:T(128)S(1)} %pad_add_fusion.place, bf16[512,768]{1,0:T(8,128)(2,1)S(1)} %collective-permute-done.26.grad_b.hg_next, bf16[512,768]{1,0:T(8,128)(2,1)S(1)} %get-tuple-element.107.grad_b.grad_a.hg_b, ...), custom_call_target="tpu_custom_call" | custom-call | flops 1 | bytes 1 | tf_op jit(solution)/shard_map/pallas_call | solution.py:108
  210.0 5.6 %shard_map.94 = bf16[2,512,1536]{2,1,0:T(8,128)(2,1)} custom-call(s32[4]{0:T(128)S(1)} %pad_add_fusion.place, bf16[2,512,768]{2,1,0:T(8,128)(2,1)S(1)} %get-tuple-element.92.gated, bf16[512,768]{1,0:T(8,128)(2,1)S(1)} %collective-permute-done.19.got, bf16[1536,768]{1,0:T(8,128)(2,1)S(1)} %bitcast.71, bf16[2,512,1536]{2,1,0:T(8,128)(2,1)S(1)} %copy-done), custom_call_target="tpu_custom_call" | custom-call | flops 1 | bytes 1 | tf_op jit(solution)/shard_map/pallas_call | solution.py:108
  217.3 3.9 %collective-permute-done.44 = bf16[96,768]{1,0:T(8,128)(2,1)S(1)} collective-permute-done((bf16[96,768]{1,0:T(8,128)(2,1)S(1)}, bf16[96,768]{1,0:T(8,128)(2,1)S(1)}, u32[]{:S(2)}, u32[]{:S(2)}) %collective-permute-start.44) | collective-permute-done | bytes 147488 | tf_op jit(solution)/shard_map/ppermute | solution.py:250
  227.1 3.2 %collective-permute-done.47 = bf16[96,768]{1,0:T(8,128)(2,1)S(1)} collective-permute-done((bf16[96,768]{1,0:T(8,128)(2,1)S(1)}, bf16[96,768]{1,0:T(8,128)(2,1)S(1)}, u32[]{:S(2)}, u32[]{:S(2)}) %collective-permute-start.47) | collective-permute-done | bytes 147488 | tf_op jit(solution)/shard_map/ppermute | solution.py:250
  230.3 4.9 %collective-permute-done.48 = bf16[96,768]{1,0:T(8,128)(2,1)S(1)} collective-permute-done((bf16[96,768]{1,0:T(8,128)(2,1)S(1)}, bf16[96,768]{1,0:T(8,128)(2,1)S(1)}, u32[]{:S(2)}, u32[]{:S(2)}) %collective-permute-start.48) | collective-permute-done | bytes 147488 | tf_op jit(solution)/shard_map/ppermute | solution.py:250
  235.2 3.7 %collective-permute-done.49 = bf16[96,768]{1,0:T(8,128)(2,1)S(1)} collective-permute-done((bf16[96,768]{1,0:T(8,128)(2,1)S(1)}, bf16[96,768]{1,0:T(8,128)(2,1)S(1)}, u32[]{:S(2)}, u32[]{:S(2)}) %collective-permute-start.49) | collective-permute-done | bytes 147488 | tf_op jit(solution)/shard_map/ppermute | solution.py:250
  (139 shorter events, 86.3 us)
Async XLA Ops:
  13.1 13.2 %collective-permute-start.4 = (bf16[2,48,768]{2,1,0:T(8,128)(2,1)S(1)}, bf16[2,48,768]{2,1,0:T(8,128)(2,1)S(1)}, u32[]{:S(2)}, u32[]{:S(2)}) collective-permute-start(bf16[2,48,768]{2,1,0:T(8,128)(2,1)S(1)} %get-tuple-element.177), channel_id=1, source_target_pairs={{0,12},{1,13},{2,14},{3,15},{4,8},{5,9},{6,10},{7,11},{8,4},{9,5},... | collective-permute-start | bytes 442376 | tf_op jit(solution)/shard_map/ppermute | solution.py:250
  17.4 41.4 %collective-permute-start.1 = (bf16[512,1536]{1,0:T(8,128)(2,1)}, bf16[512,1536]{1,0:T(8,128)(2,1)S(1)}, u32[]{:S(2)}, u32[]{:S(2)}) collective-permute-start(bf16[512,1536]{1,0:T(8,128)(2,1)} %dynamic-slice_bitcast_fusion.1), channel_id=1, source_target_pairs={{0,2},{1,3},{2,0},{3,1},{4,6},{5,7},{6,4},{7,5},{8,10},{9,11},{10,... | collective-permute-start | bytes 4718600 | tf_op jit(solution)/shard_map/ppermute | solution.py:250
  26.4 14.8 %collective-permute-start.8 = (bf16[4,2,48,768]{3,2,1,0:T(8,128)(2,1)S(1)}, bf16[4,2,48,768]{3,2,1,0:T(8,128)(2,1)S(1)}, u32[]{:S(2)}, u32[]{:S(2)}) collective-permute-start(bf16[4,2,48,768]{3,2,1,0:T(8,128)(2,1)S(1)} %get-tuple-element.167), channel_id=1, source_target_pairs={{0,16},{16,0},{1,17},{17,1},{2,18},{18,2},{3,19},{19,3},{4,20},{20... | collective-permute-start | bytes 1769480 | tf_op jit(solution)/shard_map/ppermute | solution.py:277
  41.4 14.6 %collective-permute-start.9 = (bf16[4,2,48,768]{3,2,1,0:T(8,128)(2,1)S(1)}, bf16[4,2,48,768]{3,2,1,0:T(8,128)(2,1)}, u32[]{:S(2)}, u32[]{:S(2)}) collective-permute-start(bf16[4,2,48,768]{3,2,1,0:T(8,128)(2,1)S(1)} %pad_maximum_fusion.8), channel_id=1, source_target_pairs={{0,16},{16,0},{1,17},{17,1},{2,18},{18,2},{3,19},{19,3},{4,20},{20... | collective-permute-start | bytes 1769480 | tf_op jit(solution)/shard_map/ppermute | solution.py:277
  43.2 11.5 %collective-permute-start.12 = (bf16[2,48,768]{2,1,0:T(8,128)(2,1)S(1)}, bf16[2,48,768]{2,1,0:T(8,128)(2,1)}, u32[]{:S(2)}, u32[]{:S(2)}) collective-permute-start(bf16[2,48,768]{2,1,0:T(8,128)(2,1)S(1)} %pad_maximum_fusion.13), channel_id=1, source_target_pairs={{0,8},{1,9},{2,10},{3,11},{4,12},{5,13},{6,14},{7,15},{8,0},{9,1},... | collective-permute-start | bytes 442376 | tf_op jit(solution)/shard_map/ppermute | solution.py:250
  57.1 15.8 %collective-permute-start.15 = (bf16[4,2,48,768]{3,2,1,0:T(8,128)(2,1)S(1)}, bf16[4,2,48,768]{3,2,1,0:T(8,128)(2,1)S(1)}, u32[]{:S(2)}, u32[]{:S(2)}) collective-permute-start(bf16[4,2,48,768]{3,2,1,0:T(8,128)(2,1)S(1)} %pad_maximum_fusion.9), channel_id=1, source_target_pairs={{0,16},{16,0},{1,17},{17,1},{2,18},{18,2},{3,19},{19,3},{4,20},{20... | collective-permute-start | bytes 1769480 | tf_op jit(solution)/shard_map/ppermute | solution.py:277
  58.7 36.8 %collective-permute-start.20 = (bf16[512,1536]{1,0:T(8,128)(2,1)}, bf16[512,1536]{1,0:T(8,128)(2,1)}, u32[]{:S(2)}, u32[]{:S(2)}) collective-permute-start(bf16[512,1536]{1,0:T(8,128)(2,1)} %dynamic-slice_bitcast_fusion), channel_id=1, source_target_pairs={{0,2},{1,3},{2,0},{3,1},{4,6},{5,7},{6,4},{7,5},{8,10},{9,11},{10,... | collective-permute-start | bytes 4718600 | tf_op jit(solution)/shard_map/ppermute | solution.py:250
  73.2 16.3 %collective-permute-start.23 = (bf16[2,48,768]{2,1,0:T(8,128)(2,1)S(1)}, bf16[2,48,768]{2,1,0:T(8,128)(2,1)S(1)}, u32[]{:S(2)}, u32[]{:S(2)}) collective-permute-start(bf16[2,48,768]{2,1,0:T(8,128)(2,1)S(1)} %pad_maximum_fusion.14), channel_id=1, source_target_pairs={{0,12},{1,13},{2,14},{3,15},{4,8},{5,9},{6,10},{7,11},{8,4},{9,5},... | collective-permute-start | bytes 442376 | tf_op jit(solution)/shard_map/ppermute | solution.py:250
  73.8 18.1 %collective-permute-start.22 = (bf16[2,48,768]{2,1,0:T(8,128)(2,1)S(1)}, bf16[2,48,768]{2,1,0:T(8,128)(2,1)S(1)}, u32[]{:S(2)}, u32[]{:S(2)}) collective-permute-start(bf16[2,48,768]{2,1,0:T(8,128)(2,1)S(1)} %pad_maximum_fusion.14), channel_id=1, source_target_pairs={{0,8},{1,9},{2,10},{3,11},{4,12},{5,13},{6,14},{7,15},{8,0},{9,1},... | collective-permute-start | bytes 442376 | tf_op jit(solution)/shard_map/ppermute | solution.py:250
  76.9 15.0 %collective-permute-start.21 = (bf16[2,48,768]{2,1,0:T(8,128)(2,1)S(1)}, bf16[2,48,768]{2,1,0:T(8,128)(2,1)S(1)}, u32[]{:S(2)}, u32[]{:S(2)}) collective-permute-start(bf16[2,48,768]{2,1,0:T(8,128)(2,1)S(1)} %pad_maximum_fusion.14), channel_id=1, source_target_pairs={{0,4},{1,5},{2,6},{3,7},{4,0},{5,1},{6,2},{7,3},{8,12},{9,13},{10,... | collective-permute-start | bytes 442376 | tf_op jit(solution)/shard_map/ppermute | solution.py:250
  81.3 25.2 %collective-permute-start.17 = (bf16[512,768]{1,0:T(8,128)(2,1)S(1)}, bf16[512,768]{1,0:T(8,128)(2,1)S(1)}, u32[]{:S(2)}, u32[]{:S(2)}) collective-permute-start(bf16[512,768]{1,0:T(8,128)(2,1)S(1)} %get-tuple-element.82), channel_id=1, source_target_pairs={{0,4},{1,5},{2,6},{3,7},{4,8},{5,9},{6,10},{7,11},{8,12},{9,13},{1... | collective-permute-start | bytes 2359304 | tf_op jit(solution)/shard_map/ppermute | solution.py:253
  89.4 20.7 %collective-permute-start.18 = (bf16[512,768]{1,0:T(8,128)(2,1)S(1)}, bf16[512,768]{1,0:T(8,128)(2,1)S(1)}, u32[]{:S(2)}, u32[]{:S(2)}) collective-permute-start(bf16[512,768]{1,0:T(8,128)(2,1)S(1)} %get-tuple-element.91), channel_id=1, source_target_pairs={{4,0},{5,1},{6,2},{7,3},{8,4},{9,5},{10,6},{11,7},{12,8},{13,9},{1... | collective-permute-start | bytes 2359304 | tf_op jit(solution)/shard_map/ppermute | solution.py:256
  92.0 14.4 %collective-permute-start.24 = (bf16[4,2,48,768]{3,2,1,0:T(8,128)(2,1)S(1)}, bf16[4,2,48,768]{3,2,1,0:T(8,128)(2,1)S(1)}, u32[]{:S(2)}, u32[]{:S(2)}) collective-permute-start(bf16[4,2,48,768]{3,2,1,0:T(8,128)(2,1)S(1)} %pad_maximum_fusion.10), channel_id=1, source_target_pairs={{0,16},{16,0},{1,17},{17,1},{2,18},{18,2},{3,19},{19,3},{4,20},{20... | collective-permute-start | bytes 1769480 | tf_op jit(solution)/shard_map/ppermute | solution.py:277
  113.8 20.0 %collective-permute-start.19 = (bf16[512,768]{1,0:T(8,128)(2,1)S(1)}, bf16[512,768]{1,0:T(8,128)(2,1)S(1)}, u32[]{:S(2)}, u32[]{:S(2)}) collective-permute-start(bf16[512,768]{1,0:T(8,128)(2,1)S(1)} %get-tuple-element.93), channel_id=1, source_target_pairs={{0,2},{1,3},{2,0},{3,1},{4,6},{5,7},{6,4},{7,5},{8,10},{9,11},{10,... | collective-permute-start | bytes 2359304 | tf_op jit(solution)/shard_map/ppermute | solution.py:250
  120.1 13.7 %collective-permute-start.28 = (bf16[2,4,96,768]{3,2,1,0:T(8,128)(2,1)S(1)}, bf16[2,4,96,768]{3,2,1,0:T(8,128)(2,1)S(1)}, u32[]{:S(2)}, u32[]{:S(2)}) collective-permute-start(bf16[2,4,96,768]{3,2,1,0:T(8,128)(2,1)S(1)} %get-tuple-element.104), channel_id=1, source_target_pairs={{0,1},{1,0},{2,3},{3,2},{4,5},{5,4},{6,7},{7,6},{8,9},{9,8},{10,11... | collective-permute-start | bytes 3538952 | tf_op jit(solution)/shard_map/ppermute | solution.py:250
  127.4 21.8 %collective-permute-start.27 = (bf16[512,768]{1,0:T(8,128)(2,1)S(1)}, bf16[512,768]{1,0:T(8,128)(2,1)S(1)}, u32[]{:S(2)}, u32[]{:S(2)}) collective-permute-start(bf16[512,768]{1,0:T(8,128)(2,1)S(1)} %get-tuple-element.107.grad_b.grad_a.hg_b), channel_id=1, source_target_pairs={{0,4},{1,5},{2,6},{3,7},{4,8},{5,9},{6,10},{7,11},{8,12},{9,13},{1... | collective-permute-start | bytes 2359304 | tf_op jit(solution)/shard_map/ppermute | solution.py:253
  129.3 21.8 %collective-permute-start.26 = (bf16[512,768]{1,0:T(8,128)(2,1)S(1)}, bf16[512,768]{1,0:T(8,128)(2,1)S(1)}, u32[]{:S(2)}, u32[]{:S(2)}) collective-permute-start(bf16[512,768]{1,0:T(8,128)(2,1)S(1)} %get-tuple-element.115.grad_a.grad_b.hg_a), channel_id=1, source_target_pairs={{4,0},{5,1},{6,2},{7,3},{8,4},{9,5},{10,6},{11,7},{12,8},{13,9},{1... | collective-permute-start | bytes 2359304 | tf_op jit(solution)/shard_map/ppermute | solution.py:256
  136.8 19.2 %collective-permute-start.29 = (bf16[4,96,768]{2,1,0:T(8,128)(2,1)S(1)}, bf16[4,96,768]{2,1,0:T(8,128)(2,1)S(1)}, u32[]{:S(2)}, u32[]{:S(2)}) collective-permute-start(bf16[4,96,768]{2,1,0:T(8,128)(2,1)S(1)} %get-tuple-element.111), channel_id=1, source_target_pairs={{0,2},{1,3},{2,0},{3,1},{4,6},{5,7},{6,4},{7,5},{8,10},{9,11},{10,... | collective-permute-start | bytes 1769480 | tf_op jit(solution)/shard_map/ppermute | solution.py:250
  142.6 13.4 %collective-permute-start.30 = (bf16[2,4,96,768]{3,2,1,0:T(8,128)(2,1)S(1)}, bf16[2,4,96,768]{3,2,1,0:T(8,128)(2,1)S(1)}, u32[]{:S(2)}, u32[]{:S(2)}) collective-permute-start(bf16[2,4,96,768]{3,2,1,0:T(8,128)(2,1)S(1)} %get-tuple-element.113), channel_id=1, source_target_pairs={{0,1},{1,0},{2,3},{3,2},{4,5},{5,4},{6,7},{7,6},{8,9},{9,8},{10,11... | collective-permute-start | bytes 3538952 | tf_op jit(solution)/shard_map/ppermute | solution.py:250
  161.4 26.8 %collective-permute-start.37 = (bf16[2,4,96,768]{3,2,1,0:T(8,128)(2,1)S(1)}, bf16[2,4,96,768]{3,2,1,0:T(8,128)(2,1)S(1)}, u32[]{:S(2)}, u32[]{:S(2)}) collective-permute-start(bf16[2,4,96,768]{3,2,1,0:T(8,128)(2,1)S(1)} %get-tuple-element.133), channel_id=1, source_target_pairs={{0,1},{1,0},{2,3},{3,2},{4,5},{5,4},{6,7},{7,6},{8,9},{9,8},{10,11... | collective-permute-start | bytes 3538952 | tf_op jit(solution)/shard_map/ppermute | solution.py:250
  161.9 25.6 %collective-permute-start.36 = (bf16[4,96,768]{2,1,0:T(8,128)(2,1)S(1)}, bf16[4,96,768]{2,1,0:T(8,128)(2,1)S(1)}, u32[]{:S(2)}, u32[]{:S(2)}) collective-permute-start(bf16[4,96,768]{2,1,0:T(8,128)(2,1)S(1)} %get-tuple-element.130), channel_id=1, source_target_pairs={{0,2},{1,3},{2,0},{3,1},{4,6},{5,7},{6,4},{7,5},{8,10},{9,11},{10,... | collective-permute-start | bytes 1769480 | tf_op jit(solution)/shard_map/ppermute | solution.py:250
  164.1 14.3 %collective-permute-start.33 = (bf16[96,768]{1,0:T(8,128)(2,1)S(1)}, bf16[96,768]{1,0:T(8,128)(2,1)S(1)}, u32[]{:S(2)}, u32[]{:S(2)}) collective-permute-start(bf16[96,768]{1,0:T(8,128)(2,1)S(1)} %get-tuple-element.126), channel_id=1, source_target_pairs={{0,4},{1,5},{2,6},{3,7},{4,0},{5,1},{6,2},{7,3},{8,12},{9,13},{10,... | collective-permute-start | bytes 442376 | tf_op jit(solution)/shard_map/ppermute | solution.py:250
  164.2 15.7 %collective-permute-start.34 = (bf16[96,768]{1,0:T(8,128)(2,1)S(1)}, bf16[96,768]{1,0:T(8,128)(2,1)S(1)}, u32[]{:S(2)}, u32[]{:S(2)}) collective-permute-start(bf16[96,768]{1,0:T(8,128)(2,1)S(1)} %get-tuple-element.127), channel_id=1, source_target_pairs={{0,8},{1,9},{2,10},{3,11},{4,12},{5,13},{6,14},{7,15},{8,0},{9,1},... | collective-permute-start | bytes 442376 | tf_op jit(solution)/shard_map/ppermute | solution.py:250
  170.7 34.3 %collective-permute-start.41 = (bf16[4,96,768]{2,1,0:T(8,128)(2,1)S(1)}, bf16[4,96,768]{2,1,0:T(8,128)(2,1)S(1)}, u32[]{:S(2)}, u32[]{:S(2)}) collective-permute-start(bf16[4,96,768]{2,1,0:T(8,128)(2,1)S(1)} %get-tuple-element.142), channel_id=1, source_target_pairs={{0,2},{1,3},{2,0},{3,1},{4,6},{5,7},{6,4},{7,5},{8,10},{9,11},{10,... | collective-permute-start | bytes 1769480 | tf_op jit(solution)/shard_map/ppermute | solution.py:250
  178.3 31.7 %collective-permute-start.32 = (bf16[512,768]{1,0:T(8,128)(2,1)S(1)}, bf16[512,768]{1,0:T(8,128)(2,1)S(1)}, u32[]{:S(2)}, u32[]{:S(2)}) collective-permute-start(bf16[512,768]{1,0:T(8,128)(2,1)S(1)} %get-tuple-element.123), channel_id=1, source_target_pairs={{0,2},{1,3},{2,0},{3,1},{4,6},{5,7},{6,4},{7,5},{8,10},{9,11},{10,... | collective-permute-start | bytes 2359304 | tf_op jit(solution)/shard_map/ppermute | solution.py:250
  189.3 32.0 %collective-permute-start.45 = (bf16[4,96,768]{2,1,0:T(8,128)(2,1)S(1)}, bf16[4,96,768]{2,1,0:T(8,128)(2,1)S(1)}, u32[]{:S(2)}, u32[]{:S(2)}) collective-permute-start(bf16[4,96,768]{2,1,0:T(8,128)(2,1)S(1)} %get-tuple-element.148), channel_id=1, source_target_pairs={{0,2},{1,3},{2,0},{3,1},{4,6},{5,7},{6,4},{7,5},{8,10},{9,11},{10,... | collective-permute-start | bytes 1769480 | tf_op jit(solution)/shard_map/ppermute | solution.py:250
  189.9 13.8 %collective-permute-start.39 = (bf16[96,768]{1,0:T(8,128)(2,1)S(1)}, bf16[96,768]{1,0:T(8,128)(2,1)S(1)}, u32[]{:S(2)}, u32[]{:S(2)}) collective-permute-start(bf16[96,768]{1,0:T(8,128)(2,1)S(1)} %get-tuple-element.139), channel_id=1, source_target_pairs={{0,8},{1,9},{2,10},{3,11},{4,12},{5,13},{6,14},{7,15},{8,0},{9,1},... | collective-permute-start | bytes 442376 | tf_op jit(solution)/shard_map/ppermute | solution.py:250
  205.8 11.5 %collective-permute-start.43 = (bf16[96,768]{1,0:T(8,128)(2,1)S(1)}, bf16[96,768]{1,0:T(8,128)(2,1)S(1)}, u32[]{:S(2)}, u32[]{:S(2)}) collective-permute-start(bf16[96,768]{1,0:T(8,128)(2,1)S(1)} %get-tuple-element.145), channel_id=1, source_target_pairs={{0,8},{1,9},{2,10},{3,11},{4,12},{5,13},{6,14},{7,15},{8,0},{9,1},... | collective-permute-start | bytes 442376 | tf_op jit(solution)/shard_map/ppermute | solution.py:250
  207.9 13.3 %collective-permute-start.44 = (bf16[96,768]{1,0:T(8,128)(2,1)S(1)}, bf16[96,768]{1,0:T(8,128)(2,1)S(1)}, u32[]{:S(2)}, u32[]{:S(2)}) collective-permute-start(bf16[96,768]{1,0:T(8,128)(2,1)S(1)} %get-tuple-element.146), channel_id=1, source_target_pairs={{0,12},{1,13},{2,14},{3,15},{4,8},{5,9},{6,10},{7,11},{8,4},{9,5},... | collective-permute-start | bytes 442376 | tf_op jit(solution)/shard_map/ppermute | solution.py:250
  221.9 18.9 %collective-permute-start.46 = (bf16[512,768]{1,0:T(8,128)(2,1)S(1)}, bf16[512,768]{1,0:T(8,128)(2,1)S(1)}, u32[]{:S(2)}, u32[]{:S(2)}) collective-permute-start(bf16[512,768]{1,0:T(8,128)(2,1)S(1)} %get-tuple-element.150), channel_id=1, source_target_pairs={{0,2},{1,3},{2,0},{3,1},{4,6},{5,7},{6,4},{7,5},{8,10},{9,11},{10,... | collective-permute-start | bytes 2359304 | tf_op jit(solution)/shard_map/ppermute | solution.py:250
  223.6 11.6 %collective-permute-start.48 = (bf16[96,768]{1,0:T(8,128)(2,1)S(1)}, bf16[96,768]{1,0:T(8,128)(2,1)S(1)}, u32[]{:S(2)}, u32[]{:S(2)}) collective-permute-start(bf16[96,768]{1,0:T(8,128)(2,1)S(1)} %get-tuple-element.152), channel_id=1, source_target_pairs={{0,8},{1,9},{2,10},{3,11},{4,12},{5,13},{6,14},{7,15},{8,0},{9,1},... | collective-permute-start | bytes 442376 | tf_op jit(solution)/shard_map/ppermute | solution.py:250
  225.2 13.7 %collective-permute-start.49 = (bf16[96,768]{1,0:T(8,128)(2,1)S(1)}, bf16[96,768]{1,0:T(8,128)(2,1)S(1)}, u32[]{:S(2)}, u32[]{:S(2)}) collective-permute-start(bf16[96,768]{1,0:T(8,128)(2,1)S(1)} %get-tuple-element.153), channel_id=1, source_target_pairs={{0,12},{1,13},{2,14},{3,15},{4,8},{5,9},{6,10},{7,11},{8,4},{9,5},... | collective-permute-start | bytes 442376 | tf_op jit(solution)/shard_map/ppermute | solution.py:250
  (27 other events, 202.5 us)
